TPU v7x, 768 devices: a whole 4x8x12 slice. The times are simulated.
768 devices in a mesh: row: 192 (over z, y, core), col: 4 (over x).
Axes of the slice: x: 4, y: 8, z: 12, core: 2. Of those that a mesh axis runs over, the one named last changes fastest.
Arguments:
- slab: bfloat16 [2, 49152, 6144], P(None, 'row', 'col'), may hold values from 0.049804688 to 1
- slab_fill: int32 [2, 384, 48], P(None, 'row', 'col'), may hold values from 0 to 1, as said below
- panel: bfloat16 [2, 6144, 512], P(None, 'row', 'col'), may hold values from 0.049804688 to 1
- out_fill: int32 [384, 4], P('row', 'col'), may hold values from 0 to 1, as said below
Outputs:
- inflated: float32 [49152, 512], P('row', 'col')
Inputs may be any that keep to these rules, and one draw needn't show every extreme that they name: `slab_fill`: in every section and block row, each aligned group of 12 tile columns (one index of col) holds 1 to 6 filled tiles, and some group of each section holds exactly 6. `out_fill`: every block column holds at least one kept tile.
All inputs are finite; a program needn't handle non-finite values.
Results may differ from a plain program's by a relative error of at most 0.0003.
Values may be sent and summed in bfloat16 or wider, within the bound.
No kernel may reach another device: no remote copies, remote signals or barrier semaphores. Data moves between devices by JAX's collectives and lax.ppermute only.
A program may use at most 64 MiB of HBM per device.

v0:
```python
import jax
import jax.numpy as jnp
from jax import lax
from jax.sharding import PartitionSpec as P

TILE = 128


def shards(slab, slab_fill, panel, out_fill):
    sections, row_count, local_cols = slab.shape
    tile_mask = jnp.repeat(jnp.repeat(slab_fill, TILE, axis=1), TILE, axis=2).astype(jnp.bfloat16)
    masked = slab * tile_mask
    gathered = lax.all_gather(masked, "col", axis=2, tiled=True)
    zero_sum = jnp.zeros((row_count, panel.shape[2]), jnp.float32)
    product = zero_sum
    for step_index in range(sections):
        section_slab = gathered[step_index]

        def add_section(running, panel_piece, offset, section_slab=section_slab):
            return running + jnp.dot(section_slab, panel_piece, preferred_element_type=jnp.float32)

        product = add_section(
            product, lax.all_gather(panel[step_index], "row", axis=0, tiled=True), jnp.int32(0)
        )
    out_mask = jnp.repeat(jnp.repeat(out_fill, TILE, axis=0), TILE, axis=1).astype(jnp.float32)
    squares = product * product * out_mask
    column_sums = lax.psum(jnp.sum(squares, axis=0), "row")
    factor_col = jnp.float32(row_count * lax.axis_size("row")) / column_sums
    return squares * factor_col


def solution(mesh):
    placed = (P(None, "row", "col"), P(None, "row", "col"), P(None, "row", "col"), P("row", "col"))
    return jax.shard_map(
        shards, mesh=mesh, in_specs=placed, out_specs=P("row", "col"), check_vma=False
    )
```

profile of v0, /device:TPU:1, one launch (start us, length us, event | category | flops | bytes accessed | tf_op | source)
XLA Modules:
  0.0 699.2 jit_solution(4150476223237299438)
XLA Ops:
  6.5 0.0 all-gather.10.cloned.1.call-start
  6.5 1.3 fusion.13
  7.9 0.0 all-gather.10.cloned.1.call-update
  7.9 0.0 copy-start
  7.9 0.0 all-gather.6.cloned.1.call-start
  7.9 1.7 copy.9
  9.7 0.0 copy-done
  9.7 0.1 copy.7
  9.8 0.1 broadcast_in_dim.11
  9.9 1.3 bitcast_multiply_fusion
  11.2 0.0 copy-start.1
  11.2 0.0 all-gather.6.cloned.1.call-update
  11.2 0.0 all-gather.8.cloned.1.call-start
  11.3 0.7 all-gather.8.cloned.1.call-update
  12.0 0.0 copy-done.1
  12.0 0.1 broadcast_bitcast_fusion
  12.1 118.0 %all-gather.10.cloned.1.call-done = bf16[1,6144,128]{2,1,0:T(8,128)(2,1)} async-done(((bf16[1,32,128]{2,1,0:T(8,128)(2,1)}), bf16[1,6144,128]{2,1,0:T(8,128)(2,1)}) %all-gather.10.cloned.1.call-update) | async-done | bytes 1572880 | tf_op jit(solution)/shard_map/all_gather | solution.py:23
  130.1 73.4 %all-gather.6.cloned.1.call-done = bf16[2,256,6144]{1,2,0:T(8,128)(2,1)} async-done(((bf16[2,256,1536]{1,2,0:T(8,128)(2,1)}), bf16[2,256,6144]{1,2,0:T(8,128)(2,1)}) %all-gather.6.cloned.1.call-update) | async-done | bytes 6291472 | tf_op jit(solution)/shard_map/all_gather | solution.py:13
  203.5 3.4 fusion
  206.9 112.5 %all-gather.8.cloned.1.call-done = bf16[1,6144,128]{2,1,0:T(8,128)(2,1)} async-done(((bf16[1,32,128]{2,1,0:T(8,128)(2,1)}), bf16[1,6144,128]{2,1,0:T(8,128)(2,1)}) %all-gather.8.cloned.1.call-update) | async-done | bytes 1572880 | tf_op jit(solution)/shard_map/all_gather | solution.py:23
  319.5 3.4 fusion.14
  322.9 369.2 %psum.7 = f32[128]{0:T(128)S(1)} all-reduce(f32[128]{0:T(128)S(1)} %get-tuple-element.7), channel_id=1, replica_groups=mesh['row'=192,'col'=4] {'row'}, use_global_device_ids=true, to_apply=%region_1.0 | all-reduce | flops 128 | bytes 1024 | tf_op jit(solution)/shard_map/psum | solution.py:27
  692.0 0.7 broadcast_multiply_fusion
  (5 shorter events, 0.0 us)
Async XLA Ops:
  6.5 123.6 %all-gather.10.cloned.1.call-start = ((), (), s32[]{:S(2)}) async-start(), calls=%async_computation.2 | async-start | bytes 1581056 | tf_op jit(solution)/shard_map/all_gather | solution.py:23
  7.9 1.8 copy-start
  7.9 195.6 %all-gather.6.cloned.1.call-start = ((), (), s32[]{:S(2)}) async-start(), calls=%async_computation | async-start | bytes 7864320 | tf_op jit(solution)/shard_map/all_gather | solution.py:13
  11.2 0.8 copy-start.1
  11.2 308.2 %all-gather.8.cloned.1.call-start = ((), (), s32[]{:S(2)}) async-start(), calls=%async_computation.1 | async-start | bytes 1581056 | tf_op jit(solution)/shard_map/all_gather | solution.py:23
Sparse Core Ops, SparseCore 0:
  11.1 118.9 all-gather.9
  132.5 70.9 all-gather.5
  207.3 112.1 all-gather.7
where the time goes:
time: 702 us; the launch traced here: 699 us
  blocking collectives  369 us (53%)
  waiting for transfers between devices  305 us (43%)
  between operations  13.2 us (2%)
    psum x1, blocking collectives, shards(): column_sums = lax.psum(jnp.sum(squares, axis=0), 'row')  369 us
    all_gather x2, waiting for transfers between devices, shards(): lax.all_gather(panel[step_index], 'row', axis=0, tiled=True)  231 us
    all_gather x1, waiting for transfers between devices, shards(): gathered = lax.all_gather(masked, 'col', axis=2, tiled=True)  73.4 us
  transfers between devices with their start and end apart: 3, of which 3 were waited for; matrix products, arithmetic and copies ran while one was open for 1% of the time, Pallas kernels for 0%

commit v1 on v0

v1 whole, which is shorter than its diff:
```python
import jax
import jax.numpy as jnp
from jax import lax
from jax.sharding import Mesh, PartitionSpec as P

TILE = 128
NZ, NY, NC, NX = 12, 8, 2, 4


def spread(piece, axis, size):
    copies = jnp.broadcast_to(piece[None], (size,) + piece.shape)
    return lax.all_to_all(copies, axis, 0, 0, tiled=True)


def shards(slab, slab_fill, panel, out_fill):
    sections, row_count, local_cols = slab.shape
    depth, width = panel.shape[1], panel.shape[2]
    tile_mask = jnp.repeat(jnp.repeat(slab_fill, TILE, axis=1), TILE, axis=2).astype(jnp.bfloat16)
    masked = slab * tile_mask
    moves = [
        (z * NX + x, ((z % 3) * 4 + x) * NX + z // 3) for z in range(NZ) for x in range(NX)
    ]
    piece = lax.ppermute(panel, ("z", "x"), moves)
    piece = spread(piece, "z", NZ)
    piece = spread(piece, "y", NY)
    piece = spread(piece, "core", NC)
    piece = piece.reshape(NC, NY, 3, NX, sections, depth, width)
    right = piece.transpose(4, 2, 1, 0, 5, 3, 6).reshape(sections, local_cols, NX * width)
    product = jnp.einsum("srk,skn->rn", masked, right, preferred_element_type=jnp.float32)
    product = product.reshape(row_count, NX, width).transpose(1, 0, 2)
    product = jnp.sum(lax.all_to_all(product, "x", 0, 0, tiled=True), axis=0)
    out_mask = jnp.repeat(jnp.repeat(out_fill, TILE, axis=0), TILE, axis=1).astype(jnp.float32)
    squares = product * product * out_mask
    sums = jnp.sum(squares.reshape(-1, 8, width), axis=0)
    sums = jnp.sum(spread(sums, ("y", "core"), NY * NC), axis=0)
    sums = jnp.sum(spread(sums, "z", NZ), axis=(0, 1))
    factor_col = jnp.float32(row_count * NZ * NY * NC) / sums
    return squares * factor_col


def solution(mesh):
    fine = Mesh(mesh.devices.reshape(NZ, NY, NC, NX), ("z", "y", "core", "x"))
    row = ("z", "y", "core")
    placed = (P(None, row, "x"), P(None, row, "x"), P(None, row, "x"), P(row, "x"))
    return jax.shard_map(
        shards, mesh=fine, in_specs=placed, out_specs=P(row, "x"), check_vma=False
    )
```

time: 702 us -> 150 us (0.21)
  blocking collectives: 369 us -> 59.3 us
  waiting for transfers between devices: 305 us -> 52.6 us
  starting transfers between devices: 0.09 us -> 15.8 us
  between operations: 13.2 us -> 0.14 us
  local copies, waits for them, and re-layouts: 3.33 us -> 15.9 us
    psum x1 -> x0, blocking collectives: 369 us -> none  [shards(): column_sums = lax.psum(jnp.sum(squares, axis=0), 'row')]
    all_gather x3 -> x0, waiting for transfers between devices: 304 us -> none  [the longest x2 231 us: shards(): lax.all_gather(panel[step_index], 'row', axis=0, tiled=True)]
    all_to_all x0 -> x3, blocking collectives: none -> 59.3 us  [spread(): return lax.all_to_all(copies, axis, 0, 0, tiled=True)]
    all_to_all x0 -> x3, waiting for transfers between devices: none -> 52.6 us  [the longest x2 43.6 us: spread(): return lax.all_to_all(copies, axis, 0, 0, tiled=True)]
    all_to_all x0 -> x3, starting transfers between devices: none -> 14.4 us  [the longest x2 11 us: spread(): return lax.all_to_all(copies, axis, 0, 0, tiled=True)]
  transfers between devices with their start and end apart: 3 -> 4, of which waited for: 3 -> 3; matrix products, arithmetic and copies ran while one was open for 1% -> 2% of each run, Pallas kernels for 0% -> 0%
where the time goes in v1:
time: 150 us; the launch traced here: 149 us
  blocking collectives  59.3 us (40%)
  waiting for transfers between devices  52.6 us (35%)
  local copies, waits for them, and re-layouts  15.9 us (11%)
  starting transfers between devices  15.8 us (11%)
  matrix products  3.23 us (2%)
  other arithmetic  2.2 us (1%)
    all_to_all x3, blocking collectives, spread(): return lax.all_to_all(copies, axis, 0, 0, tiled=True)  59.3 us
    all_to_all x2, waiting for transfers between devices, spread(): return lax.all_to_all(copies, axis, 0, 0, tiled=True)  43.6 us
    all_to_all x2, starting transfers between devices, spread(): return lax.all_to_all(copies, axis, 0, 0, tiled=True)  11 us
    all_to_all x1, waiting for transfers between devices, shards(): product = jnp.sum(lax.all_to_all(product, 'x', 0, 0, tiled=True), axis=0)  9.02 us
    transpose x1, local copies, waits for them, and re-layouts, shards(): piece.transpose(4, 2, 1, 0, 5, 3, 6)  4.05 us
    all_to_all x1, starting transfers between devices, shards(): product = jnp.sum(lax.all_to_all(product, 'x', 0, 0, tiled=True), axis=0)  3.47 us
    broadcast_in_dim x5, local copies, waits for them, and re-layouts, spread(): copies = jnp.broadcast_to(piece[None], (size,) + piece.shape)  3.26 us
    reshape x1, local copies, waits for them, and re-layouts, shards(): piece.transpose(4, 2, 1, 0, 5, 3, 6)  3.25 us
  transfers between devices with their start and end apart: 4, of which 3 were waited for; matrix products, arithmetic and copies ran while one was open for 2% of the time, Pallas kernels for 0%

profile of v1, /device:TPU:1, one launch (start us, length us, event | category | flops | bytes accessed | tf_op | source)
XLA Modules:
  0.0 149.2 jit_solution(6600782410895279087)
XLA Ops:
  0.0 1.4 collective-permute-start
  1.4 0.0 collective-permute-done
  1.4 38.3 %all_to_all.30 = bf16[12,2,32,128]{3,2,1,0:T(8,128)(2,1)S(1)} all-to-all(bf16[12,2,32,128]{3,2,1,0:T(8,128)(2,1)S(1)} %broadcast_in_dim.20), channel_id=1, replica_groups=mesh['z'=12,'y'=8,'core'=2,'x'=4] {'z'}, dimensions={0} | all-to-all | bytes 393216 | tf_op jit(solution)/shard_map/all_to_all | solution.py:12
  39.7 1.5 %broadcast_in_dim.21 = bf16[8,12,2,32,128]{4,3,2,1,0:T(8,128)(2,1)} broadcast(bf16[12,2,32,128]{3,2,1,0:T(8,128)(2,1)S(1)} %all_to_all.30), dimensions={1,2,3,4} | broadcast | bytes 1769472 | tf_op jit(solution)/shard_map/broadcast_in_dim | solution.py:11
  41.3 6.8 %all-to-all-start.1 = ((bf16[8,12,2,32,128]{4,3,2,1,0:T(8,128)(2,1)}), bf16[8,12,2,32,128]{4,3,2,1,0:T(8,128)(2,1)S(1)}, u32[]{:S(2)}, u32[]{:S(2)}) async-start(bf16[8,12,2,32,128]{4,3,2,1,0:T(8,128)(2,1)} %broadcast_in_dim.21), calls=%async_computation.1 | async-start | bytes 3145728 | tf_op jit(solution)/shard_map/all_to_all | solution.py:12
  48.1 0.0 copy-start
  48.1 1.7 %copy.19 = bf16[2,256,1536]{1,2,0:T(8,128)(2,1)S(1)} copy(bf16[2,256,1536]{2,1,0:T(8,128)(2,1)} %param.4) | data formatting | bytes 3145728 | tf_op args[0]
  49.8 0.0 copy-done
  49.8 0.1 copy.17
  49.9 0.1 broadcast_in_dim.18
  50.1 1.2 bitcast_multiply_fusion
  51.3 34.0 %all-to-all-done.1 = bf16[8,12,2,32,128]{4,3,2,1,0:T(8,128)(2,1)S(1)} async-done(((bf16[8,12,2,32,128]{4,3,2,1,0:T(8,128)(2,1)}), bf16[8,12,2,32,128]{4,3,2,1,0:T(8,128)(2,1)S(1)}, u32[]{:S(2)}, u32[]{:S(2)}) %all-to-all-start.1) | async-done | bytes 1572896 | tf_op jit(solution)/shard_map/all_to_all | solution.py:12
  85.3 1.1 broadcast_in_dim.22
  86.3 9.6 %all_to_all.31 = bf16[2,8,12,2,32,128]{5,4,3,2,1,0:T(8,128)(2,1)S(1)} all-to-all(bf16[2,8,12,2,32,128]{5,4,3,2,1,0:T(8,128)(2,1)S(1)} %broadcast_in_dim.22), channel_id=1, replica_groups=mesh['z'=12,'y'=8,'core'=2,'x'=4] {'core'}, dimensions={0} | all-to-all | bytes 6291456 | tf_op jit(solution)/shard_map/all_to_all | solution.py:12
  95.9 4.0 %copy.20 = bf16[2,3,8,2,32,4,128]{6,5,4,3,2,1,0:T(4,128)(2,1)S(1)} copy(bf16[2,3,8,2,32,4,128]{6,4,0,5,1,2,3:T(8,128)(2,1)S(1)} %bitcast.32) | data formatting | bytes 6291456 | tf_op jit(solution)/shard_map/transpose | solution.py:28
  100.0 3.3 %reshape.44 = bf16[2,1536,512]{2,1,0:T(8,128)(2,1)} reshape(bf16[2,3,8,2,32,4,128]{6,5,4,3,2,1,0:T(4,128)(2,1)S(1)} %copy.20) | data formatting | bytes 6291456 | tf_op jit(solution)/shard_map/reshape | solution.py:28
  103.2 3.2 %copy.21 = bf16[512,1536,2]{1,0,2:T(8,128)(2,1)S(1)} copy(bf16[512,1536,2]{0,1,2:T(8,128)(2,1)} %bitcast.33) | data formatting | bytes 6291456 | tf_op jit(solution)/shard_map/srk,skn->rn/dot_general | solution.py:29
  106.4 0.0 copy-start.1
  106.4 3.2 %fusion.2 = f32[4,256,128]{2,1,0:T(8,128)} fusion(bf16[4,128,1536,2]{2,1,0,3:T(8,128)(2,1)S(1)} %bitcast.34, bf16[2,256,1536]{1,2,0:T(8,128)(2,1)} %bitcast_multiply_fusion), kind=kOutput, calls=%fused_computation.3 | convolution fusion | flops 805306368 | bytes 5242880 | tf_op jit(solution)/shard_map/srk,skn->rn/dot_general | solution.py:29
  109.7 3.5 %all-to-all-start.3 = ((f32[4,256,128]{2,1,0:T(8,128)}), f32[4,256,128]{2,1,0:T(8,128)S(1)}, u32[]{:S(2)}, u32[]{:S(2)}) async-start(f32[4,256,128]{2,1,0:T(8,128)} %fusion.2), calls=%async_computation.3 | async-start | bytes 1048576 | tf_op jit(solution)/shard_map/all_to_all | solution.py:31
  113.2 0.0 copy-done.1
  113.2 0.1 broadcast_in_dim.24
  113.2 0.1 convert_element_type.36
  113.3 9.0 %all-to-all-done.3 = f32[4,256,128]{2,1,0:T(8,128)S(1)} async-done(((f32[4,256,128]{2,1,0:T(8,128)}), f32[4,256,128]{2,1,0:T(8,128)S(1)}, u32[]{:S(2)}, u32[]{:S(2)}) %all-to-all-start.3) | async-done | bytes 524320 | tf_op jit(solution)/shard_map/all_to_all | solution.py:31
  122.4 0.1 fusion.5
  122.5 11.4 %all_to_all.32 = f32[16,8,128]{2,1,0:T(8,128)S(1)} all-to-all(f32[16,8,128]{2,1,0:T(8,128)S(1)} %broadcast_in_dim.50), channel_id=1, replica_groups=mesh['z'=12,'y'=8,'core'=2,'x'=4] {'y','core'}, dimensions={0} | all-to-all | bytes 131072 | tf_op jit(solution)/shard_map/all_to_all | solution.py:12
  134.0 0.6 broadcast_in_dim.51
  134.6 4.1 %all-to-all-start.5 = ((f32[12,8,128]{2,1,0:T(8,128)}), f32[12,8,128]{2,1,0:T(8,128)S(1)}, u32[]{:S(2)}, u32[]{:S(2)}) async-start(f32[12,8,128]{2,1,0:T(8,128)} %broadcast_in_dim.51), calls=%async_computation.5 | async-start | bytes 98304 | tf_op jit(solution)/shard_map/all_to_all | solution.py:12
  138.7 0.1 broadcast_bitcast_fusion
  138.8 9.6 %all-to-all-done.5 = f32[12,8,128]{2,1,0:T(8,128)S(1)} async-done(((f32[12,8,128]{2,1,0:T(8,128)}), f32[12,8,128]{2,1,0:T(8,128)S(1)}, u32[]{:S(2)}, u32[]{:S(2)}) %all-to-all-start.5) | async-done | bytes 49184 | tf_op jit(solution)/shard_map/all_to_all | solution.py:12
  148.5 0.8 multiply_multiply_fusion
  (10 shorter events, 0.1 us)
Async XLA Ops:
  0.0 1.4 collective-permute-start
  41.3 44.0 %all-to-all-start.1 = ((bf16[8,12,2,32,128]{4,3,2,1,0:T(8,128)(2,1)}), bf16[8,12,2,32,128]{4,3,2,1,0:T(8,128)(2,1)S(1)}, u32[]{:S(2)}, u32[]{:S(2)}) async-start(bf16[8,12,2,32,128]{4,3,2,1,0:T(8,128)(2,1)} %broadcast_in_dim.21), calls=%async_computation.1 | async-start | bytes 3145728 | tf_op jit(solution)/shard_map/all_to_all | solution.py:12
  48.1 1.7 %copy-start = (s32[2,2,12]{2,1,0:T(2,128)S(1)}, s32[2,2,12]{2,1,0:T(2,128)}, u32[]{:S(2)}) copy-start(s32[2,2,12]{2,1,0:T(2,128)} %param.5) | copy-start | bytes 580
  106.4 6.7 %copy-start.1 = (s32[2,1]{0,1:T(1,128)S(1)}, s32[2,1]{0,1:T(1,128)}, u32[]{:S(2)}) copy-start(s32[2,1]{0,1:T(1,128)} %param.7) | copy-start | bytes 28
  109.7 12.7 %all-to-all-start.3 = ((f32[4,256,128]{2,1,0:T(8,128)}), f32[4,256,128]{2,1,0:T(8,128)S(1)}, u32[]{:S(2)}, u32[]{:S(2)}) async-start(f32[4,256,128]{2,1,0:T(8,128)} %fusion.2), calls=%async_computation.3 | async-start | bytes 1048576 | tf_op jit(solution)/shard_map/all_to_all | solution.py:31
  134.6 13.9 %all-to-all-start.5 = ((f32[12,8,128]{2,1,0:T(8,128)}), f32[12,8,128]{2,1,0:T(8,128)S(1)}, u32[]{:S(2)}, u32[]{:S(2)}) async-start(f32[12,8,128]{2,1,0:T(8,128)} %broadcast_in_dim.51), calls=%async_computation.5 | async-start | bytes 98304 | tf_op jit(solution)/shard_map/all_to_all | solution.py:12

commit v2 on v0

v2 whole, which is shorter than its diff:
```python
import jax
import jax.numpy as jnp
from jax import lax
from jax.experimental import pallas as pl
from jax.experimental.pallas import tpu as pltpu
from jax.sharding import PartitionSpec as P

TILE = 128
NZ, NY, NC, NX = 12, 8, 2, 4


def row_of(z, y, core):
    return (z % NZ) * NY * NC + (y % NY) * NC + core


def spread(piece, axis, size, groups):
    copies = jnp.broadcast_to(piece[None], (size,) + piece.shape)
    return lax.all_to_all(copies, axis, 0, 0, tiled=True, axis_index_groups=groups)


def first_moves(turn):
    moves = []
    for z in range(NZ):
        for y in range(NY):
            for core in range(NC):
                for x in range(NX):
                    plane, third = z // 3, z % 3
                    target = row_of(x + 4 * ((third + turn) % 3), y, core)
                    moves.append((row_of(z, y, core) * NX + x, target * NX + plane))
    return moves


def step_of(position, shift):
    if shift == 2:
        return 2 if position % 2 == 0 else -2
    return shift


def shift_moves(shift):
    moves = []
    for z in range(NZ):
        for y in range(NY):
            moves.append((row_of(z, y, 0), row_of(z, y + step_of(y, shift), 0)))
            moves.append((row_of(z, y, 1), row_of(z + step_of(z, shift), y, 1)))
    return moves


SHIFTS = (0, 1, -1, 2)
MIXED_GROUPS = [
    [row_of(4 * a + j, b + 4 * h, 0) for j in range(4) for h in range(2)]
    for a in range(3)
    for b in range(4)
] + [[row_of(z, y, 1) for y in range(NY)] for z in range(NZ)]
PLANE_GROUPS = [[row_of(z, j // 2, j % 2) for j in range(NY * NC)] for z in range(NZ)]
Z_GROUPS = [[row_of(z, j // 2, j % 2) for z in range(NZ)] for j in range(NY * NC)]
SWAP = [(r, r ^ 1) for r in range(NZ * NY * NC)]


def places(row):
    z, y = row // (NY * NC), (row // NC) % NY
    shift = jnp.arange(4).reshape(4, 1, 1)
    slot = jnp.arange(8).reshape(1, 8, 1)
    turn = jnp.arange(3).reshape(1, 1, 3)

    def origin(position, size):
        two = jnp.where(position % 2 == 0, position - 2, position + 2)
        out = jnp.where(shift == 0, position, jnp.where(shift == 1, position - 1, position + 1))
        return (jnp.where(shift == 3, two, out) + size) % size

    y_from = origin(y, NY)
    z_from = origin(z, NZ)
    y0, c0 = y_from % 4 + 4 * (slot % 2), slot // 2
    third0 = (z // 4 - turn + 3) % 3
    y1, c1 = slot, z_from % 4
    third1 = (z_from // 4 - turn + 3) % 3
    k0 = (third0 * 16 + y0 * 2) * 32
    k1 = (third1 * 16 + y1 * 2 + 1) * 32
    full = (4, 8, 3)
    k = jnp.stack([jnp.broadcast_to(k0, full), jnp.broadcast_to(k1, full)])
    c = jnp.stack([jnp.broadcast_to(c0, full), jnp.broadcast_to(c1, full)])
    mine = row % NC
    flip = jnp.where(mine == 0, jnp.stack([k, c], -1), jnp.stack([k[::-1], c[::-1]], -1))
    return flip.reshape(-1).astype(jnp.int32)


def product_kernel(place_ref, fill_ref, slab_ref, *refs):
    pieces, out_ref, right_ref, left_ref = refs[:8], refs[8], refs[9], refs[10]
    sections = slab_ref.shape[0]
    for index, piece in enumerate(pieces):

        @pl.loop(0, 8)
        def _(slot, index=index, piece=piece):
            for turn in range(3):
                at = ((index * 8 + slot) * 3 + turn) * 2
                first = pl.multiple_of(place_ref[at], 32)
                column = pl.multiple_of(place_ref[at + 1] * TILE, TILE)
                for s in range(sections):
                    right_ref[s, pl.ds(first, 32), pl.ds(column, TILE)] = piece[slot, turn, s]

    rows, cols = slab_ref.shape[1] // TILE, slab_ref.shape[2] // TILE
    for s in range(sections):
        for r in range(rows):
            for k in range(cols):
                at = (s, slice(r * TILE, (r + 1) * TILE), slice(k * TILE, (k + 1) * TILE))
                keep = fill_ref[(s * rows + r) * cols + k].astype(jnp.float32).astype(jnp.bfloat16)
                left_ref[at] = slab_ref[at] * keep
    for r in range(rows):
        block = slice(r * TILE, (r + 1) * TILE)
        total = jnp.dot(left_ref[0, block], right_ref[0], preferred_element_type=jnp.float32)
        for s in range(1, sections):
            total += jnp.dot(left_ref[s, block], right_ref[s], preferred_element_type=jnp.float32)
        for c in range(NX):
            out_ref[c, block] = total[:, c * TILE : (c + 1) * TILE]


def multiply(place, fill, slab, pieces):
    sections, rows, cols = slab.shape
    smem = pl.BlockSpec(memory_space=pltpu.SMEM)
    vmem = pl.BlockSpec(memory_space=pltpu.VMEM)
    return pl.pallas_call(
        product_kernel,
        out_shape=jax.ShapeDtypeStruct((NX, rows, TILE), jnp.float32),
        in_specs=[smem, smem, vmem] + [vmem] * 8,
        out_specs=vmem,
        scratch_shapes=[
            pltpu.VMEM((sections, cols, NX * TILE), jnp.bfloat16),
            pltpu.VMEM((sections, rows, cols), jnp.bfloat16),
        ],
        compiler_params=pltpu.CompilerParams(vmem_limit_bytes=32 * 2**20),
        cost_estimate=pl.CostEstimate(
            flops=2 * sections * rows * cols * NX * TILE, bytes_accessed=5 * 2**20, transcendentals=0
        ),
    )(place, fill, slab, *pieces)


def shards(slab, slab_fill, panel, out_fill):
    sections, row_count, local_cols = slab.shape
    width = panel.shape[2]
    row = lax.axis_index("row")
    place = places(row)
    near = jnp.stack([lax.ppermute(panel, ("row", "col"), first_moves(t)) for t in range(3)])
    held = spread(near, "row", 8, MIXED_GROUPS).reshape(8, 3, sections, 32, width)
    mine = [held] + [lax.ppermute(held, "row", shift_moves(s)) for s in SHIFTS[1:]]
    theirs = [lax.ppermute(piece, "row", SWAP) for piece in mine]
    product = multiply(place, slab_fill.reshape(-1), slab, mine + theirs)
    product = jnp.sum(lax.all_to_all(product, "col", 0, 0, tiled=True), axis=0)
    out_mask = jnp.repeat(jnp.repeat(out_fill, TILE, axis=0), TILE, axis=1).astype(jnp.float32)
    squares = product * product * out_mask
    sums = jnp.sum(squares.reshape(-1, 8, width), axis=0)
    sums = jnp.sum(spread(sums, "row", NY * NC, PLANE_GROUPS), axis=0)
    sums = jnp.sum(spread(sums, "row", NZ, Z_GROUPS), axis=(0, 1))
    factor_col = jnp.float32(row_count * NZ * NY * NC) / sums
    return squares * factor_col


def solution(mesh):
    placed = (P(None, "row", "col"), P(None, "row", "col"), P(None, "row", "col"), P("row", "col"))
    return jax.shard_map(
        shards, mesh=mesh, in_specs=placed, out_specs=P("row", "col"), check_vma=False
    )
```

time: 702 us -> 134 us (0.19)
  blocking collectives: 369 us -> 13.5 us
  waiting for transfers between devices: 305 us -> 31.3 us
  starting transfers between devices: 0.09 us -> 74.1 us
  between operations: 13.2 us -> 0.32 us
    psum x1 -> x0, blocking collectives: 369 us -> none  [shards(): column_sums = lax.psum(jnp.sum(squares, axis=0), 'row')]
    all_gather x3 -> x0, waiting for transfers between devices: 304 us -> none  [the longest x2 231 us: shards(): lax.all_gather(panel[step_index], 'row', axis=0, tiled=True)]
    ppermute x0 -> x10, starting transfers between devices: none -> 51.4 us  [the longest x3 21.8 us: shards(): lax.ppermute(panel, ('row', 'col'), first_moves(t))]
    all_to_all x0 -> x3, waiting for transfers between devices: none -> 28.8 us  [the longest x2 19.9 us: spread(): lax.all_to_all(copies, axis, 0, 0, tiled=True, axis_index_groups=groups)]
    all_to_all x0 -> x3, starting transfers between devices: none -> 22.7 us  [the longest x2 16.8 us: spread(): lax.all_to_all(copies, axis, 0, 0, tiled=True, axis_index_groups=groups)]
    all_to_all x0 -> x1, blocking collectives: none -> 13.5 us  [spread(): lax.all_to_all(copies, axis, 0, 0, tiled=True, axis_index_groups=groups)]
  transfers between devices with their start and end apart: 3 -> 13, of which waited for: 3 -> 4; matrix products, arithmetic and copies ran while one was open for 1% -> 6% of each run, Pallas kernels for 0% -> 0%
where the time goes in v2:
time: 134 us
  starting transfers between devices  74.1 us (55%)
  waiting for transfers between devices  31.3 us (23%)
  blocking collectives  13.5 us (10%)
  local copies, waits for them, and re-layouts  5.79 us (4%)
  Pallas kernels  4.3 us (3%)
  other arithmetic  4.25 us (3%)
    ppermute x3, starting transfers between devices, shards(): lax.ppermute(panel, ('row', 'col'), first_moves(t))  21.8 us
    all_to_all x2, waiting for transfers between devices, spread(): lax.all_to_all(copies, axis, 0, 0, tiled=True, axis_index_groups=groups)  19.9 us
    all_to_all x2, starting transfers between devices, spread(): lax.all_to_all(copies, axis, 0, 0, tiled=True, axis_index_groups=groups)  16.8 us
    ppermute x3, starting transfers between devices, shards(): lax.ppermute(held, 'row', shift_moves(s))  15.2 us
    ppermute x4, starting transfers between devices, shards(): theirs = [lax.ppermute(piece, 'row', SWAP) for piece in mine]  14.4 us
    all_to_all x1, blocking collectives, spread(): lax.all_to_all(copies, axis, 0, 0, tiled=True, axis_index_groups=groups)  13.5 us
    all_to_all x1, waiting for transfers between devices, shards(): product = jnp.sum(lax.all_to_all(product, 'col', 0, 0, tiled=True), axis=0)  8.97 us
    all_to_all x1, starting transfers between devices, shards(): product = jnp.sum(lax.all_to_all(product, 'col', 0, 0, tiled=True), axis=0)  5.81 us
  transfers between devices with their start and end apart: 13, of which 4 were waited for; matrix products, arithmetic and copies ran while one was open for 6% of the time, Pallas kernels for 0%

profile of v2, /device:TPU:1, one launch (start us, length us, event | category | flops | bytes accessed | tf_op | source)
XLA Modules:
  0.0 133.6 jit_solution(15135368010390084855)
XLA Ops:
  0.0 0.0 copy-start.1
  0.0 0.0 copy-start
  0.0 1.5 %collective-permute-start = (bf16[2,32,128]{2,1,0:T(8,128)(2,1)}, bf16[2,32,128]{2,1,0:T(8,128)(2,1)S(1)}, u32[]{:S(2)}, u32[]{:S(2)}) collective-permute-start(bf16[2,32,128]{2,1,0:T(8,128)(2,1)} %param.6), channel_id=1, source_target_pairs={{0,0},{1,64},{2,128},{3,192},{4,4},{5,68},{6,132},{7,196},{8,8},{9... | collective-permute-start | bytes 49160 | tf_op jit(solution)/shard_map/ppermute | solution.py:141
  1.5 13.2 %collective-permute-start.1 = (bf16[2,32,128]{2,1,0:T(8,128)(2,1)}, bf16[2,32,128]{2,1,0:T(8,128)(2,1)S(1)}, u32[]{:S(2)}, u32[]{:S(2)}) collective-permute-start(bf16[2,32,128]{2,1,0:T(8,128)(2,1)} %param.6), channel_id=1, source_target_pairs={{0,256},{1,320},{2,384},{3,448},{4,260},{5,324},{6,388},{7,452},{8... | collective-permute-start | bytes 49160 | tf_op jit(solution)/shard_map/ppermute | solution.py:141
  14.7 7.1 %collective-permute-start.2 = (bf16[2,32,128]{2,1,0:T(8,128)(2,1)}, bf16[2,32,128]{2,1,0:T(8,128)(2,1)S(1)}, u32[]{:S(2)}, u32[]{:S(2)}) collective-permute-start(bf16[2,32,128]{2,1,0:T(8,128)(2,1)} %param.6), channel_id=1, source_target_pairs={{0,512},{1,576},{2,640},{3,704},{4,516},{5,580},{6,644},{7,708},{8... | collective-permute-start | bytes 49160 | tf_op jit(solution)/shard_map/ppermute | solution.py:141
  21.8 0.0 collective-permute-done
  21.8 0.0 collective-permute-done.1
  21.9 2.5 %collective-permute-done.2 = bf16[2,32,128]{2,1,0:T(8,128)(2,1)S(1)} collective-permute-done((bf16[2,32,128]{2,1,0:T(8,128)(2,1)}, bf16[2,32,128]{2,1,0:T(8,128)(2,1)S(1)}, u32[]{:S(2)}, u32[]{:S(2)}) %collective-permute-start.2) | collective-permute-done | bytes 16416 | tf_op jit(solution)/shard_map/ppermute | solution.py:141
  24.3 0.8 broadcast_in_dim.60
  25.2 6.8 %all-to-all-start = ((bf16[8,3,2,32,128]{4,3,2,1,0:T(8,128)(2,1)}), bf16[8,3,2,32,128]{4,3,2,1,0:T(8,128)(2,1)S(1)}, u32[]{:S(2)}, u32[]{:S(2)}) async-start(bf16[8,3,2,32,128]{4,3,2,1,0:T(8,128)(2,1)} %broadcast_in_dim.60), calls=%async_computation | async-start | bytes 786432 | tf_op jit(solution)/shard_map/all_to_all | solution.py:18
  32.2 0.1 add_multiply_fusion.2
  32.2 0.1 add_multiply_fusion
  32.3 10.4 %all-to-all-done.refs_0_ = bf16[8,3,2,32,128]{4,3,2,1,0:T(8,128)(2,1)S(1)} async-done(((bf16[8,3,2,32,128]{4,3,2,1,0:T(8,128)(2,1)}), bf16[8,3,2,32,128]{4,3,2,1,0:T(8,128)(2,1)S(1)}, u32[]{:S(2)}, u32[]{:S(2)}) %all-to-all-start) | async-done | bytes 393248 | tf_op jit(solution)/shard_map/all_to_all | solution.py:18
  42.7 3.4 %collective-permute-start.3 = (bf16[8,3,2,32,128]{4,3,2,1,0:T(8,128)(2,1)S(1)}, bf16[8,3,2,32,128]{4,3,2,1,0:T(8,128)(2,1)S(1)}, u32[]{:S(2)}, u32[]{:S(2)}) collective-permute-start(bf16[8,3,2,32,128]{4,3,2,1,0:T(8,128)(2,1)S(1)} %all-to-all-done.refs_0_), channel_id=1, source_target_pairs={{0,8},{4,68},{8,16},{12,76},{16,24},{20,84},{24,32},{28,92},{32,40... | collective-permute-start | bytes 1179656 | tf_op jit(solution)/shard_map/ppermute | solution.py:143
  46.1 10.0 %collective-permute-start.4 = (bf16[8,3,2,32,128]{4,3,2,1,0:T(8,128)(2,1)S(1)}, bf16[8,3,2,32,128]{4,3,2,1,0:T(8,128)(2,1)S(1)}, u32[]{:S(2)}, u32[]{:S(2)}) collective-permute-start(bf16[8,3,2,32,128]{4,3,2,1,0:T(8,128)(2,1)S(1)} %all-to-all-done.refs_0_), channel_id=1, source_target_pairs={{0,56},{4,708},{8,0},{12,716},{16,8},{20,724},{24,16},{28,732},{32... | collective-permute-start | bytes 1179656 | tf_op jit(solution)/shard_map/ppermute | solution.py:143
  56.1 1.9 %collective-permute-start.5 = (bf16[8,3,2,32,128]{4,3,2,1,0:T(8,128)(2,1)S(1)}, bf16[8,3,2,32,128]{4,3,2,1,0:T(8,128)(2,1)S(1)}, u32[]{:S(2)}, u32[]{:S(2)}) collective-permute-start(bf16[8,3,2,32,128]{4,3,2,1,0:T(8,128)(2,1)S(1)} %all-to-all-done.refs_0_), channel_id=1, source_target_pairs={{0,16},{4,132},{8,56},{12,140},{16,32},{20,148},{24,8},{28,156},{3... | collective-permute-start | bytes 1179656 | tf_op jit(solution)/shard_map/ppermute | solution.py:143
  58.0 0.6 pad_add_fusion
  58.6 0.6 and_select_fusion
  59.2 5.8 %collective-permute-start.6 = (bf16[8,3,2,32,128]{4,3,2,1,0:T(8,128)(2,1)S(1)}, bf16[8,3,2,32,128]{4,3,2,1,0:T(8,128)(2,1)S(1)}, u32[]{:S(2)}, u32[]{:S(2)}) collective-permute-start(bf16[8,3,2,32,128]{4,3,2,1,0:T(8,128)(2,1)S(1)} %all-to-all-done.refs_0_), channel_id=1, source_target_pairs={{0,4},{4,0},{8,12},{12,8},{16,20},{20,16},{24,28},{28,24},{32,36},... | collective-permute-start | bytes 1179656 | tf_op jit(solution)/shard_map/ppermute | solution.py:144
  65.0 0.0 collective-permute-done.3.refs_1_
  65.0 1.9 %collective-permute-start.7 = (bf16[8,3,2,32,128]{4,3,2,1,0:T(8,128)(2,1)S(1)}, bf16[8,3,2,32,128]{4,3,2,1,0:T(8,128)(2,1)}, u32[]{:S(2)}, u32[]{:S(2)}) collective-permute-start(bf16[8,3,2,32,128]{4,3,2,1,0:T(8,128)(2,1)S(1)} %collective-permute-done.3.refs_1_), channel_id=1, source_target_pairs={{0,4},{4,0},{8,12},{12,8},{16,20},{20,16},{24,28},{28,24},{32,36},... | collective-permute-start | bytes 1179656 | tf_op jit(solution)/shard_map/ppermute | solution.py:144
  66.9 0.0 collective-permute-done.4.refs_2_
  66.9 4.4 %collective-permute-start.8 = (bf16[8,3,2,32,128]{4,3,2,1,0:T(8,128)(2,1)S(1)}, bf16[8,3,2,32,128]{4,3,2,1,0:T(8,128)(2,1)}, u32[]{:S(2)}, u32[]{:S(2)}) collective-permute-start(bf16[8,3,2,32,128]{4,3,2,1,0:T(8,128)(2,1)S(1)} %collective-permute-done.4.refs_2_), channel_id=1, source_target_pairs={{0,4},{4,0},{8,12},{12,8},{16,20},{20,16},{24,28},{28,24},{32,36},... | collective-permute-start | bytes 1179656 | tf_op jit(solution)/shard_map/ppermute | solution.py:144
  71.4 0.0 collective-permute-done.5.refs_3_
  71.4 2.2 %collective-permute-start.9 = (bf16[8,3,2,32,128]{4,3,2,1,0:T(8,128)(2,1)S(1)}, bf16[8,3,2,32,128]{4,3,2,1,0:T(8,128)(2,1)}, u32[]{:S(2)}, u32[]{:S(2)}) collective-permute-start(bf16[8,3,2,32,128]{4,3,2,1,0:T(8,128)(2,1)S(1)} %collective-permute-done.5.refs_3_), channel_id=1, source_target_pairs={{0,4},{4,0},{8,12},{12,8},{16,20},{20,16},{24,28},{28,24},{32,36},... | collective-permute-start | bytes 1179656 | tf_op jit(solution)/shard_map/ppermute | solution.py:144
  73.6 0.5 and_select_fusion.1
  74.2 0.7 stack_broadcast_in_dim.5
  74.9 0.6 stack_broadcast_in_dim.4
  75.5 1.3 add_select_fusion
  76.9 1.6 %copy.10 = s32[2,4,8,3,2]{4,3,2,1,0:T(4,128)} copy(s32[2,4,8,3,2]{2,1,4,3,0:T(4,128)} %add_select_fusion) | data formatting | bytes 3072 | tf_op jit(solution)/shard_map/jit(_where)/select_n | solution.py:82
  78.5 1.0 select_n.224.place_ref
  79.5 0.0 copy-done.1
  79.5 0.1 reshape.320.fill_ref
  79.6 0.0 copy-start.2
  79.6 0.0 collective-permute-done.6.refs_4_
  79.6 0.0 collective-permute-done.7.refs_5_
  79.6 0.0 collective-permute-done.8.refs_6_
  79.6 0.0 collective-permute-done.9.refs_7_
  79.6 0.0 copy-done
  79.6 4.3 %shard_map.46 = f32[4,256,128]{2,1,0:T(8,128)} custom-call(s32[384]{0:T(512)S(1)} %select_n.224.place_ref, s32[48]{0:T(128)S(1)} %reshape.320.fill_ref, bf16[2,256,1536]{2,1,0:T(8,128)(2,1)S(1)} %copy-done, bf16[8,3,2,32,128]{4,3,2,1,0:T(8,128)(2,1)S(1)} %all-to-all-done.refs_0_, bf16[8,3,2,32,128]{4,3,2,1,0:T(8,128)(2,1)S(1)} %collective-permute-done.3.refs_1_, ...), custom_call_target="tpu_custom_call" | custom-call | flops 805306368 | bytes 5242880 | tf_op jit(solution)/shard_map/pallas_call | solution.py:120
  83.9 5.8 %all-to-all-start.1 = ((f32[4,256,128]{2,1,0:T(8,128)}), f32[4,256,128]{2,1,0:T(8,128)S(1)}, u32[]{:S(2)}, u32[]{:S(2)}) async-start(f32[4,256,128]{2,1,0:T(8,128)} %shard_map.46), calls=%async_computation.1 | async-start | bytes 1048576 | tf_op jit(solution)/shard_map/all_to_all | solution.py:146
  89.7 0.0 copy-done.2
  89.7 0.1 broadcast_in_dim.62
  89.8 0.1 convert_element_type.22
  89.9 9.0 %all-to-all-done.1 = f32[4,256,128]{2,1,0:T(8,128)S(1)} async-done(((f32[4,256,128]{2,1,0:T(8,128)}), f32[4,256,128]{2,1,0:T(8,128)S(1)}, u32[]{:S(2)}, u32[]{:S(2)}) %all-to-all-start.1) | async-done | bytes 524320 | tf_op jit(solution)/shard_map/all_to_all | solution.py:146
  98.9 0.1 fusion
  99.0 13.5 %all_to_all.20 = f32[16,8,128]{2,1,0:T(8,128)S(1)} all-to-all(f32[16,8,128]{2,1,0:T(8,128)S(1)} %broadcast_in_dim.63), channel_id=1, replica_groups={{0,4,8,12,16,20,24,28,32,36,40,44,48,52,56,60},{64,68,72,76,80,84,88,92..., dimensions={0} | all-to-all | bytes 131072 | tf_op jit(solution)/shard_map/all_to_all | solution.py:18
  112.6 0.6 broadcast_in_dim.64
  113.2 10.0 %all-to-all-start.3 = ((f32[12,8,128]{2,1,0:T(8,128)}), f32[12,8,128]{2,1,0:T(8,128)S(1)}, u32[]{:S(2)}, u32[]{:S(2)}) async-start(f32[12,8,128]{2,1,0:T(8,128)} %broadcast_in_dim.64), calls=%async_computation.3 | async-start | bytes 98304 | tf_op jit(solution)/shard_map/all_to_all | solution.py:18
  123.2 0.1 broadcast_bitcast_fusion
  123.3 9.5 %all-to-all-done.3 = f32[12,8,128]{2,1,0:T(8,128)S(1)} async-done(((f32[12,8,128]{2,1,0:T(8,128)}), f32[12,8,128]{2,1,0:T(8,128)S(1)}, u32[]{:S(2)}, u32[]{:S(2)}) %all-to-all-start.3) | async-done | bytes 49184 | tf_op jit(solution)/shard_map/all_to_all | solution.py:18
  132.8 0.8 multiply_multiply_fusion
  (16 shorter events, 0.2 us)
Async XLA Ops:
  0.0 79.5 %copy-start.1 = (s32[2,2,12]{2,1,0:T(2,128)S(1)}, s32[2,2,12]{2,1,0:T(2,128)}, u32[]{:S(2)}) copy-start(s32[2,2,12]{2,1,0:T(2,128)} %param.5) | copy-start | bytes 580
  0.0 79.6 %copy-start = (bf16[2,256,1536]{2,1,0:T(8,128)(2,1)S(1)}, bf16[2,256,1536]{2,1,0:T(8,128)(2,1)}, u32[]{:S(2)}) copy-start(bf16[2,256,1536]{2,1,0:T(8,128)(2,1)} %slab_ref.1) | copy-start | bytes 4718596
  0.0 21.8 %collective-permute-start = (bf16[2,32,128]{2,1,0:T(8,128)(2,1)}, bf16[2,32,128]{2,1,0:T(8,128)(2,1)S(1)}, u32[]{:S(2)}, u32[]{:S(2)}) collective-permute-start(bf16[2,32,128]{2,1,0:T(8,128)(2,1)} %param.6), channel_id=1, source_target_pairs={{0,0},{1,64},{2,128},{3,192},{4,4},{5,68},{6,132},{7,196},{8,8},{9... | collective-permute-start | bytes 49160 | tf_op jit(solution)/shard_map/ppermute | solution.py:141
  1.5 20.3 %collective-permute-start.1 = (bf16[2,32,128]{2,1,0:T(8,128)(2,1)}, bf16[2,32,128]{2,1,0:T(8,128)(2,1)S(1)}, u32[]{:S(2)}, u32[]{:S(2)}) collective-permute-start(bf16[2,32,128]{2,1,0:T(8,128)(2,1)} %param.6), channel_id=1, source_target_pairs={{0,256},{1,320},{2,384},{3,448},{4,260},{5,324},{6,388},{7,452},{8... | collective-permute-start | bytes 49160 | tf_op jit(solution)/shard_map/ppermute | solution.py:141
  14.7 9.6 %collective-permute-start.2 = (bf16[2,32,128]{2,1,0:T(8,128)(2,1)}, bf16[2,32,128]{2,1,0:T(8,128)(2,1)S(1)}, u32[]{:S(2)}, u32[]{:S(2)}) collective-permute-start(bf16[2,32,128]{2,1,0:T(8,128)(2,1)} %param.6), channel_id=1, source_target_pairs={{0,512},{1,576},{2,640},{3,704},{4,516},{5,580},{6,644},{7,708},{8... | collective-permute-start | bytes 49160 | tf_op jit(solution)/shard_map/ppermute | solution.py:141
  25.2 17.6 %all-to-all-start = ((bf16[8,3,2,32,128]{4,3,2,1,0:T(8,128)(2,1)}), bf16[8,3,2,32,128]{4,3,2,1,0:T(8,128)(2,1)S(1)}, u32[]{:S(2)}, u32[]{:S(2)}) async-start(bf16[8,3,2,32,128]{4,3,2,1,0:T(8,128)(2,1)} %broadcast_in_dim.60), calls=%async_computation | async-start | bytes 786432 | tf_op jit(solution)/shard_map/all_to_all | solution.py:18
  42.7 22.2 %collective-permute-start.3 = (bf16[8,3,2,32,128]{4,3,2,1,0:T(8,128)(2,1)S(1)}, bf16[8,3,2,32,128]{4,3,2,1,0:T(8,128)(2,1)S(1)}, u32[]{:S(2)}, u32[]{:S(2)}) collective-permute-start(bf16[8,3,2,32,128]{4,3,2,1,0:T(8,128)(2,1)S(1)} %all-to-all-done.refs_0_), channel_id=1, source_target_pairs={{0,8},{4,68},{8,16},{12,76},{16,24},{20,84},{24,32},{28,92},{32,40... | collective-permute-start | bytes 1179656 | tf_op jit(solution)/shard_map/ppermute | solution.py:143
  46.1 20.8 %collective-permute-start.4 = (bf16[8,3,2,32,128]{4,3,2,1,0:T(8,128)(2,1)S(1)}, bf16[8,3,2,32,128]{4,3,2,1,0:T(8,128)(2,1)S(1)}, u32[]{:S(2)}, u32[]{:S(2)}) collective-permute-start(bf16[8,3,2,32,128]{4,3,2,1,0:T(8,128)(2,1)S(1)} %all-to-all-done.refs_0_), channel_id=1, source_target_pairs={{0,56},{4,708},{8,0},{12,716},{16,8},{20,724},{24,16},{28,732},{32... | collective-permute-start | bytes 1179656 | tf_op jit(solution)/shard_map/ppermute | solution.py:143
  56.1 15.3 %collective-permute-start.5 = (bf16[8,3,2,32,128]{4,3,2,1,0:T(8,128)(2,1)S(1)}, bf16[8,3,2,32,128]{4,3,2,1,0:T(8,128)(2,1)S(1)}, u32[]{:S(2)}, u32[]{:S(2)}) collective-permute-start(bf16[8,3,2,32,128]{4,3,2,1,0:T(8,128)(2,1)S(1)} %all-to-all-done.refs_0_), channel_id=1, source_target_pairs={{0,16},{4,132},{8,56},{12,140},{16,32},{20,148},{24,8},{28,156},{3... | collective-permute-start | bytes 1179656 | tf_op jit(solution)/shard_map/ppermute | solution.py:143
  59.2 20.4 %collective-permute-start.6 = (bf16[8,3,2,32,128]{4,3,2,1,0:T(8,128)(2,1)S(1)}, bf16[8,3,2,32,128]{4,3,2,1,0:T(8,128)(2,1)S(1)}, u32[]{:S(2)}, u32[]{:S(2)}) collective-permute-start(bf16[8,3,2,32,128]{4,3,2,1,0:T(8,128)(2,1)S(1)} %all-to-all-done.refs_0_), channel_id=1, source_target_pairs={{0,4},{4,0},{8,12},{12,8},{16,20},{20,16},{24,28},{28,24},{32,36},... | collective-permute-start | bytes 1179656 | tf_op jit(solution)/shard_map/ppermute | solution.py:144
  65.0 14.6 %collective-permute-start.7 = (bf16[8,3,2,32,128]{4,3,2,1,0:T(8,128)(2,1)S(1)}, bf16[8,3,2,32,128]{4,3,2,1,0:T(8,128)(2,1)}, u32[]{:S(2)}, u32[]{:S(2)}) collective-permute-start(bf16[8,3,2,32,128]{4,3,2,1,0:T(8,128)(2,1)S(1)} %collective-permute-done.3.refs_1_), channel_id=1, source_target_pairs={{0,4},{4,0},{8,12},{12,8},{16,20},{20,16},{24,28},{28,24},{32,36},... | collective-permute-start | bytes 1179656 | tf_op jit(solution)/shard_map/ppermute | solution.py:144
  66.9 12.7 %collective-permute-start.8 = (bf16[8,3,2,32,128]{4,3,2,1,0:T(8,128)(2,1)S(1)}, bf16[8,3,2,32,128]{4,3,2,1,0:T(8,128)(2,1)}, u32[]{:S(2)}, u32[]{:S(2)}) collective-permute-start(bf16[8,3,2,32,128]{4,3,2,1,0:T(8,128)(2,1)S(1)} %collective-permute-done.4.refs_2_), channel_id=1, source_target_pairs={{0,4},{4,0},{8,12},{12,8},{16,20},{20,16},{24,28},{28,24},{32,36},... | collective-permute-start | bytes 1179656 | tf_op jit(solution)/shard_map/ppermute | solution.py:144
  71.4 8.2 %collective-permute-start.9 = (bf16[8,3,2,32,128]{4,3,2,1,0:T(8,128)(2,1)S(1)}, bf16[8,3,2,32,128]{4,3,2,1,0:T(8,128)(2,1)}, u32[]{:S(2)}, u32[]{:S(2)}) collective-permute-start(bf16[8,3,2,32,128]{4,3,2,1,0:T(8,128)(2,1)S(1)} %collective-permute-done.5.refs_3_), channel_id=1, source_target_pairs={{0,4},{4,0},{8,12},{12,8},{16,20},{20,16},{24,28},{28,24},{32,36},... | collective-permute-start | bytes 1179656 | tf_op jit(solution)/shard_map/ppermute | solution.py:144
  79.6 10.1 %copy-start.2 = (s32[2,1]{0,1:T(1,128)S(1)}, s32[2,1]{0,1:T(1,128)}, u32[]{:S(2)}) copy-start(s32[2,1]{0,1:T(1,128)} %param.7) | copy-start | bytes 28
  83.9 14.9 %all-to-all-start.1 = ((f32[4,256,128]{2,1,0:T(8,128)}), f32[4,256,128]{2,1,0:T(8,128)S(1)}, u32[]{:S(2)}, u32[]{:S(2)}) async-start(f32[4,256,128]{2,1,0:T(8,128)} %shard_map.46), calls=%async_computation.1 | async-start | bytes 1048576 | tf_op jit(solution)/shard_map/all_to_all | solution.py:146
  113.2 19.6 %all-to-all-start.3 = ((f32[12,8,128]{2,1,0:T(8,128)}), f32[12,8,128]{2,1,0:T(8,128)S(1)}, u32[]{:S(2)}, u32[]{:S(2)}) async-start(f32[12,8,128]{2,1,0:T(8,128)} %broadcast_in_dim.64), calls=%async_computation.3 | async-start | bytes 98304 | tf_op jit(solution)/shard_map/all_to_all | solution.py:18

commit v3 on v0

v3 whole, which is shorter than its diff:
```python
import jax
import jax.numpy as jnp
from jax import lax
from jax.experimental import pallas as pl
from jax.experimental.pallas import tpu as pltpu
from jax.sharding import PartitionSpec as P

TILE = 128
NZ, NY, NC, NX = 12, 8, 2, 4
DEPTH = 32
SLOTS = 6
TAIL = 16


def row_of(z, y, core):
    return (z % NZ) * NY * NC + (y % NY) * NC + core


def spread(piece, axis, size, groups):
    copies = jnp.broadcast_to(piece[None], (size,) + piece.shape)
    return lax.all_to_all(copies, axis, 0, 0, tiled=True, axis_index_groups=groups)


def step_of(position, shift):
    if shift == 2:
        return 2 if position % 2 == 0 else -2
    return shift


def shift_moves(shift):
    moves = []
    for z in range(NZ):
        for y in range(NY):
            moves.append((row_of(z, y, 0), row_of(z, y + step_of(y, shift), 0)))
            moves.append((row_of(z, y, 1), row_of(z + step_of(z, shift), y, 1)))
    return moves


SHIFTS = (0, 1, -1, 2)
MIXED_GROUPS = [
    [row_of(z, b + 4 * h, 0) for z in range(NZ) for h in range(2)] for b in range(4)
] + [[row_of(j + 4 * i, y, 1) for i in range(3) for y in range(NY)] for j in range(4)]
GROUP = 24
PLANE_GROUPS = [[row_of(z, j // 2, j % 2) for j in range(NY * NC)] for z in range(NZ)]
Z_GROUPS = [[row_of(z, j // 2, j % 2) for z in range(NZ)] for j in range(NY * NC)]
SWAP = [(r, r ^ 1) for r in range(NZ * NY * NC)]


def pack_kernel(fill_ref, slab_ref, tail_ref, out_ref, tile_sems, tail_sem):
    sections, rows = slab_ref.shape[0], slab_ref.shape[1] // TILE
    cols = slab_ref.shape[2] // TILE

    def tile_copy(group, k, slot):
        s, r = group // rows, group % rows
        return pltpu.make_async_copy(
            slab_ref.at[s, pl.ds(r * TILE, TILE), pl.ds(k * TILE, TILE)],
            out_ref.at[pl.ds(group * TILE, TILE), pl.ds(pl.multiple_of(slot * TILE, TILE), TILE)],
            tile_sems.at[group, slot],
        )

    tail = pltpu.make_async_copy(
        tail_ref, out_ref.at[pl.ds(sections * rows * TILE, TAIL)], tail_sem
    )
    tail.start()
    for group in range(sections * rows):
        count = jnp.int32(0)
        for k in range(cols):
            count += fill_ref[group * cols + k]
        seen = jnp.int32(0)
        for k in range(cols):
            filled = fill_ref[group * cols + k]
            slot = jnp.where(filled == 1, seen, count + k - seen)
            seen += filled

            @pl.when(slot < SLOTS)
            def _(group=group, k=k, slot=slot):
                tile_copy(group, k, slot).start()

    for group in range(sections * rows):
        for slot in range(SLOTS):
            tile_copy(group, 0, slot).wait()
    tail.wait()


def pack(slab, slab_fill):
    sections, rows, cols = slab.shape
    groups = sections * rows // TILE
    fill = slab_fill.reshape(groups, cols // TILE)
    seen = jnp.cumsum(fill, axis=1) - fill
    count = jnp.sum(fill, axis=1, keepdims=True)
    k = jnp.arange(cols // TILE)[None, :]
    slot = jnp.where(fill == 1, seen, count + k - seen)
    hit = slot[:, None, :] == jnp.arange(SLOTS)[None, :, None]
    order = jnp.sum(jnp.where(hit, k[:, None, :], 0), axis=2)
    words = jnp.concatenate([order, count], axis=1).reshape(-1).astype(jnp.bfloat16)
    tail = jnp.pad(words[None, :], ((0, TAIL - 1), (0, SLOTS * TILE - words.shape[0])))
    anywhere = pl.BlockSpec(memory_space=pl.ANY)
    return pl.pallas_call(
        pack_kernel,
        out_shape=jax.ShapeDtypeStruct((groups * TILE + TAIL, SLOTS * TILE), jnp.bfloat16),
        in_specs=[pl.BlockSpec(memory_space=pltpu.SMEM), anywhere, anywhere],
        out_specs=anywhere,
        scratch_shapes=[pltpu.SemaphoreType.DMA((groups, SLOTS)), pltpu.SemaphoreType.DMA],
        cost_estimate=pl.CostEstimate(flops=0, bytes_accessed=2 * 2**20, transcendentals=0),
    )(fill.reshape(-1), slab, tail)


def product_kernel(place_ref, words_ref, keep_ref, *refs):
    lefts, pieces = refs[:NX], refs[NX : NX + 8]
    out_ref, sums_ref, right_ref, near_ref = refs[NX + 8 :]
    sections = right_ref.shape[0]
    row, col = place_ref[0], place_ref[1]
    z, y, core = row // (NY * NC), (row // NC) % NY, row % NC
    for index, piece in enumerate(pieces):
        step = index % 4
        if step == 3:
            y_from = jnp.where(y % 2 == 0, y - 2, y + 2)
            z_from = jnp.where(z % 2 == 0, z - 2, z + 2)
        else:
            y_from, z_from = y - SHIFTS[step], z - SHIFTS[step]
        along_y = (core == 0) == (index < 4)
        first = jnp.where(along_y, (y_from + NY) % 4 * 64, (z_from + NZ) % 4 * 512 + DEPTH)
        for slot in range(GROUP):
            offset = jnp.where(
                along_y, slot // 2 * 512 + slot % 2 * 256, slot // 8 * 2048 + slot % 8 * 64
            )
            at = pl.multiple_of(first + offset, DEPTH)
            for s in range(sections):
                right_ref[s, pl.ds(at, DEPTH)] = piece[slot, s]

    row_blocks = out_ref.shape[0] // TILE
    per_source = sections * row_blocks * (SLOTS + 1)
    colsum = jnp.zeros((8, TILE), jnp.float32)
    for r in range(row_blocks):
        total = jnp.zeros((TILE, TILE), jnp.float32)
        for source in range(NX):
            block_col = (col + (0, NX - 1, 1, 2)[source]) % NX
            for s in range(sections):
                group = s * row_blocks + r
                base = source * per_source + group * (SLOTS + 1)
                count = words_ref[base + SLOTS]
                parts = []
                for slot in range(SLOTS):
                    tile = block_col * 12 + words_ref[base + slot]
                    rows = pl.ds(pl.multiple_of(tile * TILE, TILE), TILE)
                    keep = (slot < count).astype(jnp.float32).astype(jnp.bfloat16)
                    near_ref[slot * TILE : (slot + 1) * TILE] = right_ref[s, rows] * keep
                left = lefts[source][group * TILE : (group + 1) * TILE, :]
                total += jnp.dot(left, near_ref[...], preferred_element_type=jnp.float32)
        squares = total * total * keep_ref[r].astype(jnp.float32)
        out_ref[r * TILE : (r + 1) * TILE] = squares
        colsum += jnp.sum(squares.reshape(TILE // 8, 8, TILE), axis=0)
    sums_ref[...] = jnp.broadcast_to(colsum[None], sums_ref.shape)


def multiply(place, words, keep, lefts, pieces, sections, rows):
    smem = pl.BlockSpec(memory_space=pltpu.SMEM)
    vmem = pl.BlockSpec(memory_space=pltpu.VMEM)
    depth = NZ * NY * NC * DEPTH
    return pl.pallas_call(
        product_kernel,
        out_shape=(
            jax.ShapeDtypeStruct((rows, TILE), jnp.float32),
            jax.ShapeDtypeStruct((NY * NC, 8, TILE), jnp.float32),
        ),
        in_specs=[smem, smem, smem] + [vmem] * (NX + 8),
        out_specs=(vmem, vmem),
        scratch_shapes=[
            pltpu.VMEM((sections, depth, TILE), jnp.bfloat16),
            pltpu.VMEM((SLOTS * TILE, TILE), jnp.bfloat16),
        ],
        compiler_params=pltpu.CompilerParams(vmem_limit_bytes=32 * 2**20),
        cost_estimate=pl.CostEstimate(
            flops=sections * rows * depth * TILE, bytes_accessed=7 * 2**20, transcendentals=0
        ),
    )(place, words, keep, *lefts, *pieces)


def shards(slab, slab_fill, panel, out_fill):
    sections, row_count, local_cols = slab.shape
    place = jnp.stack([lax.axis_index("row"), lax.axis_index("col")]).astype(jnp.int32)
    held = spread(panel, "row", GROUP, MIXED_GROUPS)
    packed = pack(slab, slab_fill)
    lefts = [packed] + [
        lax.ppermute(packed, "col", [(x, (x + s) % NX) for x in range(NX)]) for s in SHIFTS[1:]
    ]
    mine = [held] + [lax.ppermute(held, "row", shift_moves(s)) for s in SHIFTS[1:]]
    theirs = [lax.ppermute(piece, "row", SWAP) for piece in mine]
    tail = sections * row_count
    count = sections * row_count // TILE * (SLOTS + 1)
    words = jnp.concatenate([left[tail, :count] for left in lefts]).astype(jnp.int32)
    squares, sums = multiply(
        place, words, out_fill.reshape(-1), lefts, mine + theirs, sections, row_count
    )
    sums = lax.all_to_all(sums, "row", 0, 0, tiled=True, axis_index_groups=PLANE_GROUPS)
    sums = jnp.sum(sums, axis=0)
    sums = jnp.sum(spread(sums, "row", NZ, Z_GROUPS), axis=(0, 1))
    factor_col = jnp.float32(row_count * NZ * NY * NC) / sums
    return squares * factor_col


def solution(mesh):
    placed = (P(None, "row", "col"), P(None, "row", "col"), P(None, "row", "col"), P("row", "col"))
    return jax.shard_map(
        shards, mesh=mesh, in_specs=placed, out_specs=P("row", "col"), check_vma=False
    )
```

time: 702 us -> 142 us (0.20)
  blocking collectives: 369 us -> 32.7 us
  waiting for transfers between devices: 305 us -> 19 us
  starting transfers between devices: 0.09 us -> 51.7 us
  Pallas kernels: 0 us -> 28.8 us
  between operations: 13.2 us -> 0.21 us
    psum x1 -> x0, blocking collectives: 369 us -> none  [shards(): column_sums = lax.psum(jnp.sum(squares, axis=0), 'row')]
    all_gather x3 -> x0, waiting for transfers between devices: 304 us -> none  [the longest x2 231 us: shards(): lax.all_gather(panel[step_index], 'row', axis=0, tiled=True)]
    all_to_all x0 -> x2, blocking collectives: none -> 32.7 us  [the longest x1 18.2 us: spread(): lax.all_to_all(copies, axis, 0, 0, tiled=True, axis_index_groups=groups)]
    ppermute x0 -> x10, starting transfers between devices: none -> 31.5 us  [the longest x3 12 us: shards(): lax.ppermute(held, 'row', shift_moves(s))]
    pallas_call x0 -> x2, Pallas kernels: none -> 28.8 us  [the longest x1 26.6 us: pack(): pl.pallas_call(pack_kernel, out_shape=jax.ShapeDtypeStruct((groups * TILE...]
    all_to_all x0 -> x1, starting transfers between devices: none -> 20.1 us  [spread(): lax.all_to_all(copies, axis, 0, 0, tiled=True, axis_index_groups=groups)]
    ppermute x0 -> x10, waiting for transfers between devices: none -> 19 us  [the longest x3 17.4 us: shards(): lax.ppermute(packed, 'col', [(x, (x + s) % NX) for x in range(NX)])]
  transfers between devices with their start and end apart: 3 -> 11, of which waited for: 3 -> 3; matrix products, arithmetic and copies ran while one was open for 1% -> 4% of each run, Pallas kernels for 0% -> 19%
where the time goes in v3:
time: 142 us; the launch traced here: 141 us
  starting transfers between devices  51.7 us (36%)
  blocking collectives  32.7 us (23%)
  Pallas kernels  28.8 us (20%)
  waiting for transfers between devices  19 us (13%)
  local copies, waits for them, and re-layouts  5.65 us (4%)
  other arithmetic  3.48 us (2%)
    pallas_call x1, Pallas kernels, pack(): pl.pallas_call(pack_kernel, out_shape=jax.ShapeDtypeStruct((groups * TILE...  26.6 us
    all_to_all x1, starting transfers between devices, spread(): lax.all_to_all(copies, axis, 0, 0, tiled=True, axis_index_groups=groups)  20.1 us
    all_to_all x1, blocking collectives, spread(): lax.all_to_all(copies, axis, 0, 0, tiled=True, axis_index_groups=groups)  18.2 us
    ppermute x3, waiting for transfers between devices, shards(): lax.ppermute(packed, 'col', [(x, (x + s) % NX) for x in range(NX)])  17.4 us
    all_to_all x1, blocking collectives, shards(): lax.all_to_all(sums, 'row', 0, 0, tiled=True, axis_index_groups=PLANE_GRO...  14.5 us
    ppermute x3, starting transfers between devices, shards(): lax.ppermute(held, 'row', shift_moves(s))  12 us
    ppermute x3, starting transfers between devices, shards(): lax.ppermute(packed, 'col', [(x, (x + s) % NX) for x in range(NX)])  9.93 us
    ppermute x4, starting transfers between devices, shards(): theirs = [lax.ppermute(piece, 'row', SWAP) for piece in mine]  9.59 us
  transfers between devices with their start and end apart: 11, of which 3 were waited for; matrix products, arithmetic and copies ran while one was open for 4% of the time, Pallas kernels for 19%

profile of v3, /device:TPU:1, one launch (start us, length us, event | category | flops | bytes accessed | tf_op | source)
XLA Modules:
  0.0 141.4 jit_solution(442203567372092504)
XLA Ops:
  0.0 1.5 %broadcast_in_dim.36 = bf16[24,2,32,128]{3,2,1,0:T(8,128)(2,1)} broadcast(bf16[2,32,128]{2,1,0:T(8,128)(2,1)} %param.6), dimensions={1,2,3} | broadcast | bytes 409600 | tf_op jit(solution)/shard_map/broadcast_in_dim | solution.py:20
  1.5 0.0 copy-start.1
  1.5 20.1 %all-to-all-start = ((bf16[24,2,32,128]{3,2,1,0:T(8,128)(2,1)}), bf16[24,2,32,128]{3,2,1,0:T(8,128)(2,1)S(1)}, u32[]{:S(2)}, u32[]{:S(2)}) async-start(bf16[24,2,32,128]{3,2,1,0:T(8,128)(2,1)} %broadcast_in_dim.36), calls=%async_computation | async-start | bytes 786432 | tf_op jit(solution)/shard_map/all_to_all | solution.py:21
  21.7 0.8 reduce_sum.36
  22.5 0.1 add.21
  22.5 0.9 reduce_window_sum.11
  23.4 0.8 subtract_select_fusion
  24.2 1.3 reshape_reshape.3.fill_ref
  25.5 0.1 broadcast_in_dim.21
  25.6 0.2 select_reduce_fusion
  25.8 0.1 copy.6
  25.9 0.1 convert_element_type.16
  25.9 0.6 pad.4.tail_ref
  26.6 26.6 %shard_map.46.refs_0_ = bf16[528,768]{1,0:T(8,128)(2,1)} custom-call(s32[48]{0:T(128)} %reshape_reshape.3.fill_ref, bf16[2,256,1536]{2,1,0:T(8,128)(2,1)} %slab_ref.1, bf16[16,768]{1,0:T(8,128)(2,1)} %pad.4.tail_ref), custom_call_target="tpu_custom_call" | custom-call | bytes 2097152 | tf_op jit(solution)/shard_map/pallas_call | solution.py:98
  53.1 4.7 %collective-permute-start.2 = (bf16[528,768]{1,0:T(8,128)(2,1)}, bf16[528,768]{1,0:T(8,128)(2,1)S(1)}, u32[]{:S(2)}, u32[]{:S(2)}) collective-permute-start(bf16[528,768]{1,0:T(8,128)(2,1)} %shard_map.46.refs_0_), channel_id=1, source_target_pairs={{0,2},{1,3},{2,0},{3,1},{4,6},{5,7},{6,4},{7,5},{8,10},{9,11},{10,... | collective-permute-start | bytes 2433032 | tf_op jit(solution)/shard_map/ppermute | solution.py:185
  57.8 2.8 %collective-permute-start.1 = (bf16[528,768]{1,0:T(8,128)(2,1)}, bf16[528,768]{1,0:T(8,128)(2,1)S(1)}, u32[]{:S(2)}, u32[]{:S(2)}) collective-permute-start(bf16[528,768]{1,0:T(8,128)(2,1)} %shard_map.46.refs_0_), channel_id=1, source_target_pairs={{0,3},{1,0},{2,1},{3,2},{4,7},{5,4},{6,5},{7,6},{8,11},{9,8},{10,9... | collective-permute-start | bytes 2433032 | tf_op jit(solution)/shard_map/ppermute | solution.py:185
  60.6 2.5 %collective-permute-start = (bf16[528,768]{1,0:T(8,128)(2,1)}, bf16[528,768]{1,0:T(8,128)(2,1)S(1)}, u32[]{:S(2)}, u32[]{:S(2)}) collective-permute-start(bf16[528,768]{1,0:T(8,128)(2,1)} %shard_map.46.refs_0_), channel_id=1, source_target_pairs={{0,1},{1,2},{2,3},{3,0},{4,5},{5,6},{6,7},{7,4},{8,9},{9,10},{10,1... | collective-permute-start | bytes 2433032 | tf_op jit(solution)/shard_map/ppermute | solution.py:185
  63.1 0.1 pad_add_fusion.place_ref
  63.2 0.0 all-to-all-done.refs_4_
  63.2 4.0 %collective-permute-start.5 = (bf16[24,2,32,128]{3,2,1,0:T(8,128)(2,1)S(1)}, bf16[24,2,32,128]{3,2,1,0:T(8,128)(2,1)S(1)}, u32[]{:S(2)}, u32[]{:S(2)}) collective-permute-start(bf16[24,2,32,128]{3,2,1,0:T(8,128)(2,1)S(1)} %all-to-all-done.refs_4_), channel_id=1, source_target_pairs={{0,16},{4,132},{8,56},{12,140},{16,32},{20,148},{24,8},{28,156},{3... | collective-permute-start | bytes 1179656 | tf_op jit(solution)/shard_map/ppermute | solution.py:187
  67.2 5.3 %collective-permute-start.4 = (bf16[24,2,32,128]{3,2,1,0:T(8,128)(2,1)S(1)}, bf16[24,2,32,128]{3,2,1,0:T(8,128)(2,1)S(1)}, u32[]{:S(2)}, u32[]{:S(2)}) collective-permute-start(bf16[24,2,32,128]{3,2,1,0:T(8,128)(2,1)S(1)} %all-to-all-done.refs_4_), channel_id=1, source_target_pairs={{0,56},{4,708},{8,0},{12,716},{16,8},{20,724},{24,16},{28,732},{32... | collective-permute-start | bytes 1179656 | tf_op jit(solution)/shard_map/ppermute | solution.py:187
  72.5 1.7 %collective-permute-done.2.refs_3_ = bf16[528,768]{1,0:T(8,128)(2,1)S(1)} collective-permute-done((bf16[528,768]{1,0:T(8,128)(2,1)}, bf16[528,768]{1,0:T(8,128)(2,1)S(1)}, u32[]{:S(2)}, u32[]{:S(2)}) %collective-permute-start.2) | collective-permute-done | bytes 811040 | tf_op jit(solution)/shard_map/ppermute | solution.py:185
  74.2 2.7 %collective-permute-start.3 = (bf16[24,2,32,128]{3,2,1,0:T(8,128)(2,1)S(1)}, bf16[24,2,32,128]{3,2,1,0:T(8,128)(2,1)S(1)}, u32[]{:S(2)}, u32[]{:S(2)}) collective-permute-start(bf16[24,2,32,128]{3,2,1,0:T(8,128)(2,1)S(1)} %all-to-all-done.refs_4_), channel_id=1, source_target_pairs={{0,8},{4,68},{8,16},{12,76},{16,24},{20,84},{24,32},{28,92},{32,40... | collective-permute-start | bytes 1179656 | tf_op jit(solution)/shard_map/ppermute | solution.py:187
  76.9 0.7 slice_bitcast_fusion.3
  77.6 15.7 %collective-permute-done.1.refs_2_ = bf16[528,768]{1,0:T(8,128)(2,1)S(1)} collective-permute-done((bf16[528,768]{1,0:T(8,128)(2,1)}, bf16[528,768]{1,0:T(8,128)(2,1)S(1)}, u32[]{:S(2)}, u32[]{:S(2)}) %collective-permute-start.1) | collective-permute-done | bytes 811040 | tf_op jit(solution)/shard_map/ppermute | solution.py:185
  93.3 3.3 %collective-permute-start.6 = (bf16[24,2,32,128]{3,2,1,0:T(8,128)(2,1)S(1)}, bf16[24,2,32,128]{3,2,1,0:T(8,128)(2,1)S(1)}, u32[]{:S(2)}, u32[]{:S(2)}) collective-permute-start(bf16[24,2,32,128]{3,2,1,0:T(8,128)(2,1)S(1)} %all-to-all-done.refs_4_), channel_id=1, source_target_pairs={{0,4},{4,0},{8,12},{12,8},{16,20},{20,16},{24,28},{28,24},{32,36},... | collective-permute-start | bytes 1179656 | tf_op jit(solution)/shard_map/ppermute | solution.py:188
  96.6 0.0 collective-permute-done.5.refs_7_
  96.7 1.9 %collective-permute-start.9 = (bf16[24,2,32,128]{3,2,1,0:T(8,128)(2,1)S(1)}, bf16[24,2,32,128]{3,2,1,0:T(8,128)(2,1)S(1)}, u32[]{:S(2)}, u32[]{:S(2)}) collective-permute-start(bf16[24,2,32,128]{3,2,1,0:T(8,128)(2,1)S(1)} %collective-permute-done.5.refs_7_), channel_id=1, source_target_pairs={{0,4},{4,0},{8,12},{12,8},{16,20},{20,16},{24,28},{28,24},{32,36},... | collective-permute-start | bytes 1179656 | tf_op jit(solution)/shard_map/ppermute | solution.py:188
  98.6 0.0 collective-permute-done.4.refs_6_
  98.6 2.4 %collective-permute-start.8 = (bf16[24,2,32,128]{3,2,1,0:T(8,128)(2,1)S(1)}, bf16[24,2,32,128]{3,2,1,0:T(8,128)(2,1)S(1)}, u32[]{:S(2)}, u32[]{:S(2)}) collective-permute-start(bf16[24,2,32,128]{3,2,1,0:T(8,128)(2,1)S(1)} %collective-permute-done.4.refs_6_), channel_id=1, source_target_pairs={{0,4},{4,0},{8,12},{12,8},{16,20},{20,16},{24,28},{28,24},{32,36},... | collective-permute-start | bytes 1179656 | tf_op jit(solution)/shard_map/ppermute | solution.py:188
  101.0 0.0 collective-permute-done.3.refs_5_
  101.0 1.9 %collective-permute-start.7 = (bf16[24,2,32,128]{3,2,1,0:T(8,128)(2,1)S(1)}, bf16[24,2,32,128]{3,2,1,0:T(8,128)(2,1)S(1)}, u32[]{:S(2)}, u32[]{:S(2)}) collective-permute-start(bf16[24,2,32,128]{3,2,1,0:T(8,128)(2,1)S(1)} %collective-permute-done.3.refs_5_), channel_id=1, source_target_pairs={{0,4},{4,0},{8,12},{12,8},{16,20},{20,16},{24,28},{28,24},{32,36},... | collective-permute-start | bytes 1179656 | tf_op jit(solution)/shard_map/ppermute | solution.py:188
  103.0 0.0 collective-permute-done.refs_1_
  103.0 0.1 maximum_convert_fusion.words_ref
  103.1 0.0 collective-permute-done.6.refs_8_
  103.1 0.0 collective-permute-done.9.refs_11_
  103.1 0.0 collective-permute-done.8.refs_10_
  103.1 1.6 %collective-permute-done.7.refs_9_ = bf16[24,2,32,128]{3,2,1,0:T(8,128)(2,1)S(1)} collective-permute-done((bf16[24,2,32,128]{3,2,1,0:T(8,128)(2,1)S(1)}, bf16[24,2,32,128]{3,2,1,0:T(8,128)(2,1)S(1)}, u32[]{:S(2)}, u32[]{:S(2)}) %collective-permute-start.7) | collective-permute-done | bytes 393248 | tf_op jit(solution)/shard_map/ppermute | solution.py:188
  104.6 0.0 copy-done.1
  104.6 0.0 copy-start
  104.6 1.1 copy-done
  105.8 2.2 %shard_map.47 = (f32[256,128]{1,0:T(8,128)S(1)}, f32[16,8,128]{2,1,0:T(8,128)S(1)}) custom-call(s32[2]{0:T(128)S(1)} %pad_add_fusion.place_ref, s32[112]{0:T(128)S(1)} %maximum_convert_fusion.words_ref, s32[2]{0:T(128)S(1)} %bitcast.12, bf16[528,768]{1,0:T(8,128)(2,1)S(1)} %copy-done, bf16[528,768]{1,0:T(8,128)(2,1)S(1)} %collective-permute-done.refs_1_, ...), custom_call_target="tpu_custom_call" | custom-call | flops 402653184 | bytes 7340032 | tf_op jit(solution)/shard_map/pallas_call | solution.py:160
  108.0 14.5 %all_to_all.15 = f32[16,8,128]{2,1,0:T(8,128)S(1)} all-to-all(f32[16,8,128]{2,1,0:T(8,128)S(1)} %get-tuple-element.8), channel_id=1, replica_groups={{0,4,8,12,16,20,24,28,32,36,40,44,48,52,56,60},{64,68,72,76,80,84,88,92..., dimensions={0} | all-to-all | bytes 131072 | tf_op jit(solution)/shard_map/all_to_all | solution.py:195
  122.5 18.2 %all_to_all.16 = f32[12,8,128]{2,1,0:T(8,128)S(1)} all-to-all(f32[12,8,128]{2,1,0:T(8,128)S(1)} %broadcast_in_dim.37), channel_id=1, replica_groups={{0,64,128,192,256,320,384,448,512,576,640,704},{4,68,132,196,260,324,38..., dimensions={0} | all-to-all | bytes 98304 | tf_op jit(solution)/shard_map/all_to_all | solution.py:21
  140.7 0.7 broadcast_multiply_fusion
  (10 shorter events, 0.1 us)
Async XLA Ops:
  1.5 103.1 %copy-start.1 = (s32[2,1]{0,1:T(1,128)S(1)}, s32[2,1]{0,1:T(1,128)}, u32[]{:S(2)}) copy-start(s32[2,1]{0,1:T(1,128)} %param.7) | copy-start | bytes 28
  1.5 61.6 %all-to-all-start = ((bf16[24,2,32,128]{3,2,1,0:T(8,128)(2,1)}), bf16[24,2,32,128]{3,2,1,0:T(8,128)(2,1)S(1)}, u32[]{:S(2)}, u32[]{:S(2)}) async-start(bf16[24,2,32,128]{3,2,1,0:T(8,128)(2,1)} %broadcast_in_dim.36), calls=%async_computation | async-start | bytes 786432 | tf_op jit(solution)/shard_map/all_to_all | solution.py:21
  53.1 21.1 %collective-permute-start.2 = (bf16[528,768]{1,0:T(8,128)(2,1)}, bf16[528,768]{1,0:T(8,128)(2,1)S(1)}, u32[]{:S(2)}, u32[]{:S(2)}) collective-permute-start(bf16[528,768]{1,0:T(8,128)(2,1)} %shard_map.46.refs_0_), channel_id=1, source_target_pairs={{0,2},{1,3},{2,0},{3,1},{4,6},{5,7},{6,4},{7,5},{8,10},{9,11},{10,... | collective-permute-start | bytes 2433032 | tf_op jit(solution)/shard_map/ppermute | solution.py:185
  57.8 35.5 %collective-permute-start.1 = (bf16[528,768]{1,0:T(8,128)(2,1)}, bf16[528,768]{1,0:T(8,128)(2,1)S(1)}, u32[]{:S(2)}, u32[]{:S(2)}) collective-permute-start(bf16[528,768]{1,0:T(8,128)(2,1)} %shard_map.46.refs_0_), channel_id=1, source_target_pairs={{0,3},{1,0},{2,1},{3,2},{4,7},{5,4},{6,5},{7,6},{8,11},{9,8},{10,9... | collective-permute-start | bytes 2433032 | tf_op jit(solution)/shard_map/ppermute | solution.py:185
  60.6 42.4 %collective-permute-start = (bf16[528,768]{1,0:T(8,128)(2,1)}, bf16[528,768]{1,0:T(8,128)(2,1)S(1)}, u32[]{:S(2)}, u32[]{:S(2)}) collective-permute-start(bf16[528,768]{1,0:T(8,128)(2,1)} %shard_map.46.refs_0_), channel_id=1, source_target_pairs={{0,1},{1,2},{2,3},{3,0},{4,5},{5,6},{6,7},{7,4},{8,9},{9,10},{10,1... | collective-permute-start | bytes 2433032 | tf_op jit(solution)/shard_map/ppermute | solution.py:185
  63.2 33.5 %collective-permute-start.5 = (bf16[24,2,32,128]{3,2,1,0:T(8,128)(2,1)S(1)}, bf16[24,2,32,128]{3,2,1,0:T(8,128)(2,1)S(1)}, u32[]{:S(2)}, u32[]{:S(2)}) collective-permute-start(bf16[24,2,32,128]{3,2,1,0:T(8,128)(2,1)S(1)} %all-to-all-done.refs_4_), channel_id=1, source_target_pairs={{0,16},{4,132},{8,56},{12,140},{16,32},{20,148},{24,8},{28,156},{3... | collective-permute-start | bytes 1179656 | tf_op jit(solution)/shard_map/ppermute | solution.py:187
  67.2 31.4 %collective-permute-start.4 = (bf16[24,2,32,128]{3,2,1,0:T(8,128)(2,1)S(1)}, bf16[24,2,32,128]{3,2,1,0:T(8,128)(2,1)S(1)}, u32[]{:S(2)}, u32[]{:S(2)}) collective-permute-start(bf16[24,2,32,128]{3,2,1,0:T(8,128)(2,1)S(1)} %all-to-all-done.refs_4_), channel_id=1, source_target_pairs={{0,56},{4,708},{8,0},{12,716},{16,8},{20,724},{24,16},{28,732},{32... | collective-permute-start | bytes 1179656 | tf_op jit(solution)/shard_map/ppermute | solution.py:187
  74.2 26.8 %collective-permute-start.3 = (bf16[24,2,32,128]{3,2,1,0:T(8,128)(2,1)S(1)}, bf16[24,2,32,128]{3,2,1,0:T(8,128)(2,1)S(1)}, u32[]{:S(2)}, u32[]{:S(2)}) collective-permute-start(bf16[24,2,32,128]{3,2,1,0:T(8,128)(2,1)S(1)} %all-to-all-done.refs_4_), channel_id=1, source_target_pairs={{0,8},{4,68},{8,16},{12,76},{16,24},{20,84},{24,32},{28,92},{32,40... | collective-permute-start | bytes 1179656 | tf_op jit(solution)/shard_map/ppermute | solution.py:187
  93.3 9.8 %collective-permute-start.6 = (bf16[24,2,32,128]{3,2,1,0:T(8,128)(2,1)S(1)}, bf16[24,2,32,128]{3,2,1,0:T(8,128)(2,1)S(1)}, u32[]{:S(2)}, u32[]{:S(2)}) collective-permute-start(bf16[24,2,32,128]{3,2,1,0:T(8,128)(2,1)S(1)} %all-to-all-done.refs_4_), channel_id=1, source_target_pairs={{0,4},{4,0},{8,12},{12,8},{16,20},{20,16},{24,28},{28,24},{32,36},... | collective-permute-start | bytes 1179656 | tf_op jit(solution)/shard_map/ppermute | solution.py:188
  96.7 6.4 %collective-permute-start.9 = (bf16[24,2,32,128]{3,2,1,0:T(8,128)(2,1)S(1)}, bf16[24,2,32,128]{3,2,1,0:T(8,128)(2,1)S(1)}, u32[]{:S(2)}, u32[]{:S(2)}) collective-permute-start(bf16[24,2,32,128]{3,2,1,0:T(8,128)(2,1)S(1)} %collective-permute-done.5.refs_7_), channel_id=1, source_target_pairs={{0,4},{4,0},{8,12},{12,8},{16,20},{20,16},{24,28},{28,24},{32,36},... | collective-permute-start | bytes 1179656 | tf_op jit(solution)/shard_map/ppermute | solution.py:188
  98.6 4.5 %collective-permute-start.8 = (bf16[24,2,32,128]{3,2,1,0:T(8,128)(2,1)S(1)}, bf16[24,2,32,128]{3,2,1,0:T(8,128)(2,1)S(1)}, u32[]{:S(2)}, u32[]{:S(2)}) collective-permute-start(bf16[24,2,32,128]{3,2,1,0:T(8,128)(2,1)S(1)} %collective-permute-done.4.refs_6_), channel_id=1, source_target_pairs={{0,4},{4,0},{8,12},{12,8},{16,20},{20,16},{24,28},{28,24},{32,36},... | collective-permute-start | bytes 1179656 | tf_op jit(solution)/shard_map/ppermute | solution.py:188
  101.0 3.6 %collective-permute-start.7 = (bf16[24,2,32,128]{3,2,1,0:T(8,128)(2,1)S(1)}, bf16[24,2,32,128]{3,2,1,0:T(8,128)(2,1)S(1)}, u32[]{:S(2)}, u32[]{:S(2)}) collective-permute-start(bf16[24,2,32,128]{3,2,1,0:T(8,128)(2,1)S(1)} %collective-permute-done.3.refs_5_), channel_id=1, source_target_pairs={{0,4},{4,0},{8,12},{12,8},{16,20},{20,16},{24,28},{28,24},{32,36},... | collective-permute-start | bytes 1179656 | tf_op jit(solution)/shard_map/ppermute | solution.py:188
  104.6 1.1 copy-start

commit v4 on v3

v4 whole, which is shorter than its diff:
```python
import jax
import jax.numpy as jnp
from jax import lax
from jax.experimental import pallas as pl
from jax.experimental.pallas import tpu as pltpu
from jax.sharding import PartitionSpec as P

TILE = 128
NZ, NY, NC, NX = 12, 8, 2, 4
DEPTH = 32
SLOTS = 6
TAIL = 16


def row_of(z, y, core):
    return (z % NZ) * NY * NC + (y % NY) * NC + core


def spread(piece, axis, size, groups):
    copies = jnp.broadcast_to(piece[None], (size,) + piece.shape)
    return lax.all_to_all(copies, axis, 0, 0, tiled=True, axis_index_groups=groups)


def step_of(position, shift):
    if shift == 2:
        return 2 if position % 2 == 0 else -2
    return shift


def shift_moves(shift):
    moves = []
    for z in range(NZ):
        for y in range(NY):
            moves.append((row_of(z, y, 0), row_of(z, y + step_of(y, shift), 0)))
            moves.append((row_of(z, y, 1), row_of(z + step_of(z, shift), y, 1)))
    return moves


SHIFTS = (0, 1, -1, 2)
MIXED_GROUPS = [
    [row_of(z, b + 4 * h, 0) for z in range(NZ) for h in range(2)] for b in range(4)
] + [[row_of(j + 4 * i, y, 1) for i in range(3) for y in range(NY)] for j in range(4)]
GROUP = 24
PLANE_GROUPS = [[row_of(z, j // 2, j % 2) for j in range(NY * NC)] for z in range(NZ)]
Z_GROUPS = [[row_of(z, j // 2, j % 2) for z in range(NZ)] for j in range(NY * NC)]
SWAP = [(r, r ^ 1) for r in range(NZ * NY * NC)]


def pack_kernel(fill_ref, slab_ref, out_ref):
    sections, rows = slab_ref.shape[0], slab_ref.shape[1] // TILE
    cols = slab_ref.shape[2] // TILE
    lane = lax.broadcasted_iota(jnp.int32, (TAIL, TILE), 1)
    words = jnp.zeros((TAIL, TILE), jnp.float32)
    for group in range(sections * rows):
        s, r = group // rows, group % rows
        count = jnp.int32(0)
        for k in range(cols):
            count += fill_ref[s, r, k]
        seen = jnp.int32(0)
        for k in range(cols):
            filled = fill_ref[s, r, k]
            slot = jnp.where(filled == 1, seen, count + k - seen)
            seen += filled

            @pl.when(slot < SLOTS)
            def _(group=group, s=s, r=r, k=k, slot=slot):
                column = pl.multiple_of(slot * TILE, TILE)
                out_ref[pl.ds(group * TILE, TILE), pl.ds(column, TILE)] = slab_ref[
                    s, r * TILE : (r + 1) * TILE, k * TILE : (k + 1) * TILE
                ]

            place = jnp.where(slot < SLOTS, group * (SLOTS + 1) + slot, -1)
            words = jnp.where(lane == place, jnp.float32(k), words)
        words = jnp.where(lane == group * (SLOTS + 1) + SLOTS, count.astype(jnp.float32), words)
    tail = slice(sections * rows * TILE, sections * rows * TILE + TAIL)
    out_ref[tail, :] = jnp.zeros((TAIL, SLOTS * TILE), jnp.bfloat16)
    out_ref[tail, :TILE] = words.astype(jnp.bfloat16)


def pack(slab, slab_fill):
    sections, rows, cols = slab.shape
    height = sections * rows + TAIL
    vmem = pl.BlockSpec(memory_space=pltpu.VMEM)
    return pl.pallas_call(
        pack_kernel,
        out_shape=jax.ShapeDtypeStruct((height, SLOTS * TILE), jnp.bfloat16),
        in_specs=[pl.BlockSpec(memory_space=pltpu.SMEM), vmem],
        out_specs=vmem,
        compiler_params=pltpu.CompilerParams(vmem_limit_bytes=16 * 2**20),
        cost_estimate=pl.CostEstimate(flops=0, bytes_accessed=2 * 2**20, transcendentals=0),
    )(slab_fill, slab)


def product_kernel(place_ref, words_ref, keep_ref, *refs):
    lefts_ref, pieces = refs[0], refs[1:9]
    out_ref, sums_ref, right_ref, near_ref, left_ref, left_sem = refs[9:]
    fetch = pltpu.make_async_copy(lefts_ref, left_ref, left_sem)
    fetch.start()
    sections = right_ref.shape[0]
    row = place_ref[0]
    z, y, core = row // (NY * NC), (row // NC) % NY, row % NC
    for index, piece in enumerate(pieces):
        step = index % 4
        if step == 3:
            y_from = jnp.where(y % 2 == 0, y - 2, y + 2)
            z_from = jnp.where(z % 2 == 0, z - 2, z + 2)
        else:
            y_from, z_from = y - SHIFTS[step], z - SHIFTS[step]
        along_y = (core == 0) == (index < 4)
        first = jnp.where(along_y, (y_from + NY) % 4 * 64, (z_from + NZ) % 4 * 512 + DEPTH)
        for slot in range(GROUP):
            offset = jnp.where(
                along_y, slot // 2 * 512 + slot % 2 * 256, slot // 8 * 2048 + slot % 8 * 64
            )
            at = pl.multiple_of(first + offset, DEPTH)
            for s in range(sections):
                right_ref[s, pl.ds(at, DEPTH)] = piece[slot, s]

    fetch.wait()
    row_blocks = out_ref.shape[0] // TILE
    per_source = sections * row_blocks * (SLOTS + 1)
    colsum = jnp.zeros((8, TILE), jnp.float32)
    for r in range(row_blocks):
        total = jnp.zeros((TILE, TILE), jnp.float32)
        for source in range(NX):
            for s in range(sections):
                group = s * row_blocks + r
                base = source * per_source + group * (SLOTS + 1)
                count = words_ref[base + SLOTS]
                for slot in range(SLOTS):
                    tile = source * 12 + words_ref[base + slot]
                    rows = pl.ds(pl.multiple_of(tile * TILE, TILE), TILE)
                    keep = (slot < count).astype(jnp.float32).astype(jnp.bfloat16)
                    near_ref[slot * TILE : (slot + 1) * TILE] = right_ref[s, rows] * keep
                left = left_ref[source, group * TILE : (group + 1) * TILE, :]
                total += jnp.dot(left, near_ref[...], preferred_element_type=jnp.float32)
        squares = total * total * keep_ref[r].astype(jnp.float32)
        out_ref[r * TILE : (r + 1) * TILE] = squares
        colsum += jnp.sum(squares.reshape(TILE // 8, 8, TILE), axis=0)
    sums_ref[...] = jnp.broadcast_to(colsum[None], sums_ref.shape)


def multiply(place, words, keep, lefts, pieces, sections, rows):
    smem = pl.BlockSpec(memory_space=pltpu.SMEM)
    vmem = pl.BlockSpec(memory_space=pltpu.VMEM)
    depth = NZ * NY * NC * DEPTH
    return pl.pallas_call(
        product_kernel,
        out_shape=(
            jax.ShapeDtypeStruct((rows, TILE), jnp.float32),
            jax.ShapeDtypeStruct((NY * NC, 8, TILE), jnp.float32),
        ),
        in_specs=[smem, smem, smem] + [pl.BlockSpec(memory_space=pl.ANY)] + [vmem] * 8,
        out_specs=(vmem, vmem),
        scratch_shapes=[
            pltpu.VMEM((sections, depth, TILE), jnp.bfloat16),
            pltpu.VMEM((SLOTS * TILE, TILE), jnp.bfloat16),
            pltpu.VMEM(lefts.shape, jnp.bfloat16),
            pltpu.SemaphoreType.DMA,
        ],
        compiler_params=pltpu.CompilerParams(vmem_limit_bytes=32 * 2**20),
        cost_estimate=pl.CostEstimate(
            flops=sections * rows * depth * TILE, bytes_accessed=7 * 2**20, transcendentals=0
        ),
    )(place, words, keep, lefts, *pieces)


def shards(slab, slab_fill, panel, out_fill):
    sections, row_count, local_cols = slab.shape
    place = lax.axis_index("row").astype(jnp.int32).reshape(1)
    held = spread(panel, "row", GROUP, MIXED_GROUPS)
    lefts = lax.all_gather(pack(slab, slab_fill), "col", axis=0)
    mine = [held] + [lax.ppermute(held, "row", shift_moves(s)) for s in SHIFTS[1:]]
    theirs = [lax.ppermute(piece, "row", SWAP) for piece in mine]
    tail = sections * row_count
    count = sections * row_count // TILE * (SLOTS + 1)
    words = lefts[:, tail, :count].reshape(-1).astype(jnp.int32)
    squares, sums = multiply(
        place, words, out_fill.reshape(-1), lefts, mine + theirs, sections, row_count
    )
    sums = lax.all_to_all(sums, "row", 0, 0, tiled=True, axis_index_groups=PLANE_GROUPS)
    sums = jnp.sum(sums, axis=0)
    sums = jnp.sum(spread(sums, "row", NZ, Z_GROUPS), axis=(0, 1))
    factor_col = jnp.float32(row_count * NZ * NY * NC) / sums
    return squares * factor_col


def solution(mesh):
    placed = (P(None, "row", "col"), P(None, "row", "col"), P(None, "row", "col"), P("row", "col"))
    return jax.shard_map(
        shards, mesh=mesh, in_specs=placed, out_specs=P("row", "col"), check_vma=False
    )
```

time: 142 us -> 117 us (0.82)
  blocking collectives: 32.7 us -> 59 us
  Pallas kernels: 28.8 us -> 4.7 us
  starting transfers between devices: 51.7 us -> 32.4 us
  waiting for transfers between devices: 19 us -> 0.53 us
  between operations: 0.21 us -> 13.5 us
  other arithmetic: 3.48 us -> 1.45 us
    all_to_all x1 -> x2, blocking collectives: 18.2 us -> 46.3 us  [spread(): lax.all_to_all(copies, axis, 0, 0, tiled=True, axis_index_groups=groups)]
    pallas_call x1, Pallas kernels: 26.6 us -> 2.04 us  [pack(): pl.pallas_call(pack_kernel, out_shape=jax.ShapeDtypeStruct((height, SLOTS...]
    all_to_all x1 -> x0, starting transfers between devices: 20.1 us -> none  [spread(): lax.all_to_all(copies, axis, 0, 0, tiled=True, axis_index_groups=groups)]
    ppermute x3 -> x0, waiting for transfers between devices: 17.4 us -> none  [shards(): lax.ppermute(packed, 'col', [(x, (x + s) % NX) for x in range(NX)])]
    ppermute x3 -> x0, starting transfers between devices: 9.93 us -> none  [shards(): lax.ppermute(packed, 'col', [(x, (x + s) % NX) for x in range(NX)])]
    ppermute x4, starting transfers between devices: 9.59 us -> 16 us  [shards(): theirs = [lax.ppermute(piece, 'row', SWAP) for piece in mine]]
    ppermute x3, starting transfers between devices: 12 us -> 16.4 us  [shards(): lax.ppermute(held, 'row', shift_moves(s))]
    unnamed x4 -> x8, local copies, waits for them, and re-layouts: 1.15 us -> 4.01 us
  transfers between devices with their start and end apart: 11 -> 8, of which waited for: 3 -> 1; matrix products, arithmetic and copies ran while one was open for 4% -> 1% of each run, Pallas kernels for 19% -> 0%
where the time goes in v4:
time: 117 us
  blocking collectives  59 us (50%)
  starting transfers between devices  32.4 us (28%)
  between operations  13.5 us (12%)
  local copies, waits for them, and re-layouts  4.9 us (4%)
  Pallas kernels  4.7 us (4%)
  other arithmetic  1.45 us (1%)
    all_to_all x2, blocking collectives, spread(): lax.all_to_all(copies, axis, 0, 0, tiled=True, axis_index_groups=groups)  46.3 us
    ppermute x3, starting transfers between devices, shards(): lax.ppermute(held, 'row', shift_moves(s))  16.4 us
    ppermute x4, starting transfers between devices, shards(): theirs = [lax.ppermute(piece, 'row', SWAP) for piece in mine]  16 us
    all_to_all x1, blocking collectives, shards(): lax.all_to_all(sums, 'row', 0, 0, tiled=True, axis_index_groups=PLANE_GRO...  12.7 us
    unnamed x8, local copies, waits for them, and re-layouts  4.01 us
    pallas_call x1, Pallas kernels, multiply(): pl.pallas_call(product_kernel, out_shape=(jax.ShapeDtypeStruct((rows, TIL...  2.65 us
  transfers between devices with their start and end apart: 8, of which 1 were waited for; matrix products, arithmetic and copies ran while one was open for 1% of the time, Pallas kernels for 0%

profile of v4, /device:TPU:1, one launch (start us, length us, event | category | flops | bytes accessed | tf_op | source)
XLA Modules:
  0.0 116.5 jit_solution(9108627430673257645)
XLA Ops:
  6.5 0.0 all-gather.3.cloned.1.call-start
  6.5 0.0 copy-start.1
  6.5 1.4 %copy-done.1 = bf16[2,256,1536]{2,1,0:T(8,128)(2,1)S(1)} copy-done((bf16[2,256,1536]{2,1,0:T(8,128)(2,1)S(1)}, bf16[2,256,1536]{2,1,0:T(8,128)(2,1)}, u32[]{:S(2)}) %copy-start.1) | copy-done | bytes 1572888
  7.9 0.0 copy-start.2
  7.9 0.7 copy-done.2
  8.6 0.0 copy-start.3
  8.6 2.0 %shard_map.46 = bf16[528,768]{1,0:T(8,128)(2,1)} custom-call(s32[2,2,12]{2,1,0:T(2,128)S(1)} %copy-done.2, bf16[2,256,1536]{2,1,0:T(8,128)(2,1)S(1)} %copy-done.1), custom_call_target="tpu_custom_call" | custom-call | bytes 2097152 | tf_op jit(solution)/shard_map/pallas_call | solution.py:84
  10.7 0.0 all-gather.3.cloned.1.call-update
  10.7 0.8 broadcast_in_dim.4
  11.5 32.6 %all_to_all.15.refs_1_ = bf16[24,2,32,128]{3,2,1,0:T(8,128)(2,1)S(1)} all-to-all(bf16[24,2,32,128]{3,2,1,0:T(8,128)(2,1)S(1)} %broadcast_in_dim.4), channel_id=1, replica_groups={{0,32,64,96,128,160,192,224,256,288,320,352,384,416,448,480,512,544,576..., dimensions={0} | all-to-all | bytes 786432 | tf_op jit(solution)/shard_map/all_to_all | solution.py:21
  44.1 7.2 %collective-permute-start = (bf16[24,2,32,128]{3,2,1,0:T(8,128)(2,1)S(1)}, bf16[24,2,32,128]{3,2,1,0:T(8,128)(2,1)S(1)}, u32[]{:S(2)}, u32[]{:S(2)}) collective-permute-start(bf16[24,2,32,128]{3,2,1,0:T(8,128)(2,1)S(1)} %all_to_all.15.refs_1_), channel_id=1, source_target_pairs={{0,8},{4,68},{8,16},{12,76},{16,24},{20,84},{24,32},{28,92},{32,40... | collective-permute-start | bytes 1179656 | tf_op jit(solution)/shard_map/ppermute | solution.py:173
  51.4 6.7 %collective-permute-start.1 = (bf16[24,2,32,128]{3,2,1,0:T(8,128)(2,1)S(1)}, bf16[24,2,32,128]{3,2,1,0:T(8,128)(2,1)S(1)}, u32[]{:S(2)}, u32[]{:S(2)}) collective-permute-start(bf16[24,2,32,128]{3,2,1,0:T(8,128)(2,1)S(1)} %all_to_all.15.refs_1_), channel_id=1, source_target_pairs={{0,56},{4,708},{8,0},{12,716},{16,8},{20,724},{24,16},{28,732},{32... | collective-permute-start | bytes 1179656 | tf_op jit(solution)/shard_map/ppermute | solution.py:173
  58.1 2.4 %collective-permute-start.2 = (bf16[24,2,32,128]{3,2,1,0:T(8,128)(2,1)S(1)}, bf16[24,2,32,128]{3,2,1,0:T(8,128)(2,1)S(1)}, u32[]{:S(2)}, u32[]{:S(2)}) collective-permute-start(bf16[24,2,32,128]{3,2,1,0:T(8,128)(2,1)S(1)} %all_to_all.15.refs_1_), channel_id=1, source_target_pairs={{0,16},{4,132},{8,56},{12,140},{16,32},{20,148},{24,8},{28,156},{3... | collective-permute-start | bytes 1179656 | tf_op jit(solution)/shard_map/ppermute | solution.py:173
  60.5 6.3 %collective-permute-start.3 = (bf16[24,2,32,128]{3,2,1,0:T(8,128)(2,1)S(1)}, bf16[24,2,32,128]{3,2,1,0:T(8,128)(2,1)S(1)}, u32[]{:S(2)}, u32[]{:S(2)}) collective-permute-start(bf16[24,2,32,128]{3,2,1,0:T(8,128)(2,1)S(1)} %all_to_all.15.refs_1_), channel_id=1, source_target_pairs={{0,4},{4,0},{8,12},{12,8},{16,20},{20,16},{24,28},{28,24},{32,36},... | collective-permute-start | bytes 1179656 | tf_op jit(solution)/shard_map/ppermute | solution.py:174
  66.8 0.0 collective-permute-done.refs_2_
  66.8 1.9 %collective-permute-start.4 = (bf16[24,2,32,128]{3,2,1,0:T(8,128)(2,1)S(1)}, bf16[24,2,32,128]{3,2,1,0:T(8,128)(2,1)S(1)}, u32[]{:S(2)}, u32[]{:S(2)}) collective-permute-start(bf16[24,2,32,128]{3,2,1,0:T(8,128)(2,1)S(1)} %collective-permute-done.refs_2_), channel_id=1, source_target_pairs={{0,4},{4,0},{8,12},{12,8},{16,20},{20,16},{24,28},{28,24},{32,36},... | collective-permute-start | bytes 1179656 | tf_op jit(solution)/shard_map/ppermute | solution.py:174
  68.8 0.0 collective-permute-done.1.refs_3_
  68.8 5.6 %collective-permute-start.5 = (bf16[24,2,32,128]{3,2,1,0:T(8,128)(2,1)S(1)}, bf16[24,2,32,128]{3,2,1,0:T(8,128)(2,1)S(1)}, u32[]{:S(2)}, u32[]{:S(2)}) collective-permute-start(bf16[24,2,32,128]{3,2,1,0:T(8,128)(2,1)S(1)} %collective-permute-done.1.refs_3_), channel_id=1, source_target_pairs={{0,4},{4,0},{8,12},{12,8},{16,20},{20,16},{24,28},{28,24},{32,36},... | collective-permute-start | bytes 1179656 | tf_op jit(solution)/shard_map/ppermute | solution.py:174
  74.4 0.0 collective-permute-done.2.refs_4_
  74.4 2.3 %collective-permute-start.6 = (bf16[24,2,32,128]{3,2,1,0:T(8,128)(2,1)S(1)}, bf16[24,2,32,128]{3,2,1,0:T(8,128)(2,1)S(1)}, u32[]{:S(2)}, u32[]{:S(2)}) collective-permute-start(bf16[24,2,32,128]{3,2,1,0:T(8,128)(2,1)S(1)} %collective-permute-done.2.refs_4_), channel_id=1, source_target_pairs={{0,4},{4,0},{8,12},{12,8},{16,20},{20,16},{24,28},{28,24},{32,36},... | collective-permute-start | bytes 1179656 | tf_op jit(solution)/shard_map/ppermute | solution.py:174
  76.7 0.0 all-gather.3.cloned.1.call-done
  76.7 0.7 fusion
  77.4 0.1 reshape.15.words_ref
  77.5 0.0 collective-permute-done.3.refs_5_
  77.5 0.0 collective-permute-done.4.refs_6_
  77.5 0.0 collective-permute-done.5.refs_7_
  77.5 0.5 collective-permute-done.6.refs_8_
  78.0 0.0 copy-done.3
  78.0 0.0 copy-start
  78.0 1.9 %copy-done = bf16[2112,768]{1,0:T(8,128)(2,1)S(1)} copy-done((bf16[2112,768]{1,0:T(8,128)(2,1)S(1)}, bf16[2112,768]{1,0:T(8,128)(2,1)}, u32[]{:S(2)}) %copy-start) | copy-done | bytes 3244056
  79.9 2.7 %shard_map.47 = (f32[256,128]{1,0:T(8,128)S(1)}, f32[16,8,128]{2,1,0:T(8,128)S(1)}) custom-call(s32[1]{0:T(128)} %bitcast.place_ref, s32[112]{0:T(128)S(1)} %reshape.15.words_ref, s32[2]{0:T(128)S(1)} %bitcast.5, bf16[4,528,768]{2,1,0:T(8,128)(2,1)S(1)} %bitcast.4, bf16[24,2,32,128]{3,2,1,0:T(8,128)(2,1)S(1)} %all_to_all.15.refs_1_, ...), custom_call_target="tpu_custom_call" | custom-call | flops 402653184 | bytes 7340032 | tf_op jit(solution)/shard_map/pallas_call | solution.py:147
  82.6 12.7 %all_to_all.16 = f32[16,8,128]{2,1,0:T(8,128)S(1)} all-to-all(f32[16,8,128]{2,1,0:T(8,128)S(1)} %get-tuple-element.8), channel_id=1, replica_groups={{0,4,8,12,16,20,24,28,32,36,40,44,48,52,56,60},{64,68,72,76,80,84,88,92..., dimensions={0} | all-to-all | bytes 131072 | tf_op jit(solution)/shard_map/all_to_all | solution.py:181
  95.3 13.6 %all_to_all.17 = f32[12,8,128]{2,1,0:T(8,128)S(1)} all-to-all(f32[12,8,128]{2,1,0:T(8,128)S(1)} %broadcast_in_dim.5), channel_id=1, replica_groups={{0,64,128,192,256,320,384,448,512,576,640,704},{4,68,132,196,260,324,38..., dimensions={0} | all-to-all | bytes 98304 | tf_op jit(solution)/shard_map/all_to_all | solution.py:21
  109.0 0.7 broadcast_multiply_fusion
  (4 shorter events, 0.1 us)
Async XLA Ops:
  6.5 70.2 %all-gather.3.cloned.1.call-start = ((), (), s32[]{:S(2)}) async-start(), calls=%async_computation.3 | async-start | bytes 4055040 | tf_op jit(solution)/shard_map/all_gather | solution.py:172
  6.5 1.4 %copy-start.1 = (bf16[2,256,1536]{2,1,0:T(8,128)(2,1)S(1)}, bf16[2,256,1536]{2,1,0:T(8,128)(2,1)}, u32[]{:S(2)}) copy-start(bf16[2,256,1536]{2,1,0:T(8,128)(2,1)} %slab_ref.1) | copy-start | bytes 4718596
  7.9 0.7 copy-start.2
  8.6 69.4 %copy-start.3 = (s32[2,1]{0,1:T(1,128)S(1)}, s32[2,1]{0,1:T(1,128)}, u32[]{:S(2)}) copy-start(s32[2,1]{0,1:T(1,128)} %param.7) | copy-start | bytes 28
  44.1 22.7 %collective-permute-start = (bf16[24,2,32,128]{3,2,1,0:T(8,128)(2,1)S(1)}, bf16[24,2,32,128]{3,2,1,0:T(8,128)(2,1)S(1)}, u32[]{:S(2)}, u32[]{:S(2)}) collective-permute-start(bf16[24,2,32,128]{3,2,1,0:T(8,128)(2,1)S(1)} %all_to_all.15.refs_1_), channel_id=1, source_target_pairs={{0,8},{4,68},{8,16},{12,76},{16,24},{20,84},{24,32},{28,92},{32,40... | collective-permute-start | bytes 1179656 | tf_op jit(solution)/shard_map/ppermute | solution.py:173
  51.4 17.4 %collective-permute-start.1 = (bf16[24,2,32,128]{3,2,1,0:T(8,128)(2,1)S(1)}, bf16[24,2,32,128]{3,2,1,0:T(8,128)(2,1)S(1)}, u32[]{:S(2)}, u32[]{:S(2)}) collective-permute-start(bf16[24,2,32,128]{3,2,1,0:T(8,128)(2,1)S(1)} %all_to_all.15.refs_1_), channel_id=1, source_target_pairs={{0,56},{4,708},{8,0},{12,716},{16,8},{20,724},{24,16},{28,732},{32... | collective-permute-start | bytes 1179656 | tf_op jit(solution)/shard_map/ppermute | solution.py:173
  58.1 16.2 %collective-permute-start.2 = (bf16[24,2,32,128]{3,2,1,0:T(8,128)(2,1)S(1)}, bf16[24,2,32,128]{3,2,1,0:T(8,128)(2,1)S(1)}, u32[]{:S(2)}, u32[]{:S(2)}) collective-permute-start(bf16[24,2,32,128]{3,2,1,0:T(8,128)(2,1)S(1)} %all_to_all.15.refs_1_), channel_id=1, source_target_pairs={{0,16},{4,132},{8,56},{12,140},{16,32},{20,148},{24,8},{28,156},{3... | collective-permute-start | bytes 1179656 | tf_op jit(solution)/shard_map/ppermute | solution.py:173
  60.5 17.0 %collective-permute-start.3 = (bf16[24,2,32,128]{3,2,1,0:T(8,128)(2,1)S(1)}, bf16[24,2,32,128]{3,2,1,0:T(8,128)(2,1)S(1)}, u32[]{:S(2)}, u32[]{:S(2)}) collective-permute-start(bf16[24,2,32,128]{3,2,1,0:T(8,128)(2,1)S(1)} %all_to_all.15.refs_1_), channel_id=1, source_target_pairs={{0,4},{4,0},{8,12},{12,8},{16,20},{20,16},{24,28},{28,24},{32,36},... | collective-permute-start | bytes 1179656 | tf_op jit(solution)/shard_map/ppermute | solution.py:174
  66.8 10.7 %collective-permute-start.4 = (bf16[24,2,32,128]{3,2,1,0:T(8,128)(2,1)S(1)}, bf16[24,2,32,128]{3,2,1,0:T(8,128)(2,1)S(1)}, u32[]{:S(2)}, u32[]{:S(2)}) collective-permute-start(bf16[24,2,32,128]{3,2,1,0:T(8,128)(2,1)S(1)} %collective-permute-done.refs_2_), channel_id=1, source_target_pairs={{0,4},{4,0},{8,12},{12,8},{16,20},{20,16},{24,28},{28,24},{32,36},... | collective-permute-start | bytes 1179656 | tf_op jit(solution)/shard_map/ppermute | solution.py:174
  68.8 8.7 %collective-permute-start.5 = (bf16[24,2,32,128]{3,2,1,0:T(8,128)(2,1)S(1)}, bf16[24,2,32,128]{3,2,1,0:T(8,128)(2,1)S(1)}, u32[]{:S(2)}, u32[]{:S(2)}) collective-permute-start(bf16[24,2,32,128]{3,2,1,0:T(8,128)(2,1)S(1)} %collective-permute-done.1.refs_3_), channel_id=1, source_target_pairs={{0,4},{4,0},{8,12},{12,8},{16,20},{20,16},{24,28},{28,24},{32,36},... | collective-permute-start | bytes 1179656 | tf_op jit(solution)/shard_map/ppermute | solution.py:174
  74.4 3.6 %collective-permute-start.6 = (bf16[24,2,32,128]{3,2,1,0:T(8,128)(2,1)S(1)}, bf16[24,2,32,128]{3,2,1,0:T(8,128)(2,1)S(1)}, u32[]{:S(2)}, u32[]{:S(2)}) collective-permute-start(bf16[24,2,32,128]{3,2,1,0:T(8,128)(2,1)S(1)} %collective-permute-done.2.refs_4_), channel_id=1, source_target_pairs={{0,4},{4,0},{8,12},{12,8},{16,20},{20,16},{24,28},{28,24},{32,36},... | collective-permute-start | bytes 1179656 | tf_op jit(solution)/shard_map/ppermute | solution.py:174
  78.0 1.9 %copy-start = (bf16[2112,768]{1,0:T(8,128)(2,1)S(1)}, bf16[2112,768]{1,0:T(8,128)(2,1)}, u32[]{:S(2)}) copy-start(bf16[2112,768]{1,0:T(8,128)(2,1)} %all-gather.3.cloned.1.call-done) | copy-start | bytes 9732100
Sparse Core Ops, SparseCore 0:
  10.8 55.9 all-gather.2

commit v5 on v4

--- a/solution.py
+++ b/solution.py
@@ -10,6 +10,7 @@
 DEPTH = 32
 SLOTS = 6
 TAIL = 16
+HALF = 2
 
 
 def row_of(z, y, core):
@@ -43,7 +44,9 @@
 GROUP = 24
 PLANE_GROUPS = [[row_of(z, j // 2, j % 2) for j in range(NY * NC)] for z in range(NZ)]
 Z_GROUPS = [[row_of(z, j // 2, j % 2) for z in range(NZ)] for j in range(NY * NC)]
-SWAP = [(r, r ^ 1) for r in range(NZ * NY * NC)]
+UP = [(x, (x + 1) % NX) for x in range(NX)]
+DOWN = [((x + 1) % NX, x) for x in range(NX)]
+CORE_GROUPS = [[r, r + 1] for r in range(0, NZ * NY * NC, NC)]
 
 
 def pack_kernel(fill_ref, slab_ref, out_ref):
@@ -92,47 +95,43 @@
 
 
 def product_kernel(place_ref, words_ref, keep_ref, *refs):
-    lefts_ref, pieces = refs[0], refs[1:9]
-    out_ref, sums_ref, right_ref, near_ref, left_ref, left_sem = refs[9:]
-    fetch = pltpu.make_async_copy(lefts_ref, left_ref, left_sem)
-    fetch.start()
+    lefts, pieces = refs[:NX], refs[NX : NX + 4]
+    out_ref, sums_ref, right_ref, near_ref = refs[NX + 4 :]
     sections = right_ref.shape[0]
-    row = place_ref[0]
-    z, y, core = row // (NY * NC), (row // NC) % NY, row % NC
-    for index, piece in enumerate(pieces):
-        step = index % 4
+    row, col = place_ref[0], place_ref[1]
+    z, y = row // (NY * NC), (row // NC) % NY
+    for step, piece in enumerate(pieces):
         if step == 3:
             y_from = jnp.where(y % 2 == 0, y - 2, y + 2)
             z_from = jnp.where(z % 2 == 0, z - 2, z + 2)
         else:
             y_from, z_from = y - SHIFTS[step], z - SHIFTS[step]
-        along_y = (core == 0) == (index < 4)
-        first = jnp.where(along_y, (y_from + NY) % 4 * 64, (z_from + NZ) % 4 * 512 + DEPTH)
+        first_y, first_z = (y_from + NY) % 4 * 64, (z_from + NZ) % 4 * 512
         for slot in range(GROUP):
-            offset = jnp.where(
-                along_y, slot // 2 * 512 + slot % 2 * 256, slot // 8 * 2048 + slot % 8 * 64
-            )
-            at = pl.multiple_of(first + offset, DEPTH)
-            for s in range(sections):
-                right_ref[s, pl.ds(at, DEPTH)] = piece[slot, s]
+            at_y = first_y + (slot // 2 * 512 + slot % 2 * 256)
+            at_z = first_z + (slot // 8 * 2048 + slot % 8 * 64 + DEPTH)
+            for core, at in enumerate((at_y, at_z)):
+                rows = pl.ds(pl.multiple_of(at, DEPTH), DEPTH)
+                for s in range(sections):
+                    right_ref[s, rows] = piece[core, slot, s]
 
-    fetch.wait()
     row_blocks = out_ref.shape[0] // TILE
     per_source = sections * row_blocks * (SLOTS + 1)
     colsum = jnp.zeros((8, TILE), jnp.float32)
     for r in range(row_blocks):
         total = jnp.zeros((TILE, TILE), jnp.float32)
         for source in range(NX):
+            block_col = (col + (0, NX - 1, 1, 2)[source]) % NX
             for s in range(sections):
                 group = s * row_blocks + r
                 base = source * per_source + group * (SLOTS + 1)
                 count = words_ref[base + SLOTS]
                 for slot in range(SLOTS):
-                    tile = source * 12 + words_ref[base + slot]
+                    tile = block_col * 12 + words_ref[base + slot]
                     rows = pl.ds(pl.multiple_of(tile * TILE, TILE), TILE)
                     keep = (slot < count).astype(jnp.float32).astype(jnp.bfloat16)
                     near_ref[slot * TILE : (slot + 1) * TILE] = right_ref[s, rows] * keep
-                left = left_ref[source, group * TILE : (group + 1) * TILE, :]
+                left = lefts[source][group * TILE : (group + 1) * TILE, :]
                 total += jnp.dot(left, near_ref[...], preferred_element_type=jnp.float32)
         squares = total * total * keep_ref[r].astype(jnp.float32)
         out_ref[r * TILE : (r + 1) * TILE] = squares
@@ -150,33 +149,35 @@
             jax.ShapeDtypeStruct((rows, TILE), jnp.float32),
             jax.ShapeDtypeStruct((NY * NC, 8, TILE), jnp.float32),
         ),
-        in_specs=[smem, smem, smem] + [pl.BlockSpec(memory_space=pl.ANY)] + [vmem] * 8,
+        in_specs=[smem, smem, smem] + [vmem] * (NX + 4),
         out_specs=(vmem, vmem),
         scratch_shapes=[
             pltpu.VMEM((sections, depth, TILE), jnp.bfloat16),
             pltpu.VMEM((SLOTS * TILE, TILE), jnp.bfloat16),
-            pltpu.VMEM(lefts.shape, jnp.bfloat16),
-            pltpu.SemaphoreType.DMA,
         ],
         compiler_params=pltpu.CompilerParams(vmem_limit_bytes=32 * 2**20),
         cost_estimate=pl.CostEstimate(
             flops=sections * rows * depth * TILE, bytes_accessed=7 * 2**20, transcendentals=0
         ),
-    )(place, words, keep, lefts, *pieces)
+    )(place, words, keep, *lefts, *pieces)
 
 
 def shards(slab, slab_fill, panel, out_fill):
     sections, row_count, local_cols = slab.shape
-    place = lax.axis_index("row").astype(jnp.int32).reshape(1)
+    place = jnp.stack([lax.axis_index("row"), lax.axis_index("col")]).astype(jnp.int32)
     held = spread(panel, "row", GROUP, MIXED_GROUPS)
-    lefts = lax.all_gather(pack(slab, slab_fill), "col", axis=0)
+    packed = pack(slab, slab_fill)
+    lefts = [packed] + [
+        lax.ppermute(packed, "col", [(x, (x + step) % NX) for x in range(NX)])
+        for step in (1, NX - 1, 2)
+    ]
     mine = [held] + [lax.ppermute(held, "row", shift_moves(s)) for s in SHIFTS[1:]]
-    theirs = [lax.ppermute(piece, "row", SWAP) for piece in mine]
+    pieces = [lax.all_gather(piece, "row", axis_index_groups=CORE_GROUPS) for piece in mine]
     tail = sections * row_count
     count = sections * row_count // TILE * (SLOTS + 1)
-    words = lefts[:, tail, :count].reshape(-1).astype(jnp.int32)
+    words = jnp.concatenate([left[tail, :count] for left in lefts]).astype(jnp.int32)
     squares, sums = multiply(
-        place, words, out_fill.reshape(-1), lefts, mine + theirs, sections, row_count
+        place, words, out_fill.reshape(-1), lefts, pieces, sections, row_count
     )
     sums = lax.all_to_all(sums, "row", 0, 0, tiled=True, axis_index_groups=PLANE_GROUPS)
     sums = jnp.sum(sums, axis=0)

time: 117 us -> 107 us (0.915)
  blocking collectives: 59 us -> 39.4 us
  waiting for transfers between devices: 0.53 us -> 14.6 us
  between operations: 13.5 us -> 0.12 us
  starting transfers between devices: 32.4 us -> 45.3 us
  local copies, waits for them, and re-layouts: 4.9 us -> 2.95 us
  Pallas kernels: 4.7 us -> 3.26 us
    all_to_all x2 -> x1, blocking collectives: 46.3 us -> 15 us  [spread(): lax.all_to_all(copies, axis, 0, 0, tiled=True, axis_index_groups=groups)]
    all_to_all x0 -> x1, starting transfers between devices: none -> 19.2 us  [spread(): lax.all_to_all(copies, axis, 0, 0, tiled=True, axis_index_groups=groups)]
    ppermute x4 -> x3, waiting for transfers between devices: 0.48 us -> 13.7 us  [shards(): lax.ppermute(packed, 'col', [(x, (x + step) % NX) for x in range(NX)])]
    all_gather x0 -> x4, blocking collectives: none -> 9.78 us  [shards(): lax.all_gather(piece, 'row', axis_index_groups=CORE_GROUPS)]
    ppermute x4 -> x3, starting transfers between devices: 16 us -> 10.8 us  [shards(): lax.ppermute(packed, 'col', [(x, (x + step) % NX) for x in range(NX)])]
    unnamed x8, local copies, waits for them, and re-layouts: 4.01 us -> 2.1 us
    all_to_all x1, blocking collectives: 12.7 us -> 14.6 us  [shards(): lax.all_to_all(sums, 'row', 0, 0, tiled=True, axis_index_groups=PLANE_GRO...]
  transfers between devices with their start and end apart: 8 -> 7, of which waited for: 1 -> 2; matrix products, arithmetic and copies ran while one was open for 1% -> 1% of each run, Pallas kernels for 0% -> 0%
where the time goes in v5:
time: 107 us
  starting transfers between devices  45.3 us (42%)
  blocking collectives  39.4 us (37%)
  waiting for transfers between devices  14.6 us (14%)
  Pallas kernels  3.26 us (3%)
  local copies, waits for them, and re-layouts  2.95 us (3%)
    all_to_all x1, starting transfers between devices, spread(): lax.all_to_all(copies, axis, 0, 0, tiled=True, axis_index_groups=groups)  19.2 us
    ppermute x3, starting transfers between devices, shards(): lax.ppermute(held, 'row', shift_moves(s))  15.3 us
    all_to_all x1, blocking collectives, spread(): lax.all_to_all(copies, axis, 0, 0, tiled=True, axis_index_groups=groups)  15 us
    all_to_all x1, blocking collectives, shards(): lax.all_to_all(sums, 'row', 0, 0, tiled=True, axis_index_groups=PLANE_GRO...  14.6 us
    ppermute x3, waiting for transfers between devices, shards(): lax.ppermute(packed, 'col', [(x, (x + step) % NX) for x in range(NX)])  13.7 us
    ppermute x3, starting transfers between devices, shards(): lax.ppermute(packed, 'col', [(x, (x + step) % NX) for x in range(NX)])  10.8 us
    all_gather x4, blocking collectives, shards(): lax.all_gather(piece, 'row', axis_index_groups=CORE_GROUPS)  9.78 us
  transfers between devices with their start and end apart: 7, of which 2 were waited for; matrix products, arithmetic and copies ran while one was open for 1% of the time, Pallas kernels for 0%

profile of v5, /device:TPU:1, one launch (start us, length us, event | category | flops | bytes accessed | tf_op | source)
XLA Modules:
  0.0 106.5 jit_solution(16474240433334275668)
XLA Ops:
  0.0 0.0 copy-start
  0.0 1.4 %copy-done = bf16[2,256,1536]{2,1,0:T(8,128)(2,1)S(1)} copy-done((bf16[2,256,1536]{2,1,0:T(8,128)(2,1)S(1)}, bf16[2,256,1536]{2,1,0:T(8,128)(2,1)}, u32[]{:S(2)}) %copy-start) | copy-done | bytes 1572888
  1.4 0.0 copy-start.1
  1.4 0.7 copy-done.1
  2.1 0.0 copy-start.3
  2.1 1.1 %shard_map.46.refs_0_ = bf16[528,768]{1,0:T(8,128)(2,1)S(1)} custom-call(s32[2,2,12]{2,1,0:T(2,128)S(1)} %copy-done.1, bf16[2,256,1536]{2,1,0:T(8,128)(2,1)S(1)} %copy-done), custom_call_target="tpu_custom_call" | custom-call | bytes 2097152 | tf_op jit(solution)/shard_map/pallas_call | solution.py:87
  3.2 5.5 %collective-permute-start.2 = (bf16[528,768]{1,0:T(8,128)(2,1)S(1)}, bf16[528,768]{1,0:T(8,128)(2,1)S(1)}, u32[]{:S(2)}, u32[]{:S(2)}) collective-permute-start(bf16[528,768]{1,0:T(8,128)(2,1)S(1)} %shard_map.46.refs_0_), channel_id=1, source_target_pairs={{0,2},{1,3},{2,0},{3,1},{4,6},{5,7},{6,4},{7,5},{8,10},{9,11},{10,... | collective-permute-start | bytes 2433032 | tf_op jit(solution)/shard_map/ppermute | solution.py:171
  8.7 0.0 copy-done.3
  8.7 0.8 broadcast_in_dim.4
  9.6 19.2 %all-to-all-start = ((bf16[24,2,32,128]{3,2,1,0:T(8,128)(2,1)}), bf16[24,2,32,128]{3,2,1,0:T(8,128)(2,1)}, u32[]{:S(2)}, u32[]{:S(2)}) async-start(bf16[24,2,32,128]{3,2,1,0:T(8,128)(2,1)} %broadcast_in_dim.4), calls=%async_computation | async-start | bytes 786432 | tf_op jit(solution)/shard_map/all_to_all | solution.py:22
  28.8 2.8 %collective-permute-start.1 = (bf16[528,768]{1,0:T(8,128)(2,1)S(1)}, bf16[528,768]{1,0:T(8,128)(2,1)S(1)}, u32[]{:S(2)}, u32[]{:S(2)}) collective-permute-start(bf16[528,768]{1,0:T(8,128)(2,1)S(1)} %shard_map.46.refs_0_), channel_id=1, source_target_pairs={{0,3},{1,0},{2,1},{3,2},{4,7},{5,4},{6,5},{7,6},{8,11},{9,8},{10,9... | collective-permute-start | bytes 2433032 | tf_op jit(solution)/shard_map/ppermute | solution.py:171
  31.6 2.5 %collective-permute-start = (bf16[528,768]{1,0:T(8,128)(2,1)S(1)}, bf16[528,768]{1,0:T(8,128)(2,1)S(1)}, u32[]{:S(2)}, u32[]{:S(2)}) collective-permute-start(bf16[528,768]{1,0:T(8,128)(2,1)S(1)} %shard_map.46.refs_0_), channel_id=1, source_target_pairs={{0,1},{1,2},{2,3},{3,0},{4,5},{5,6},{6,7},{7,4},{8,9},{9,10},{10,1... | collective-permute-start | bytes 2433032 | tf_op jit(solution)/shard_map/ppermute | solution.py:171
  34.1 0.1 pad_add_fusion.place_ref
  34.2 0.0 collective-permute-done.2.refs_3_
  34.2 13.7 %collective-permute-done.1.refs_2_ = bf16[528,768]{1,0:T(8,128)(2,1)S(1)} collective-permute-done((bf16[528,768]{1,0:T(8,128)(2,1)S(1)}, bf16[528,768]{1,0:T(8,128)(2,1)S(1)}, u32[]{:S(2)}, u32[]{:S(2)}) %collective-permute-start.1) | collective-permute-done | bytes 811040 | tf_op jit(solution)/shard_map/ppermute | solution.py:171
  48.0 0.0 all-to-all-done
  48.0 3.7 %collective-permute-start.5 = (bf16[24,2,32,128]{3,2,1,0:T(8,128)(2,1)}, bf16[24,2,32,128]{3,2,1,0:T(8,128)(2,1)S(1)}, u32[]{:S(2)}, u32[]{:S(2)}) collective-permute-start(bf16[24,2,32,128]{3,2,1,0:T(8,128)(2,1)} %all-to-all-done), channel_id=1, source_target_pairs={{0,16},{4,132},{8,56},{12,140},{16,32},{20,148},{24,8},{28,156},{3... | collective-permute-start | bytes 1179656 | tf_op jit(solution)/shard_map/ppermute | solution.py:174
  51.7 0.0 collective-permute-done.refs_1_
  51.7 0.1 maximum_convert_fusion.words_ref
  51.8 9.4 %collective-permute-start.4 = (bf16[24,2,32,128]{3,2,1,0:T(8,128)(2,1)}, bf16[24,2,32,128]{3,2,1,0:T(8,128)(2,1)S(1)}, u32[]{:S(2)}, u32[]{:S(2)}) collective-permute-start(bf16[24,2,32,128]{3,2,1,0:T(8,128)(2,1)} %all-to-all-done), channel_id=1, source_target_pairs={{0,56},{4,708},{8,0},{12,716},{16,8},{20,724},{24,16},{28,732},{32... | collective-permute-start | bytes 1179656 | tf_op jit(solution)/shard_map/ppermute | solution.py:174
  61.2 2.1 %collective-permute-start.3 = (bf16[24,2,32,128]{3,2,1,0:T(8,128)(2,1)}, bf16[24,2,32,128]{3,2,1,0:T(8,128)(2,1)S(1)}, u32[]{:S(2)}, u32[]{:S(2)}) collective-permute-start(bf16[24,2,32,128]{3,2,1,0:T(8,128)(2,1)} %all-to-all-done), channel_id=1, source_target_pairs={{0,8},{4,68},{8,16},{12,76},{16,24},{20,84},{24,32},{28,92},{32,40... | collective-permute-start | bytes 1179656 | tf_op jit(solution)/shard_map/ppermute | solution.py:174
  63.4 2.6 %all-gather = bf16[48,2,32,128]{3,2,1,0:T(8,128)(2,1)S(1)} all-gather(bf16[24,2,32,128]{3,2,1,0:T(8,128)(2,1)} %all-to-all-done), channel_id=2, replica_groups={{0,4},{8,12},{16,20},{24,28},{32,36},{40,44},{48,52},{56,60},{64,68},{7..., dimensions={0}, use_global_device_ids=true | all-gather | bytes 1179648 | tf_op jit(solution)/shard_map/all_gather | solution.py:175
  66.0 0.0 copy-start.2
  66.0 0.0 collective-permute-done.5
  66.0 2.5 %all-gather.3 = bf16[48,2,32,128]{3,2,1,0:T(8,128)(2,1)S(1)} all-gather(bf16[24,2,32,128]{3,2,1,0:T(8,128)(2,1)S(1)} %collective-permute-done.5), channel_id=5, replica_groups={{0,4},{8,12},{16,20},{24,28},{32,36},{40,44},{48,52},{56,60},{64,68},{7..., dimensions={0}, use_global_device_ids=true | all-gather | bytes 1179648 | tf_op jit(solution)/shard_map/all_gather | solution.py:175
  68.5 0.9 collective-permute-done.4
  69.3 2.4 %all-gather.2 = bf16[48,2,32,128]{3,2,1,0:T(8,128)(2,1)S(1)} all-gather(bf16[24,2,32,128]{3,2,1,0:T(8,128)(2,1)S(1)} %collective-permute-done.4), channel_id=4, replica_groups={{0,4},{8,12},{16,20},{24,28},{32,36},{40,44},{48,52},{56,60},{64,68},{7..., dimensions={0}, use_global_device_ids=true | all-gather | bytes 1179648 | tf_op jit(solution)/shard_map/all_gather | solution.py:175
  71.7 0.0 collective-permute-done.3
  71.7 2.4 %all-gather.1 = bf16[48,2,32,128]{3,2,1,0:T(8,128)(2,1)S(1)} all-gather(bf16[24,2,32,128]{3,2,1,0:T(8,128)(2,1)S(1)} %collective-permute-done.3), channel_id=3, replica_groups={{0,4},{8,12},{16,20},{24,28},{32,36},{40,44},{48,52},{56,60},{64,68},{7..., dimensions={0}, use_global_device_ids=true | all-gather | bytes 1179648 | tf_op jit(solution)/shard_map/all_gather | solution.py:175
  74.1 0.0 copy-done.2
  74.1 2.1 %shard_map.47 = (f32[256,128]{1,0:T(8,128)S(1)}, f32[16,8,128]{2,1,0:T(8,128)S(1)}) custom-call(s32[2]{0:T(128)S(1)} %pad_add_fusion.place_ref, s32[112]{0:T(128)S(1)} %maximum_convert_fusion.words_ref, s32[2]{0:T(128)S(1)} %bitcast.19, bf16[528,768]{1,0:T(8,128)(2,1)S(1)} %shard_map.46.refs_0_, bf16[528,768]{1,0:T(8,128)(2,1)S(1)} %collective-permute-done.refs_1_, ...), custom_call_target="tpu_custom_call" | custom-call | flops 402653184 | bytes 7340032 | tf_op jit(solution)/shard_map/pallas_call | solution.py:146
  76.2 14.6 %all_to_all.15 = f32[16,8,128]{2,1,0:T(8,128)S(1)} all-to-all(f32[16,8,128]{2,1,0:T(8,128)S(1)} %get-tuple-element.8), channel_id=1, replica_groups={{0,4,8,12,16,20,24,28,32,36,40,44,48,52,56,60},{64,68,72,76,80,84,88,92..., dimensions={0} | all-to-all | bytes 131072 | tf_op jit(solution)/shard_map/all_to_all | solution.py:182
  90.8 15.0 %all_to_all.16 = f32[12,8,128]{2,1,0:T(8,128)S(1)} all-to-all(f32[12,8,128]{2,1,0:T(8,128)S(1)} %broadcast_in_dim.5), channel_id=1, replica_groups={{0,64,128,192,256,320,384,448,512,576,640,704},{4,68,132,196,260,324,38..., dimensions={0} | all-to-all | bytes 98304 | tf_op jit(solution)/shard_map/all_to_all | solution.py:22
  105.9 0.7 broadcast_multiply_fusion
  (8 shorter events, 0.1 us)
Async XLA Ops:
  0.0 1.4 %copy-start = (bf16[2,256,1536]{2,1,0:T(8,128)(2,1)S(1)}, bf16[2,256,1536]{2,1,0:T(8,128)(2,1)}, u32[]{:S(2)}) copy-start(bf16[2,256,1536]{2,1,0:T(8,128)(2,1)} %slab_ref.1) | copy-start | bytes 4718596
  1.4 0.7 copy-start.1
  2.1 6.6 %copy-start.3 = (bf16[2,32,128]{2,1,0:T(8,128)(2,1)S(1)}, bf16[2,32,128]{2,1,0:T(8,128)(2,1)}, u32[]{:S(2)}) copy-start(bf16[2,32,128]{2,1,0:T(8,128)(2,1)} %param.6) | copy-start | bytes 49156
  3.2 31.0 %collective-permute-start.2 = (bf16[528,768]{1,0:T(8,128)(2,1)S(1)}, bf16[528,768]{1,0:T(8,128)(2,1)S(1)}, u32[]{:S(2)}, u32[]{:S(2)}) collective-permute-start(bf16[528,768]{1,0:T(8,128)(2,1)S(1)} %shard_map.46.refs_0_), channel_id=1, source_target_pairs={{0,2},{1,3},{2,0},{3,1},{4,6},{5,7},{6,4},{7,5},{8,10},{9,11},{10,... | collective-permute-start | bytes 2433032 | tf_op jit(solution)/shard_map/ppermute | solution.py:171
  9.6 38.4 %all-to-all-start = ((bf16[24,2,32,128]{3,2,1,0:T(8,128)(2,1)}), bf16[24,2,32,128]{3,2,1,0:T(8,128)(2,1)}, u32[]{:S(2)}, u32[]{:S(2)}) async-start(bf16[24,2,32,128]{3,2,1,0:T(8,128)(2,1)} %broadcast_in_dim.4), calls=%async_computation | async-start | bytes 786432 | tf_op jit(solution)/shard_map/all_to_all | solution.py:22
  28.8 19.1 %collective-permute-start.1 = (bf16[528,768]{1,0:T(8,128)(2,1)S(1)}, bf16[528,768]{1,0:T(8,128)(2,1)S(1)}, u32[]{:S(2)}, u32[]{:S(2)}) collective-permute-start(bf16[528,768]{1,0:T(8,128)(2,1)S(1)} %shard_map.46.refs_0_), channel_id=1, source_target_pairs={{0,3},{1,0},{2,1},{3,2},{4,7},{5,4},{6,5},{7,6},{8,11},{9,8},{10,9... | collective-permute-start | bytes 2433032 | tf_op jit(solution)/shard_map/ppermute | solution.py:171
  31.6 20.1 %collective-permute-start = (bf16[528,768]{1,0:T(8,128)(2,1)S(1)}, bf16[528,768]{1,0:T(8,128)(2,1)S(1)}, u32[]{:S(2)}, u32[]{:S(2)}) collective-permute-start(bf16[528,768]{1,0:T(8,128)(2,1)S(1)} %shard_map.46.refs_0_), channel_id=1, source_target_pairs={{0,1},{1,2},{2,3},{3,0},{4,5},{5,6},{6,7},{7,4},{8,9},{9,10},{10,1... | collective-permute-start | bytes 2433032 | tf_op jit(solution)/shard_map/ppermute | solution.py:171
  48.0 18.0 %collective-permute-start.5 = (bf16[24,2,32,128]{3,2,1,0:T(8,128)(2,1)}, bf16[24,2,32,128]{3,2,1,0:T(8,128)(2,1)S(1)}, u32[]{:S(2)}, u32[]{:S(2)}) collective-permute-start(bf16[24,2,32,128]{3,2,1,0:T(8,128)(2,1)} %all-to-all-done), channel_id=1, source_target_pairs={{0,16},{4,132},{8,56},{12,140},{16,32},{20,148},{24,8},{28,156},{3... | collective-permute-start | bytes 1179656 | tf_op jit(solution)/shard_map/ppermute | solution.py:174
  51.8 17.6 %collective-permute-start.4 = (bf16[24,2,32,128]{3,2,1,0:T(8,128)(2,1)}, bf16[24,2,32,128]{3,2,1,0:T(8,128)(2,1)S(1)}, u32[]{:S(2)}, u32[]{:S(2)}) collective-permute-start(bf16[24,2,32,128]{3,2,1,0:T(8,128)(2,1)} %all-to-all-done), channel_id=1, source_target_pairs={{0,56},{4,708},{8,0},{12,716},{16,8},{20,724},{24,16},{28,732},{32... | collective-permute-start | bytes 1179656 | tf_op jit(solution)/shard_map/ppermute | solution.py:174
  61.2 10.5 %collective-permute-start.3 = (bf16[24,2,32,128]{3,2,1,0:T(8,128)(2,1)}, bf16[24,2,32,128]{3,2,1,0:T(8,128)(2,1)S(1)}, u32[]{:S(2)}, u32[]{:S(2)}) collective-permute-start(bf16[24,2,32,128]{3,2,1,0:T(8,128)(2,1)} %all-to-all-done), channel_id=1, source_target_pairs={{0,8},{4,68},{8,16},{12,76},{16,24},{20,84},{24,32},{28,92},{32,40... | collective-permute-start | bytes 1179656 | tf_op jit(solution)/shard_map/ppermute | solution.py:174
  66.0 8.1 %copy-start.2 = (s32[2,1]{0,1:T(1,128)S(1)}, s32[2,1]{0,1:T(1,128)}, u32[]{:S(2)}) copy-start(s32[2,1]{0,1:T(1,128)} %param.7) | copy-start | bytes 28

commit v6 on v5

--- a/solution.py
+++ b/solution.py
@@ -167,11 +167,13 @@
     place = jnp.stack([lax.axis_index("row"), lax.axis_index("col")]).astype(jnp.int32)
     held = spread(panel, "row", GROUP, MIXED_GROUPS)
     packed = pack(slab, slab_fill)
-    lefts = [packed] + [
-        lax.ppermute(packed, "col", [(x, (x + step) % NX) for x in range(NX)])
-        for step in (1, NX - 1, 2)
-    ]
+    below = lax.ppermute(packed, "col", UP)
+    above = lax.ppermute(packed, "col", DOWN)
+    across = lax.ppermute(below, "col", UP)
     mine = [held] + [lax.ppermute(held, "row", shift_moves(s)) for s in SHIFTS[1:]]
+    moved, (above, across) = lax.optimization_barrier((mine[1:], (above, across)))
+    mine = [held] + moved
+    lefts = [packed, below, above, across]
     pieces = [lax.all_gather(piece, "row", axis_index_groups=CORE_GROUPS) for piece in mine]
     tail = sections * row_count
     count = sections * row_count // TILE * (SLOTS + 1)

time: 107 us -> 106 us (level)
  waiting for transfers between devices: 14.6 us -> 9.58 us
  blocking collectives: 39.4 us -> 43.5 us
    ppermute x3, waiting for transfers between devices: 13.7 us -> 0.01 us  [the longest x1 0.01 us: shards(): below = lax.ppermute(packed, 'col', UP)]
    all_gather x4, blocking collectives: 9.78 us -> 18.9 us  [shards(): lax.all_gather(piece, 'row', axis_index_groups=CORE_GROUPS)]
    all_to_all x1, waiting for transfers between devices: 0.01 us -> 7.47 us  [spread(): lax.all_to_all(copies, axis, 0, 0, tiled=True, axis_index_groups=groups)]
    all_to_all x1, blocking collectives: 14.6 us -> 11.1 us  [shards(): lax.all_to_all(sums, 'row', 0, 0, tiled=True, axis_index_groups=PLANE_GRO...]
    all_to_all x1, blocking collectives: 15 us -> 13.5 us  [spread(): lax.all_to_all(copies, axis, 0, 0, tiled=True, axis_index_groups=groups)]
    ppermute x3, starting transfers between devices: 10.8 us -> 9.24 us  [the longest x1 3.95 us: shards(): below = lax.ppermute(packed, 'col', UP)]
    ppermute x3, waiting for transfers between devices: 0.89 us -> 2.1 us  [shards(): lax.ppermute(held, 'row', shift_moves(s))]
where the time goes in v6:
time: 106 us; the launch traced here: 105 us
  starting transfers between devices  44.8 us (42%)
  blocking collectives  43.5 us (41%)
  waiting for transfers between devices  9.58 us (9%)
  Pallas kernels  3.26 us (3%)
  local copies, waits for them, and re-layouts  2.95 us (3%)
    all_to_all x1, starting transfers between devices, spread(): lax.all_to_all(copies, axis, 0, 0, tiled=True, axis_index_groups=groups)  19.2 us
    all_gather x4, blocking collectives, shards(): lax.all_gather(piece, 'row', axis_index_groups=CORE_GROUPS)  18.9 us
    ppermute x3, starting transfers between devices, shards(): lax.ppermute(held, 'row', shift_moves(s))  16.3 us
    all_to_all x1, blocking collectives, spread(): lax.all_to_all(copies, axis, 0, 0, tiled=True, axis_index_groups=groups)  13.5 us
    all_to_all x1, blocking collectives, shards(): lax.all_to_all(sums, 'row', 0, 0, tiled=True, axis_index_groups=PLANE_GRO...  11.1 us
    all_to_all x1, waiting for transfers between devices, spread(): lax.all_to_all(copies, axis, 0, 0, tiled=True, axis_index_groups=groups)  7.47 us
    ppermute x1, starting transfers between devices, shards(): below = lax.ppermute(packed, 'col', UP)  3.95 us
    ppermute x1, starting transfers between devices, shards(): above = lax.ppermute(packed, 'col', DOWN)  3.37 us
  transfers between devices with their start and end apart: 7, of which 2 were waited for; matrix products, arithmetic and copies ran while one was open for 1% of the time, Pallas kernels for 0%

profile of v6, /device:TPU:1, one launch (start us, length us, event | category | flops | bytes accessed | tf_op | source)
XLA Modules:
  0.0 105.1 jit_solution(14182988477827795473)
XLA Ops:
  0.0 0.0 copy-start
  0.0 1.4 %copy-done = bf16[2,256,1536]{2,1,0:T(8,128)(2,1)S(1)} copy-done((bf16[2,256,1536]{2,1,0:T(8,128)(2,1)S(1)}, bf16[2,256,1536]{2,1,0:T(8,128)(2,1)}, u32[]{:S(2)}) %copy-start) | copy-done | bytes 1572888
  1.4 0.0 copy-start.1
  1.4 0.7 copy-done.1
  2.1 0.0 copy-start.3
  2.1 1.1 %shard_map.46.refs_0_ = bf16[528,768]{1,0:T(8,128)(2,1)S(1)} custom-call(s32[2,2,12]{2,1,0:T(2,128)S(1)} %copy-done.1, bf16[2,256,1536]{2,1,0:T(8,128)(2,1)S(1)} %copy-done), custom_call_target="tpu_custom_call" | custom-call | bytes 2097152 | tf_op jit(solution)/shard_map/pallas_call | solution.py:87
  3.2 3.9 %collective-permute-start = (bf16[528,768]{1,0:T(8,128)(2,1)S(1)}, bf16[528,768]{1,0:T(8,128)(2,1)S(1)}, u32[]{:S(2)}, u32[]{:S(2)}) collective-permute-start(bf16[528,768]{1,0:T(8,128)(2,1)S(1)} %shard_map.46.refs_0_), channel_id=1, source_target_pairs={{0,1},{1,2},{2,3},{3,0},{4,5},{5,6},{6,7},{7,4},{8,9},{9,10},{10,1... | collective-permute-start | bytes 2433032 | tf_op jit(solution)/shard_map/ppermute | solution.py:170
  7.2 0.0 copy-done.3
  7.2 0.8 broadcast_in_dim.4
  8.0 19.2 %all-to-all-start = ((bf16[24,2,32,128]{3,2,1,0:T(8,128)(2,1)}), bf16[24,2,32,128]{3,2,1,0:T(8,128)(2,1)}, u32[]{:S(2)}, u32[]{:S(2)}) async-start(bf16[24,2,32,128]{3,2,1,0:T(8,128)(2,1)} %broadcast_in_dim.4), calls=%async_computation | async-start | bytes 786432 | tf_op jit(solution)/shard_map/all_to_all | solution.py:22
  27.3 3.4 %collective-permute-start.4 = (bf16[528,768]{1,0:T(8,128)(2,1)S(1)}, bf16[528,768]{1,0:T(8,128)(2,1)S(1)}, u32[]{:S(2)}, u32[]{:S(2)}) collective-permute-start(bf16[528,768]{1,0:T(8,128)(2,1)S(1)} %shard_map.46.refs_0_), channel_id=1, source_target_pairs={{1,0},{2,1},{3,2},{0,3},{5,4},{6,5},{7,6},{4,7},{9,8},{10,9},{11,1... | collective-permute-start | bytes 2433032 | tf_op jit(solution)/shard_map/ppermute | solution.py:171
  30.7 0.0 collective-permute-done.refs_1_
  30.7 1.9 %collective-permute-start.5 = (bf16[528,768]{1,0:T(8,128)(2,1)S(1)}, bf16[528,768]{1,0:T(8,128)(2,1)S(1)}, u32[]{:S(2)}, u32[]{:S(2)}) collective-permute-start(bf16[528,768]{1,0:T(8,128)(2,1)S(1)} %collective-permute-done.refs_1_), channel_id=1, source_target_pairs={{0,1},{1,2},{2,3},{3,0},{4,5},{5,6},{6,7},{7,4},{8,9},{9,10},{10,1... | collective-permute-start | bytes 2433032 | tf_op jit(solution)/shard_map/ppermute | solution.py:172
  32.6 0.1 pad_add_fusion.place_ref
  32.7 7.5 %all-to-all-done = bf16[24,2,32,128]{3,2,1,0:T(8,128)(2,1)} async-done(((bf16[24,2,32,128]{3,2,1,0:T(8,128)(2,1)}), bf16[24,2,32,128]{3,2,1,0:T(8,128)(2,1)}, u32[]{:S(2)}, u32[]{:S(2)}) %all-to-all-start) | async-done | bytes 393248 | tf_op jit(solution)/shard_map/all_to_all | solution.py:22
  40.2 7.4 %collective-permute-start.1 = (bf16[24,2,32,128]{3,2,1,0:T(8,128)(2,1)}, bf16[24,2,32,128]{3,2,1,0:T(8,128)(2,1)S(1)}, u32[]{:S(2)}, u32[]{:S(2)}) collective-permute-start(bf16[24,2,32,128]{3,2,1,0:T(8,128)(2,1)} %all-to-all-done), channel_id=1, source_target_pairs={{0,8},{4,68},{8,16},{12,76},{16,24},{20,84},{24,32},{28,92},{32,40... | collective-permute-start | bytes 1179656 | tf_op jit(solution)/shard_map/ppermute | solution.py:173
  47.6 6.7 %collective-permute-start.2 = (bf16[24,2,32,128]{3,2,1,0:T(8,128)(2,1)}, bf16[24,2,32,128]{3,2,1,0:T(8,128)(2,1)S(1)}, u32[]{:S(2)}, u32[]{:S(2)}) collective-permute-start(bf16[24,2,32,128]{3,2,1,0:T(8,128)(2,1)} %all-to-all-done), channel_id=1, source_target_pairs={{0,56},{4,708},{8,0},{12,716},{16,8},{20,724},{24,16},{28,732},{32... | collective-permute-start | bytes 1179656 | tf_op jit(solution)/shard_map/ppermute | solution.py:173
  54.3 2.2 %collective-permute-start.3 = (bf16[24,2,32,128]{3,2,1,0:T(8,128)(2,1)}, bf16[24,2,32,128]{3,2,1,0:T(8,128)(2,1)S(1)}, u32[]{:S(2)}, u32[]{:S(2)}) collective-permute-start(bf16[24,2,32,128]{3,2,1,0:T(8,128)(2,1)} %all-to-all-done), channel_id=1, source_target_pairs={{0,16},{4,132},{8,56},{12,140},{16,32},{20,148},{24,8},{28,156},{3... | collective-permute-start | bytes 1179656 | tf_op jit(solution)/shard_map/ppermute | solution.py:173
  56.5 6.5 %all-gather = bf16[48,2,32,128]{3,2,1,0:T(8,128)(2,1)S(1)} all-gather(bf16[24,2,32,128]{3,2,1,0:T(8,128)(2,1)} %all-to-all-done), channel_id=2, replica_groups={{0,4},{8,12},{16,20},{24,28},{32,36},{40,44},{48,52},{56,60},{64,68},{7..., dimensions={0}, use_global_device_ids=true | all-gather | bytes 1179648 | tf_op jit(solution)/shard_map/all_gather | solution.py:177
  63.0 0.0 copy-start.2
  63.0 0.0 collective-permute-done.4.refs_2_
  63.0 0.0 collective-permute-done.1
  63.0 0.0 collective-permute-done.2
  63.0 2.1 %collective-permute-done.3 = bf16[24,2,32,128]{3,2,1,0:T(8,128)(2,1)S(1)} collective-permute-done((bf16[24,2,32,128]{3,2,1,0:T(8,128)(2,1)}, bf16[24,2,32,128]{3,2,1,0:T(8,128)(2,1)S(1)}, u32[]{:S(2)}, u32[]{:S(2)}) %collective-permute-start.3) | collective-permute-done | bytes 393248 | tf_op jit(solution)/shard_map/ppermute | solution.py:173
  65.1 0.0 collective-permute-done.5.refs_3_
  65.1 7.7 %all-gather.3 = bf16[48,2,32,128]{3,2,1,0:T(8,128)(2,1)S(1)} all-gather(bf16[24,2,32,128]{3,2,1,0:T(8,128)(2,1)S(1)} %collective-permute-done.3), channel_id=5, replica_groups={{0,4},{8,12},{16,20},{24,28},{32,36},{40,44},{48,52},{56,60},{64,68},{7..., dimensions={0}, use_global_device_ids=true | all-gather | bytes 1179648 | tf_op jit(solution)/shard_map/all_gather | solution.py:177
  72.8 2.4 %all-gather.1 = bf16[48,2,32,128]{3,2,1,0:T(8,128)(2,1)S(1)} all-gather(bf16[24,2,32,128]{3,2,1,0:T(8,128)(2,1)S(1)} %collective-permute-done.1), channel_id=3, replica_groups={{0,4},{8,12},{16,20},{24,28},{32,36},{40,44},{48,52},{56,60},{64,68},{7..., dimensions={0}, use_global_device_ids=true | all-gather | bytes 1179648 | tf_op jit(solution)/shard_map/all_gather | solution.py:177
  75.2 2.4 %all-gather.2 = bf16[48,2,32,128]{3,2,1,0:T(8,128)(2,1)S(1)} all-gather(bf16[24,2,32,128]{3,2,1,0:T(8,128)(2,1)S(1)} %collective-permute-done.2), channel_id=4, replica_groups={{0,4},{8,12},{16,20},{24,28},{32,36},{40,44},{48,52},{56,60},{64,68},{7..., dimensions={0}, use_global_device_ids=true | all-gather | bytes 1179648 | tf_op jit(solution)/shard_map/all_gather | solution.py:177
  77.5 0.1 maximum_convert_fusion.words_ref
  77.6 0.0 copy-done.2
  77.6 2.1 %shard_map.47 = (f32[256,128]{1,0:T(8,128)S(1)}, f32[16,8,128]{2,1,0:T(8,128)S(1)}) custom-call(s32[2]{0:T(128)S(1)} %pad_add_fusion.place_ref, s32[112]{0:T(128)S(1)} %maximum_convert_fusion.words_ref, s32[2]{0:T(128)S(1)} %bitcast.19, bf16[528,768]{1,0:T(8,128)(2,1)S(1)} %shard_map.46.refs_0_, bf16[528,768]{1,0:T(8,128)(2,1)S(1)} %collective-permute-done.refs_1_, ...), custom_call_target="tpu_custom_call" | custom-call | flops 402653184 | bytes 7340032 | tf_op jit(solution)/shard_map/pallas_call | solution.py:146
  79.8 11.1 %all_to_all.15 = f32[16,8,128]{2,1,0:T(8,128)S(1)} all-to-all(f32[16,8,128]{2,1,0:T(8,128)S(1)} %get-tuple-element.18), channel_id=1, replica_groups={{0,4,8,12,16,20,24,28,32,36,40,44,48,52,56,60},{64,68,72,76,80,84,88,92..., dimensions={0} | all-to-all | bytes 131072 | tf_op jit(solution)/shard_map/all_to_all | solution.py:184
  90.9 13.5 %all_to_all.16 = f32[12,8,128]{2,1,0:T(8,128)S(1)} all-to-all(f32[12,8,128]{2,1,0:T(8,128)S(1)} %broadcast_in_dim.5), channel_id=1, replica_groups={{0,64,128,192,256,320,384,448,512,576,640,704},{4,68,132,196,260,324,38..., dimensions={0} | all-to-all | bytes 98304 | tf_op jit(solution)/shard_map/all_to_all | solution.py:22
  104.5 0.7 broadcast_multiply_fusion
  (7 shorter events, 0.1 us)
Async XLA Ops:
  0.0 1.4 %copy-start = (bf16[2,256,1536]{2,1,0:T(8,128)(2,1)S(1)}, bf16[2,256,1536]{2,1,0:T(8,128)(2,1)}, u32[]{:S(2)}) copy-start(bf16[2,256,1536]{2,1,0:T(8,128)(2,1)} %slab_ref.1) | copy-start | bytes 4718596
  1.4 0.7 copy-start.1
  2.1 5.1 %copy-start.3 = (bf16[2,32,128]{2,1,0:T(8,128)(2,1)S(1)}, bf16[2,32,128]{2,1,0:T(8,128)(2,1)}, u32[]{:S(2)}) copy-start(bf16[2,32,128]{2,1,0:T(8,128)(2,1)} %param.6) | copy-start | bytes 49156
  3.2 27.4 %collective-permute-start = (bf16[528,768]{1,0:T(8,128)(2,1)S(1)}, bf16[528,768]{1,0:T(8,128)(2,1)S(1)}, u32[]{:S(2)}, u32[]{:S(2)}) collective-permute-start(bf16[528,768]{1,0:T(8,128)(2,1)S(1)} %shard_map.46.refs_0_), channel_id=1, source_target_pairs={{0,1},{1,2},{2,3},{3,0},{4,5},{5,6},{6,7},{7,4},{8,9},{9,10},{10,1... | collective-permute-start | bytes 2433032 | tf_op jit(solution)/shard_map/ppermute | solution.py:170
  8.0 32.1 %all-to-all-start = ((bf16[24,2,32,128]{3,2,1,0:T(8,128)(2,1)}), bf16[24,2,32,128]{3,2,1,0:T(8,128)(2,1)}, u32[]{:S(2)}, u32[]{:S(2)}) async-start(bf16[24,2,32,128]{3,2,1,0:T(8,128)(2,1)} %broadcast_in_dim.4), calls=%async_computation | async-start | bytes 786432 | tf_op jit(solution)/shard_map/all_to_all | solution.py:22
  27.3 35.7 %collective-permute-start.4 = (bf16[528,768]{1,0:T(8,128)(2,1)S(1)}, bf16[528,768]{1,0:T(8,128)(2,1)S(1)}, u32[]{:S(2)}, u32[]{:S(2)}) collective-permute-start(bf16[528,768]{1,0:T(8,128)(2,1)S(1)} %shard_map.46.refs_0_), channel_id=1, source_target_pairs={{1,0},{2,1},{3,2},{0,3},{5,4},{6,5},{7,6},{4,7},{9,8},{10,9},{11,1... | collective-permute-start | bytes 2433032 | tf_op jit(solution)/shard_map/ppermute | solution.py:171
  30.7 34.4 %collective-permute-start.5 = (bf16[528,768]{1,0:T(8,128)(2,1)S(1)}, bf16[528,768]{1,0:T(8,128)(2,1)S(1)}, u32[]{:S(2)}, u32[]{:S(2)}) collective-permute-start(bf16[528,768]{1,0:T(8,128)(2,1)S(1)} %collective-permute-done.refs_1_), channel_id=1, source_target_pairs={{0,1},{1,2},{2,3},{3,0},{4,5},{5,6},{6,7},{7,4},{8,9},{9,10},{10,1... | collective-permute-start | bytes 2433032 | tf_op jit(solution)/shard_map/ppermute | solution.py:172
  40.2 22.8 %collective-permute-start.1 = (bf16[24,2,32,128]{3,2,1,0:T(8,128)(2,1)}, bf16[24,2,32,128]{3,2,1,0:T(8,128)(2,1)S(1)}, u32[]{:S(2)}, u32[]{:S(2)}) collective-permute-start(bf16[24,2,32,128]{3,2,1,0:T(8,128)(2,1)} %all-to-all-done), channel_id=1, source_target_pairs={{0,8},{4,68},{8,16},{12,76},{16,24},{20,84},{24,32},{28,92},{32,40... | collective-permute-start | bytes 1179656 | tf_op jit(solution)/shard_map/ppermute | solution.py:173
  47.6 15.4 %collective-permute-start.2 = (bf16[24,2,32,128]{3,2,1,0:T(8,128)(2,1)}, bf16[24,2,32,128]{3,2,1,0:T(8,128)(2,1)S(1)}, u32[]{:S(2)}, u32[]{:S(2)}) collective-permute-start(bf16[24,2,32,128]{3,2,1,0:T(8,128)(2,1)} %all-to-all-done), channel_id=1, source_target_pairs={{0,56},{4,708},{8,0},{12,716},{16,8},{20,724},{24,16},{28,732},{32... | collective-permute-start | bytes 1179656 | tf_op jit(solution)/shard_map/ppermute | solution.py:173
  54.3 10.8 %collective-permute-start.3 = (bf16[24,2,32,128]{3,2,1,0:T(8,128)(2,1)}, bf16[24,2,32,128]{3,2,1,0:T(8,128)(2,1)S(1)}, u32[]{:S(2)}, u32[]{:S(2)}) collective-permute-start(bf16[24,2,32,128]{3,2,1,0:T(8,128)(2,1)} %all-to-all-done), channel_id=1, source_target_pairs={{0,16},{4,132},{8,56},{12,140},{16,32},{20,148},{24,8},{28,156},{3... | collective-permute-start | bytes 1179656 | tf_op jit(solution)/shard_map/ppermute | solution.py:173
  63.0 14.6 %copy-start.2 = (s32[2,1]{0,1:T(1,128)S(1)}, s32[2,1]{0,1:T(1,128)}, u32[]{:S(2)}) copy-start(s32[2,1]{0,1:T(1,128)} %param.7) | copy-start | bytes 28

commit v7 on v6

--- a/solution.py
+++ b/solution.py
@@ -37,7 +37,7 @@
     return moves
 
 
-SHIFTS = (0, 1, -1, 2)
+SHIFTS = (0, 2, 1, -1)
 MIXED_GROUPS = [
     [row_of(z, b + 4 * h, 0) for z in range(NZ) for h in range(2)] for b in range(4)
 ] + [[row_of(j + 4 * i, y, 1) for i in range(3) for y in range(NY)] for j in range(4)]
@@ -101,7 +101,7 @@
     row, col = place_ref[0], place_ref[1]
     z, y = row // (NY * NC), (row // NC) % NY
     for step, piece in enumerate(pieces):
-        if step == 3:
+        if SHIFTS[step] == 2:
             y_from = jnp.where(y % 2 == 0, y - 2, y + 2)
             z_from = jnp.where(z % 2 == 0, z - 2, z + 2)
         else:

time: 106 us -> 105 us (level)
  waiting for transfers between devices: 9.58 us -> 8.38 us
    all_gather x4, blocking collectives: 18.9 us -> 16.4 us  [shards(): lax.all_gather(piece, 'row', axis_index_groups=CORE_GROUPS)]
    all_to_all x1, blocking collectives: 11.1 us -> 12.4 us  [shards(): lax.all_to_all(sums, 'row', 0, 0, tiled=True, axis_index_groups=PLANE_GRO...]
    ppermute x3, waiting for transfers between devices: 2.1 us -> 0.91 us  [shards(): lax.ppermute(held, 'row', shift_moves(s))]
where the time goes in v7:
time: 105 us; the launch traced here: 104 us
  starting transfers between devices  45.7 us (44%)
  blocking collectives  42.7 us (41%)
  waiting for transfers between devices  8.38 us (8%)
  Pallas kernels  3.25 us (3%)
  local copies, waits for them, and re-layouts  2.95 us (3%)
    all_to_all x1, starting transfers between devices, spread(): lax.all_to_all(copies, axis, 0, 0, tiled=True, axis_index_groups=groups)  19.2 us
    ppermute x3, starting transfers between devices, shards(): lax.ppermute(held, 'row', shift_moves(s))  17.2 us
    all_gather x4, blocking collectives, shards(): lax.all_gather(piece, 'row', axis_index_groups=CORE_GROUPS)  16.4 us
    all_to_all x1, blocking collectives, spread(): lax.all_to_all(copies, axis, 0, 0, tiled=True, axis_index_groups=groups)  14 us
    all_to_all x1, blocking collectives, shards(): lax.all_to_all(sums, 'row', 0, 0, tiled=True, axis_index_groups=PLANE_GRO...  12.4 us
    all_to_all x1, waiting for transfers between devices, spread(): lax.all_to_all(copies, axis, 0, 0, tiled=True, axis_index_groups=groups)  7.47 us
    ppermute x1, starting transfers between devices, shards(): below = lax.ppermute(packed, 'col', UP)  3.95 us
    ppermute x1, starting transfers between devices, shards(): above = lax.ppermute(packed, 'col', DOWN)  3.37 us
  transfers between devices with their start and end apart: 7, of which 2 were waited for; matrix products, arithmetic and copies ran while one was open for 1% of the time, Pallas kernels for 0%

profile of v7, /device:TPU:1, one launch (start us, length us, event | category | flops | bytes accessed | tf_op | source)
XLA Modules:
  0.0 104.0 jit_solution(17781476393911661519)
XLA Ops:
  0.0 0.0 copy-start
  0.0 1.4 %copy-done = bf16[2,256,1536]{2,1,0:T(8,128)(2,1)S(1)} copy-done((bf16[2,256,1536]{2,1,0:T(8,128)(2,1)S(1)}, bf16[2,256,1536]{2,1,0:T(8,128)(2,1)}, u32[]{:S(2)}) %copy-start) | copy-done | bytes 1572888
  1.4 0.0 copy-start.1
  1.4 0.7 copy-done.1
  2.1 0.0 copy-start.3
  2.1 1.1 %shard_map.46.refs_0_ = bf16[528,768]{1,0:T(8,128)(2,1)S(1)} custom-call(s32[2,2,12]{2,1,0:T(2,128)S(1)} %copy-done.1, bf16[2,256,1536]{2,1,0:T(8,128)(2,1)S(1)} %copy-done), custom_call_target="tpu_custom_call" | custom-call | bytes 2097152 | tf_op jit(solution)/shard_map/pallas_call | solution.py:87
  3.2 3.9 %collective-permute-start = (bf16[528,768]{1,0:T(8,128)(2,1)S(1)}, bf16[528,768]{1,0:T(8,128)(2,1)S(1)}, u32[]{:S(2)}, u32[]{:S(2)}) collective-permute-start(bf16[528,768]{1,0:T(8,128)(2,1)S(1)} %shard_map.46.refs_0_), channel_id=1, source_target_pairs={{0,1},{1,2},{2,3},{3,0},{4,5},{5,6},{6,7},{7,4},{8,9},{9,10},{10,1... | collective-permute-start | bytes 2433032 | tf_op jit(solution)/shard_map/ppermute | solution.py:170
  7.2 0.0 copy-done.3
  7.2 0.8 broadcast_in_dim.4
  8.0 19.2 %all-to-all-start = ((bf16[24,2,32,128]{3,2,1,0:T(8,128)(2,1)}), bf16[24,2,32,128]{3,2,1,0:T(8,128)(2,1)}, u32[]{:S(2)}, u32[]{:S(2)}) async-start(bf16[24,2,32,128]{3,2,1,0:T(8,128)(2,1)} %broadcast_in_dim.4), calls=%async_computation | async-start | bytes 786432 | tf_op jit(solution)/shard_map/all_to_all | solution.py:22
  27.3 3.4 %collective-permute-start.4 = (bf16[528,768]{1,0:T(8,128)(2,1)S(1)}, bf16[528,768]{1,0:T(8,128)(2,1)S(1)}, u32[]{:S(2)}, u32[]{:S(2)}) collective-permute-start(bf16[528,768]{1,0:T(8,128)(2,1)S(1)} %shard_map.46.refs_0_), channel_id=1, source_target_pairs={{1,0},{2,1},{3,2},{0,3},{5,4},{6,5},{7,6},{4,7},{9,8},{10,9},{11,1... | collective-permute-start | bytes 2433032 | tf_op jit(solution)/shard_map/ppermute | solution.py:171
  30.7 0.0 collective-permute-done.refs_1_
  30.7 1.9 %collective-permute-start.5 = (bf16[528,768]{1,0:T(8,128)(2,1)S(1)}, bf16[528,768]{1,0:T(8,128)(2,1)S(1)}, u32[]{:S(2)}, u32[]{:S(2)}) collective-permute-start(bf16[528,768]{1,0:T(8,128)(2,1)S(1)} %collective-permute-done.refs_1_), channel_id=1, source_target_pairs={{0,1},{1,2},{2,3},{3,0},{4,5},{5,6},{6,7},{7,4},{8,9},{9,10},{10,1... | collective-permute-start | bytes 2433032 | tf_op jit(solution)/shard_map/ppermute | solution.py:172
  32.6 0.1 pad_add_fusion.place_ref
  32.7 7.5 %all-to-all-done = bf16[24,2,32,128]{3,2,1,0:T(8,128)(2,1)} async-done(((bf16[24,2,32,128]{3,2,1,0:T(8,128)(2,1)}), bf16[24,2,32,128]{3,2,1,0:T(8,128)(2,1)}, u32[]{:S(2)}, u32[]{:S(2)}) %all-to-all-start) | async-done | bytes 393248 | tf_op jit(solution)/shard_map/all_to_all | solution.py:22
  40.2 9.6 %collective-permute-start.1 = (bf16[24,2,32,128]{3,2,1,0:T(8,128)(2,1)}, bf16[24,2,32,128]{3,2,1,0:T(8,128)(2,1)S(1)}, u32[]{:S(2)}, u32[]{:S(2)}) collective-permute-start(bf16[24,2,32,128]{3,2,1,0:T(8,128)(2,1)} %all-to-all-done), channel_id=1, source_target_pairs={{0,16},{4,132},{8,56},{12,140},{16,32},{20,148},{24,8},{28,156},{3... | collective-permute-start | bytes 1179656 | tf_op jit(solution)/shard_map/ppermute | solution.py:173
  49.8 5.6 %collective-permute-start.2 = (bf16[24,2,32,128]{3,2,1,0:T(8,128)(2,1)}, bf16[24,2,32,128]{3,2,1,0:T(8,128)(2,1)S(1)}, u32[]{:S(2)}, u32[]{:S(2)}) collective-permute-start(bf16[24,2,32,128]{3,2,1,0:T(8,128)(2,1)} %all-to-all-done), channel_id=1, source_target_pairs={{0,8},{4,68},{8,16},{12,76},{16,24},{20,84},{24,32},{28,92},{32,40... | collective-permute-start | bytes 1179656 | tf_op jit(solution)/shard_map/ppermute | solution.py:173
  55.4 1.9 %collective-permute-start.3 = (bf16[24,2,32,128]{3,2,1,0:T(8,128)(2,1)}, bf16[24,2,32,128]{3,2,1,0:T(8,128)(2,1)S(1)}, u32[]{:S(2)}, u32[]{:S(2)}) collective-permute-start(bf16[24,2,32,128]{3,2,1,0:T(8,128)(2,1)} %all-to-all-done), channel_id=1, source_target_pairs={{0,56},{4,708},{8,0},{12,716},{16,8},{20,724},{24,16},{28,732},{32... | collective-permute-start | bytes 1179656 | tf_op jit(solution)/shard_map/ppermute | solution.py:173
  57.4 6.2 %all-gather = bf16[48,2,32,128]{3,2,1,0:T(8,128)(2,1)S(1)} all-gather(bf16[24,2,32,128]{3,2,1,0:T(8,128)(2,1)} %all-to-all-done), channel_id=2, replica_groups={{0,4},{8,12},{16,20},{24,28},{32,36},{40,44},{48,52},{56,60},{64,68},{7..., dimensions={0}, use_global_device_ids=true | all-gather | bytes 1179648 | tf_op jit(solution)/shard_map/all_gather | solution.py:177
  63.5 0.0 copy-start.2
  63.5 0.0 collective-permute-done.4.refs_2_
  63.5 0.0 collective-permute-done.1
  63.5 0.0 collective-permute-done.2
  63.6 0.9 collective-permute-done.3
  64.5 0.0 collective-permute-done.5.refs_3_
  64.5 5.5 %all-gather.3 = bf16[48,2,32,128]{3,2,1,0:T(8,128)(2,1)S(1)} all-gather(bf16[24,2,32,128]{3,2,1,0:T(8,128)(2,1)S(1)} %collective-permute-done.3), channel_id=5, replica_groups={{0,4},{8,12},{16,20},{24,28},{32,36},{40,44},{48,52},{56,60},{64,68},{7..., dimensions={0}, use_global_device_ids=true | all-gather | bytes 1179648 | tf_op jit(solution)/shard_map/all_gather | solution.py:177
  70.0 2.4 %all-gather.1 = bf16[48,2,32,128]{3,2,1,0:T(8,128)(2,1)S(1)} all-gather(bf16[24,2,32,128]{3,2,1,0:T(8,128)(2,1)S(1)} %collective-permute-done.1), channel_id=3, replica_groups={{0,4},{8,12},{16,20},{24,28},{32,36},{40,44},{48,52},{56,60},{64,68},{7..., dimensions={0}, use_global_device_ids=true | all-gather | bytes 1179648 | tf_op jit(solution)/shard_map/all_gather | solution.py:177
  72.3 2.4 %all-gather.2 = bf16[48,2,32,128]{3,2,1,0:T(8,128)(2,1)S(1)} all-gather(bf16[24,2,32,128]{3,2,1,0:T(8,128)(2,1)S(1)} %collective-permute-done.2), channel_id=4, replica_groups={{0,4},{8,12},{16,20},{24,28},{32,36},{40,44},{48,52},{56,60},{64,68},{7..., dimensions={0}, use_global_device_ids=true | all-gather | bytes 1179648 | tf_op jit(solution)/shard_map/all_gather | solution.py:177
  74.7 0.1 maximum_convert_fusion.words_ref
  74.8 0.0 copy-done.2
  74.8 2.1 %shard_map.47 = (f32[256,128]{1,0:T(8,128)S(1)}, f32[16,8,128]{2,1,0:T(8,128)S(1)}) custom-call(s32[2]{0:T(128)S(1)} %pad_add_fusion.place_ref, s32[112]{0:T(128)S(1)} %maximum_convert_fusion.words_ref, s32[2]{0:T(128)S(1)} %bitcast.19, bf16[528,768]{1,0:T(8,128)(2,1)S(1)} %shard_map.46.refs_0_, bf16[528,768]{1,0:T(8,128)(2,1)S(1)} %collective-permute-done.refs_1_, ...), custom_call_target="tpu_custom_call" | custom-call | flops 402653184 | bytes 7340032 | tf_op jit(solution)/shard_map/pallas_call | solution.py:146
  76.9 12.4 %all_to_all.15 = f32[16,8,128]{2,1,0:T(8,128)S(1)} all-to-all(f32[16,8,128]{2,1,0:T(8,128)S(1)} %get-tuple-element.18), channel_id=1, replica_groups={{0,4,8,12,16,20,24,28,32,36,40,44,48,52,56,60},{64,68,72,76,80,84,88,92..., dimensions={0} | all-to-all | bytes 131072 | tf_op jit(solution)/shard_map/all_to_all | solution.py:184
  89.3 14.0 %all_to_all.16 = f32[12,8,128]{2,1,0:T(8,128)S(1)} all-to-all(f32[12,8,128]{2,1,0:T(8,128)S(1)} %broadcast_in_dim.5), channel_id=1, replica_groups={{0,64,128,192,256,320,384,448,512,576,640,704},{4,68,132,196,260,324,38..., dimensions={0} | all-to-all | bytes 98304 | tf_op jit(solution)/shard_map/all_to_all | solution.py:22
  103.3 0.7 broadcast_multiply_fusion
  (7 shorter events, 0.1 us)
Async XLA Ops:
  0.0 1.4 %copy-start = (bf16[2,256,1536]{2,1,0:T(8,128)(2,1)S(1)}, bf16[2,256,1536]{2,1,0:T(8,128)(2,1)}, u32[]{:S(2)}) copy-start(bf16[2,256,1536]{2,1,0:T(8,128)(2,1)} %slab_ref.1) | copy-start | bytes 4718596
  1.4 0.7 copy-start.1
  2.1 5.1 %copy-start.3 = (bf16[2,32,128]{2,1,0:T(8,128)(2,1)S(1)}, bf16[2,32,128]{2,1,0:T(8,128)(2,1)}, u32[]{:S(2)}) copy-start(bf16[2,32,128]{2,1,0:T(8,128)(2,1)} %param.6) | copy-start | bytes 49156
  3.2 27.4 %collective-permute-start = (bf16[528,768]{1,0:T(8,128)(2,1)S(1)}, bf16[528,768]{1,0:T(8,128)(2,1)S(1)}, u32[]{:S(2)}, u32[]{:S(2)}) collective-permute-start(bf16[528,768]{1,0:T(8,128)(2,1)S(1)} %shard_map.46.refs_0_), channel_id=1, source_target_pairs={{0,1},{1,2},{2,3},{3,0},{4,5},{5,6},{6,7},{7,4},{8,9},{9,10},{10,1... | collective-permute-start | bytes 2433032 | tf_op jit(solution)/shard_map/ppermute | solution.py:170
  8.0 32.1 %all-to-all-start = ((bf16[24,2,32,128]{3,2,1,0:T(8,128)(2,1)}), bf16[24,2,32,128]{3,2,1,0:T(8,128)(2,1)}, u32[]{:S(2)}, u32[]{:S(2)}) async-start(bf16[24,2,32,128]{3,2,1,0:T(8,128)(2,1)} %broadcast_in_dim.4), calls=%async_computation | async-start | bytes 786432 | tf_op jit(solution)/shard_map/all_to_all | solution.py:22
  27.3 36.2 %collective-permute-start.4 = (bf16[528,768]{1,0:T(8,128)(2,1)S(1)}, bf16[528,768]{1,0:T(8,128)(2,1)S(1)}, u32[]{:S(2)}, u32[]{:S(2)}) collective-permute-start(bf16[528,768]{1,0:T(8,128)(2,1)S(1)} %shard_map.46.refs_0_), channel_id=1, source_target_pairs={{1,0},{2,1},{3,2},{0,3},{5,4},{6,5},{7,6},{4,7},{9,8},{10,9},{11,1... | collective-permute-start | bytes 2433032 | tf_op jit(solution)/shard_map/ppermute | solution.py:171
  30.7 33.8 %collective-permute-start.5 = (bf16[528,768]{1,0:T(8,128)(2,1)S(1)}, bf16[528,768]{1,0:T(8,128)(2,1)S(1)}, u32[]{:S(2)}, u32[]{:S(2)}) collective-permute-start(bf16[528,768]{1,0:T(8,128)(2,1)S(1)} %collective-permute-done.refs_1_), channel_id=1, source_target_pairs={{0,1},{1,2},{2,3},{3,0},{4,5},{5,6},{6,7},{7,4},{8,9},{9,10},{10,1... | collective-permute-start | bytes 2433032 | tf_op jit(solution)/shard_map/ppermute | solution.py:172
  40.2 23.4 %collective-permute-start.1 = (bf16[24,2,32,128]{3,2,1,0:T(8,128)(2,1)}, bf16[24,2,32,128]{3,2,1,0:T(8,128)(2,1)S(1)}, u32[]{:S(2)}, u32[]{:S(2)}) collective-permute-start(bf16[24,2,32,128]{3,2,1,0:T(8,128)(2,1)} %all-to-all-done), channel_id=1, source_target_pairs={{0,16},{4,132},{8,56},{12,140},{16,32},{20,148},{24,8},{28,156},{3... | collective-permute-start | bytes 1179656 | tf_op jit(solution)/shard_map/ppermute | solution.py:173
  49.8 13.7 %collective-permute-start.2 = (bf16[24,2,32,128]{3,2,1,0:T(8,128)(2,1)}, bf16[24,2,32,128]{3,2,1,0:T(8,128)(2,1)S(1)}, u32[]{:S(2)}, u32[]{:S(2)}) collective-permute-start(bf16[24,2,32,128]{3,2,1,0:T(8,128)(2,1)} %all-to-all-done), channel_id=1, source_target_pairs={{0,8},{4,68},{8,16},{12,76},{16,24},{20,84},{24,32},{28,92},{32,40... | collective-permute-start | bytes 1179656 | tf_op jit(solution)/shard_map/ppermute | solution.py:173
  55.4 9.0 %collective-permute-start.3 = (bf16[24,2,32,128]{3,2,1,0:T(8,128)(2,1)}, bf16[24,2,32,128]{3,2,1,0:T(8,128)(2,1)S(1)}, u32[]{:S(2)}, u32[]{:S(2)}) collective-permute-start(bf16[24,2,32,128]{3,2,1,0:T(8,128)(2,1)} %all-to-all-done), channel_id=1, source_target_pairs={{0,56},{4,708},{8,0},{12,716},{16,8},{20,724},{24,16},{28,732},{32... | collective-permute-start | bytes 1179656 | tf_op jit(solution)/shard_map/ppermute | solution.py:173
  63.5 11.2 %copy-start.2 = (s32[2,1]{0,1:T(1,128)S(1)}, s32[2,1]{0,1:T(1,128)}, u32[]{:S(2)}) copy-start(s32[2,1]{0,1:T(1,128)} %param.7) | copy-start | bytes 28

commit v8 on v7

--- a/solution.py
+++ b/solution.py
@@ -49,8 +49,17 @@
 CORE_GROUPS = [[r, r + 1] for r in range(0, NZ * NY * NC, NC)]
 
 
-def pack_kernel(fill_ref, slab_ref, out_ref):
+def pack_kernel(fill_ref, panel_ref, slab_hbm, out_ref, copies_ref, slab_ref, sems):
     sections, rows = slab_ref.shape[0], slab_ref.shape[1] // TILE
+    fetches = []
+    for group in range(sections * rows):
+        block = (group // rows, pl.ds(group % rows * TILE, TILE))
+        fetches.append(
+            pltpu.make_async_copy(slab_hbm.at[block], slab_ref.at[block], sems.at[group])
+        )
+        fetches[-1].start()
+    for copy in range(copies_ref.shape[0]):
+        copies_ref[copy] = panel_ref[...]
     cols = slab_ref.shape[2] // TILE
     lane = lax.broadcasted_iota(jnp.int32, (TAIL, TILE), 1)
     words = jnp.zeros((TAIL, TILE), jnp.float32)
@@ -59,6 +68,7 @@
         count = jnp.int32(0)
         for k in range(cols):
             count += fill_ref[s, r, k]
+        fetches[group].wait()
         seen = jnp.int32(0)
         for k in range(cols):
             filled = fill_ref[s, r, k]
@@ -80,18 +90,24 @@
     out_ref[tail, :TILE] = words.astype(jnp.bfloat16)
 
 
-def pack(slab, slab_fill):
+def pack(slab, slab_fill, panel):
     sections, rows, cols = slab.shape
     height = sections * rows + TAIL
     vmem = pl.BlockSpec(memory_space=pltpu.VMEM)
     return pl.pallas_call(
         pack_kernel,
-        out_shape=jax.ShapeDtypeStruct((height, SLOTS * TILE), jnp.bfloat16),
-        in_specs=[pl.BlockSpec(memory_space=pltpu.SMEM), vmem],
-        out_specs=vmem,
-        compiler_params=pltpu.CompilerParams(vmem_limit_bytes=16 * 2**20),
+        out_shape=(
+            jax.ShapeDtypeStruct((height, SLOTS * TILE), jnp.bfloat16),
+            jax.ShapeDtypeStruct((GROUP,) + panel.shape, jnp.bfloat16),
+        ),
+        in_specs=[pl.BlockSpec(memory_space=pltpu.SMEM), vmem, pl.BlockSpec(memory_space=pl.ANY)],
+        out_specs=(vmem, vmem),
+        scratch_shapes=[
+            pltpu.VMEM((sections, rows, cols), jnp.bfloat16),
+            pltpu.SemaphoreType.DMA((sections * rows // TILE,)),
+        ],
         cost_estimate=pl.CostEstimate(flops=0, bytes_accessed=2 * 2**20, transcendentals=0),
-    )(slab_fill, slab)
+    )(slab_fill, panel, slab)
 
 
 def product_kernel(place_ref, words_ref, keep_ref, *refs):
@@ -165,8 +181,8 @@
 def shards(slab, slab_fill, panel, out_fill):
     sections, row_count, local_cols = slab.shape
     place = jnp.stack([lax.axis_index("row"), lax.axis_index("col")]).astype(jnp.int32)
-    held = spread(panel, "row", GROUP, MIXED_GROUPS)
-    packed = pack(slab, slab_fill)
+    packed, copies = pack(slab, slab_fill, panel)
+    held = lax.all_to_all(copies, "row", 0, 0, tiled=True, axis_index_groups=MIXED_GROUPS)
     below = lax.ppermute(packed, "col", UP)
     above = lax.ppermute(packed, "col", DOWN)
     across = lax.ppermute(below, "col", UP)

time: 105 us -> 104 us (level)
  Pallas kernels: 3.25 us -> 5.55 us
  local copies, waits for them, and re-layouts: 2.95 us -> 0.69 us
    pallas_call x1, Pallas kernels: 1.13 us -> 3.37 us  [pack(): pl.pallas_call(pack_kernel, out_shape=(jax.ShapeDtypeStruct((height, SLOT...]
    unnamed x8 -> x4, local copies, waits for them, and re-layouts: 2.1 us -> 0.01 us
where the time goes in v8:
time: 104 us; the launch traced here: 103 us
  starting transfers between devices  45.6 us (44%)
  blocking collectives  42.5 us (41%)
  waiting for transfers between devices  7.7 us (7%)
  Pallas kernels  5.55 us (5%)
    all_to_all x1, starting transfers between devices, shards(): lax.all_to_all(copies, 'row', 0, 0, tiled=True, axis_index_groups=MIXED_G...  19.2 us
    ppermute x3, starting transfers between devices, shards(): lax.ppermute(held, 'row', shift_moves(s))  17.2 us
    all_gather x4, blocking collectives, shards(): lax.all_gather(piece, 'row', axis_index_groups=CORE_GROUPS)  16.2 us
    all_to_all x1, blocking collectives, spread(): lax.all_to_all(copies, axis, 0, 0, tiled=True, axis_index_groups=groups)  14 us
    all_to_all x1, blocking collectives, shards(): lax.all_to_all(sums, 'row', 0, 0, tiled=True, axis_index_groups=PLANE_GRO...  12.4 us
    all_to_all x1, waiting for transfers between devices, shards(): lax.all_to_all(copies, 'row', 0, 0, tiled=True, axis_index_groups=MIXED_G...  6.79 us
    ppermute x1, starting transfers between devices, shards(): below = lax.ppermute(packed, 'col', UP)  3.95 us
    ppermute x1, starting transfers between devices, shards(): above = lax.ppermute(packed, 'col', DOWN)  3.37 us
  transfers between devices with their start and end apart: 7, of which 2 were waited for; matrix products, arithmetic and copies ran while one was open for 1% of the time, Pallas kernels for 0%

profile of v8, /device:TPU:1, one launch (start us, length us, event | category | flops | bytes accessed | tf_op | source)
XLA Modules:
  0.0 103.0 jit_solution(3672186254859381477)
XLA Ops:
  0.0 3.4 %shard_map.46 = (bf16[528,768]{1,0:T(8,128)(2,1)}, bf16[24,2,32,128]{3,2,1,0:T(8,128)(2,1)}) custom-call(s32[2,2,12]{2,1,0:T(2,128)} %fill_ref.1, bf16[2,32,128]{2,1,0:T(8,128)(2,1)} %panel_ref.1, bf16[2,256,1536]{2,1,0:T(8,128)(2,1)} %slab_hbm.1), custom_call_target="tpu_custom_call" | custom-call | bytes 2097152 | tf_op jit(solution)/shard_map/pallas_call | solution.py:97
  3.4 3.9 %collective-permute-start = (bf16[528,768]{1,0:T(8,128)(2,1)}, bf16[528,768]{1,0:T(8,128)(2,1)S(1)}, u32[]{:S(2)}, u32[]{:S(2)}) collective-permute-start(bf16[528,768]{1,0:T(8,128)(2,1)} %get-tuple-element.14.refs_0_), channel_id=1, source_target_pairs={{0,1},{1,2},{2,3},{3,0},{4,5},{5,6},{6,7},{7,4},{8,9},{9,10},{10,1... | collective-permute-start | bytes 2433032 | tf_op jit(solution)/shard_map/ppermute | solution.py:186
  7.3 19.2 %all-to-all-start = ((bf16[24,2,32,128]{3,2,1,0:T(8,128)(2,1)}), bf16[24,2,32,128]{3,2,1,0:T(8,128)(2,1)S(1)}, u32[]{:S(2)}, u32[]{:S(2)}) async-start(bf16[24,2,32,128]{3,2,1,0:T(8,128)(2,1)} %get-tuple-element.15), calls=%async_computation | async-start | bytes 786432 | tf_op jit(solution)/shard_map/all_to_all | solution.py:185
  26.5 3.4 %collective-permute-start.4 = (bf16[528,768]{1,0:T(8,128)(2,1)}, bf16[528,768]{1,0:T(8,128)(2,1)S(1)}, u32[]{:S(2)}, u32[]{:S(2)}) collective-permute-start(bf16[528,768]{1,0:T(8,128)(2,1)} %get-tuple-element.14.refs_0_), channel_id=1, source_target_pairs={{1,0},{2,1},{3,2},{0,3},{5,4},{6,5},{7,6},{4,7},{9,8},{10,9},{11,1... | collective-permute-start | bytes 2433032 | tf_op jit(solution)/shard_map/ppermute | solution.py:187
  29.9 0.0 collective-permute-done.refs_1_
  29.9 1.9 %collective-permute-start.5 = (bf16[528,768]{1,0:T(8,128)(2,1)S(1)}, bf16[528,768]{1,0:T(8,128)(2,1)S(1)}, u32[]{:S(2)}, u32[]{:S(2)}) collective-permute-start(bf16[528,768]{1,0:T(8,128)(2,1)S(1)} %collective-permute-done.refs_1_), channel_id=1, source_target_pairs={{0,1},{1,2},{2,3},{3,0},{4,5},{5,6},{6,7},{7,4},{8,9},{9,10},{10,1... | collective-permute-start | bytes 2433032 | tf_op jit(solution)/shard_map/ppermute | solution.py:188
  31.8 0.1 pad_add_fusion.place_ref
  31.9 0.7 slice_bitcast_fusion.3
  32.6 6.8 %all-to-all-done = bf16[24,2,32,128]{3,2,1,0:T(8,128)(2,1)S(1)} async-done(((bf16[24,2,32,128]{3,2,1,0:T(8,128)(2,1)}), bf16[24,2,32,128]{3,2,1,0:T(8,128)(2,1)S(1)}, u32[]{:S(2)}, u32[]{:S(2)}) %all-to-all-start) | async-done | bytes 393248 | tf_op jit(solution)/shard_map/all_to_all | solution.py:185
  39.4 9.6 %collective-permute-start.1 = (bf16[24,2,32,128]{3,2,1,0:T(8,128)(2,1)S(1)}, bf16[24,2,32,128]{3,2,1,0:T(8,128)(2,1)S(1)}, u32[]{:S(2)}, u32[]{:S(2)}) collective-permute-start(bf16[24,2,32,128]{3,2,1,0:T(8,128)(2,1)S(1)} %all-to-all-done), channel_id=1, source_target_pairs={{0,16},{4,132},{8,56},{12,140},{16,32},{20,148},{24,8},{28,156},{3... | collective-permute-start | bytes 1179656 | tf_op jit(solution)/shard_map/ppermute | solution.py:189
  49.0 5.6 %collective-permute-start.2 = (bf16[24,2,32,128]{3,2,1,0:T(8,128)(2,1)S(1)}, bf16[24,2,32,128]{3,2,1,0:T(8,128)(2,1)S(1)}, u32[]{:S(2)}, u32[]{:S(2)}) collective-permute-start(bf16[24,2,32,128]{3,2,1,0:T(8,128)(2,1)S(1)} %all-to-all-done), channel_id=1, source_target_pairs={{0,8},{4,68},{8,16},{12,76},{16,24},{20,84},{24,32},{28,92},{32,40... | collective-permute-start | bytes 1179656 | tf_op jit(solution)/shard_map/ppermute | solution.py:189
  54.6 1.9 %collective-permute-start.3 = (bf16[24,2,32,128]{3,2,1,0:T(8,128)(2,1)S(1)}, bf16[24,2,32,128]{3,2,1,0:T(8,128)(2,1)S(1)}, u32[]{:S(2)}, u32[]{:S(2)}) collective-permute-start(bf16[24,2,32,128]{3,2,1,0:T(8,128)(2,1)S(1)} %all-to-all-done), channel_id=1, source_target_pairs={{0,56},{4,708},{8,0},{12,716},{16,8},{20,724},{24,16},{28,732},{32... | collective-permute-start | bytes 1179656 | tf_op jit(solution)/shard_map/ppermute | solution.py:189
  56.6 6.0 %all-gather = bf16[48,2,32,128]{3,2,1,0:T(8,128)(2,1)S(1)} all-gather(bf16[24,2,32,128]{3,2,1,0:T(8,128)(2,1)S(1)} %all-to-all-done), channel_id=2, replica_groups={{0,4},{8,12},{16,20},{24,28},{32,36},{40,44},{48,52},{56,60},{64,68},{7..., dimensions={0}, use_global_device_ids=true | all-gather | bytes 1179648 | tf_op jit(solution)/shard_map/all_gather | solution.py:193
  62.5 0.0 copy-start
  62.5 0.0 copy-start.1
  62.5 0.0 collective-permute-done.4.refs_2_
  62.5 0.0 collective-permute-done.1
  62.5 0.0 collective-permute-done.2
  62.5 0.9 collective-permute-done.3
  63.4 0.0 collective-permute-done.5.refs_3_
  63.5 5.5 %all-gather.3 = bf16[48,2,32,128]{3,2,1,0:T(8,128)(2,1)S(1)} all-gather(bf16[24,2,32,128]{3,2,1,0:T(8,128)(2,1)S(1)} %collective-permute-done.3), channel_id=5, replica_groups={{0,4},{8,12},{16,20},{24,28},{32,36},{40,44},{48,52},{56,60},{64,68},{7..., dimensions={0}, use_global_device_ids=true | all-gather | bytes 1179648 | tf_op jit(solution)/shard_map/all_gather | solution.py:193
  69.0 2.4 %all-gather.1 = bf16[48,2,32,128]{3,2,1,0:T(8,128)(2,1)S(1)} all-gather(bf16[24,2,32,128]{3,2,1,0:T(8,128)(2,1)S(1)} %collective-permute-done.1), channel_id=3, replica_groups={{0,4},{8,12},{16,20},{24,28},{32,36},{40,44},{48,52},{56,60},{64,68},{7..., dimensions={0}, use_global_device_ids=true | all-gather | bytes 1179648 | tf_op jit(solution)/shard_map/all_gather | solution.py:193
  71.3 2.4 %all-gather.2 = bf16[48,2,32,128]{3,2,1,0:T(8,128)(2,1)S(1)} all-gather(bf16[24,2,32,128]{3,2,1,0:T(8,128)(2,1)S(1)} %collective-permute-done.2), channel_id=4, replica_groups={{0,4},{8,12},{16,20},{24,28},{32,36},{40,44},{48,52},{56,60},{64,68},{7..., dimensions={0}, use_global_device_ids=true | all-gather | bytes 1179648 | tf_op jit(solution)/shard_map/all_gather | solution.py:193
  73.7 0.1 maximum_convert_fusion.words_ref
  73.8 0.0 copy-done
  73.8 0.0 copy-done.1
  73.8 2.2 %shard_map.47 = (f32[256,128]{1,0:T(8,128)S(1)}, f32[16,8,128]{2,1,0:T(8,128)S(1)}) custom-call(s32[2]{0:T(128)S(1)} %pad_add_fusion.place_ref, s32[112]{0:T(128)S(1)} %maximum_convert_fusion.words_ref, s32[2]{0:T(128)S(1)} %bitcast.19, bf16[528,768]{1,0:T(8,128)(2,1)S(1)} %copy-done, bf16[528,768]{1,0:T(8,128)(2,1)S(1)} %collective-permute-done.refs_1_, ...), custom_call_target="tpu_custom_call" | custom-call | flops 402653184 | bytes 7340032 | tf_op jit(solution)/shard_map/pallas_call | solution.py:162
  75.9 12.4 %all_to_all.15 = f32[16,8,128]{2,1,0:T(8,128)S(1)} all-to-all(f32[16,8,128]{2,1,0:T(8,128)S(1)} %get-tuple-element.22), channel_id=1, replica_groups={{0,4,8,12,16,20,24,28,32,36,40,44,48,52,56,60},{64,68,72,76,80,84,88,92..., dimensions={0} | all-to-all | bytes 131072 | tf_op jit(solution)/shard_map/all_to_all | solution.py:200
  88.3 14.0 %all_to_all.16 = f32[12,8,128]{2,1,0:T(8,128)S(1)} all-to-all(f32[12,8,128]{2,1,0:T(8,128)S(1)} %broadcast_in_dim.2), channel_id=1, replica_groups={{0,64,128,192,256,320,384,448,512,576,640,704},{4,68,132,196,260,324,38..., dimensions={0} | all-to-all | bytes 98304 | tf_op jit(solution)/shard_map/all_to_all | solution.py:22
  102.3 0.7 broadcast_multiply_fusion
  (6 shorter events, 0.1 us)
Async XLA Ops:
  3.4 26.5 %collective-permute-start = (bf16[528,768]{1,0:T(8,128)(2,1)}, bf16[528,768]{1,0:T(8,128)(2,1)S(1)}, u32[]{:S(2)}, u32[]{:S(2)}) collective-permute-start(bf16[528,768]{1,0:T(8,128)(2,1)} %get-tuple-element.14.refs_0_), channel_id=1, source_target_pairs={{0,1},{1,2},{2,3},{3,0},{4,5},{5,6},{6,7},{7,4},{8,9},{9,10},{10,1... | collective-permute-start | bytes 2433032 | tf_op jit(solution)/shard_map/ppermute | solution.py:186
  7.3 32.0 %all-to-all-start = ((bf16[24,2,32,128]{3,2,1,0:T(8,128)(2,1)}), bf16[24,2,32,128]{3,2,1,0:T(8,128)(2,1)S(1)}, u32[]{:S(2)}, u32[]{:S(2)}) async-start(bf16[24,2,32,128]{3,2,1,0:T(8,128)(2,1)} %get-tuple-element.15), calls=%async_computation | async-start | bytes 786432 | tf_op jit(solution)/shard_map/all_to_all | solution.py:185
  26.5 36.0 %collective-permute-start.4 = (bf16[528,768]{1,0:T(8,128)(2,1)}, bf16[528,768]{1,0:T(8,128)(2,1)S(1)}, u32[]{:S(2)}, u32[]{:S(2)}) collective-permute-start(bf16[528,768]{1,0:T(8,128)(2,1)} %get-tuple-element.14.refs_0_), channel_id=1, source_target_pairs={{1,0},{2,1},{3,2},{0,3},{5,4},{6,5},{7,6},{4,7},{9,8},{10,9},{11,1... | collective-permute-start | bytes 2433032 | tf_op jit(solution)/shard_map/ppermute | solution.py:187
  29.9 33.6 %collective-permute-start.5 = (bf16[528,768]{1,0:T(8,128)(2,1)S(1)}, bf16[528,768]{1,0:T(8,128)(2,1)S(1)}, u32[]{:S(2)}, u32[]{:S(2)}) collective-permute-start(bf16[528,768]{1,0:T(8,128)(2,1)S(1)} %collective-permute-done.refs_1_), channel_id=1, source_target_pairs={{0,1},{1,2},{2,3},{3,0},{4,5},{5,6},{6,7},{7,4},{8,9},{9,10},{10,1... | collective-permute-start | bytes 2433032 | tf_op jit(solution)/shard_map/ppermute | solution.py:188
  39.4 23.2 %collective-permute-start.1 = (bf16[24,2,32,128]{3,2,1,0:T(8,128)(2,1)S(1)}, bf16[24,2,32,128]{3,2,1,0:T(8,128)(2,1)S(1)}, u32[]{:S(2)}, u32[]{:S(2)}) collective-permute-start(bf16[24,2,32,128]{3,2,1,0:T(8,128)(2,1)S(1)} %all-to-all-done), channel_id=1, source_target_pairs={{0,16},{4,132},{8,56},{12,140},{16,32},{20,148},{24,8},{28,156},{3... | collective-permute-start | bytes 1179656 | tf_op jit(solution)/shard_map/ppermute | solution.py:189
  49.0 13.5 %collective-permute-start.2 = (bf16[24,2,32,128]{3,2,1,0:T(8,128)(2,1)S(1)}, bf16[24,2,32,128]{3,2,1,0:T(8,128)(2,1)S(1)}, u32[]{:S(2)}, u32[]{:S(2)}) collective-permute-start(bf16[24,2,32,128]{3,2,1,0:T(8,128)(2,1)S(1)} %all-to-all-done), channel_id=1, source_target_pairs={{0,8},{4,68},{8,16},{12,76},{16,24},{20,84},{24,32},{28,92},{32,40... | collective-permute-start | bytes 1179656 | tf_op jit(solution)/shard_map/ppermute | solution.py:189
  54.6 8.8 %collective-permute-start.3 = (bf16[24,2,32,128]{3,2,1,0:T(8,128)(2,1)S(1)}, bf16[24,2,32,128]{3,2,1,0:T(8,128)(2,1)S(1)}, u32[]{:S(2)}, u32[]{:S(2)}) collective-permute-start(bf16[24,2,32,128]{3,2,1,0:T(8,128)(2,1)S(1)} %all-to-all-done), channel_id=1, source_target_pairs={{0,56},{4,708},{8,0},{12,716},{16,8},{20,724},{24,16},{28,732},{32... | collective-permute-start | bytes 1179656 | tf_op jit(solution)/shard_map/ppermute | solution.py:189
  62.5 11.2 %copy-start = (bf16[528,768]{1,0:T(8,128)(2,1)S(1)}, bf16[528,768]{1,0:T(8,128)(2,1)}, u32[]{:S(2)}) copy-start(bf16[528,768]{1,0:T(8,128)(2,1)} %get-tuple-element.14.refs_0_) | copy-start | bytes 2433028
  62.5 11.2 %copy-start.1 = (s32[2,1]{0,1:T(1,128)S(1)}, s32[2,1]{0,1:T(1,128)}, u32[]{:S(2)}) copy-start(s32[2,1]{0,1:T(1,128)} %param.7) | copy-start | bytes 28

commit v9 on v8

--- a/solution.py
+++ b/solution.py
@@ -146,9 +146,9 @@
                     tile = block_col * 12 + words_ref[base + slot]
                     rows = pl.ds(pl.multiple_of(tile * TILE, TILE), TILE)
                     keep = (slot < count).astype(jnp.float32).astype(jnp.bfloat16)
-                    near_ref[slot * TILE : (slot + 1) * TILE] = right_ref[s, rows] * keep
+                    near_ref[s % 2, slot * TILE : (slot + 1) * TILE] = right_ref[s, rows] * keep
                 left = lefts[source][group * TILE : (group + 1) * TILE, :]
-                total += jnp.dot(left, near_ref[...], preferred_element_type=jnp.float32)
+                total += jnp.dot(left, near_ref[s % 2], preferred_element_type=jnp.float32)
         squares = total * total * keep_ref[r].astype(jnp.float32)
         out_ref[r * TILE : (r + 1) * TILE] = squares
         colsum += jnp.sum(squares.reshape(TILE // 8, 8, TILE), axis=0)
@@ -169,7 +169,7 @@
         out_specs=(vmem, vmem),
         scratch_shapes=[
             pltpu.VMEM((sections, depth, TILE), jnp.bfloat16),
-            pltpu.VMEM((SLOTS * TILE, TILE), jnp.bfloat16),
+            pltpu.VMEM((2, SLOTS * TILE, TILE), jnp.bfloat16),
         ],
         compiler_params=pltpu.CompilerParams(vmem_limit_bytes=32 * 2**20),
         cost_estimate=pl.CostEstimate(

time: 104 us -> 104 us (level)
  no operation moved by 1% of the time
where the time goes in v9:
time: 104 us; the launch traced here: 103 us
  starting transfers between devices  45.6 us (44%)
  blocking collectives  42.5 us (41%)
  waiting for transfers between devices  7.71 us (7%)
  Pallas kernels  5.45 us (5%)
    all_to_all x1, starting transfers between devices, shards(): lax.all_to_all(copies, 'row', 0, 0, tiled=True, axis_index_groups=MIXED_G...  19.2 us
    ppermute x3, starting transfers between devices, shards(): lax.ppermute(held, 'row', shift_moves(s))  17.2 us
    all_gather x4, blocking collectives, shards(): lax.all_gather(piece, 'row', axis_index_groups=CORE_GROUPS)  16.2 us
    all_to_all x1, blocking collectives, spread(): lax.all_to_all(copies, axis, 0, 0, tiled=True, axis_index_groups=groups)  14 us
    all_to_all x1, blocking collectives, shards(): lax.all_to_all(sums, 'row', 0, 0, tiled=True, axis_index_groups=PLANE_GRO...  12.4 us
    all_to_all x1, waiting for transfers between devices, shards(): lax.all_to_all(copies, 'row', 0, 0, tiled=True, axis_index_groups=MIXED_G...  6.8 us
    ppermute x1, starting transfers between devices, shards(): below = lax.ppermute(packed, 'col', UP)  3.95 us
    pallas_call x1, Pallas kernels, pack(): pl.pallas_call(pack_kernel, out_shape=(jax.ShapeDtypeStruct((height, SLOT...  3.37 us
  transfers between devices with their start and end apart: 7, of which 2 were waited for; matrix products, arithmetic and copies ran while one was open for 1% of the time, Pallas kernels for 0%

profile of v9, /device:TPU:1, one launch (start us, length us, event | category | flops | bytes accessed | tf_op | source)
XLA Modules:
  0.0 102.9 jit_solution(926900207844120222)
XLA Ops:
  0.0 3.4 %shard_map.46 = (bf16[528,768]{1,0:T(8,128)(2,1)}, bf16[24,2,32,128]{3,2,1,0:T(8,128)(2,1)}) custom-call(s32[2,2,12]{2,1,0:T(2,128)} %fill_ref.1, bf16[2,32,128]{2,1,0:T(8,128)(2,1)} %panel_ref.1, bf16[2,256,1536]{2,1,0:T(8,128)(2,1)} %slab_hbm.1), custom_call_target="tpu_custom_call" | custom-call | bytes 2097152 | tf_op jit(solution)/shard_map/pallas_call | solution.py:97
  3.4 3.9 %collective-permute-start = (bf16[528,768]{1,0:T(8,128)(2,1)}, bf16[528,768]{1,0:T(8,128)(2,1)S(1)}, u32[]{:S(2)}, u32[]{:S(2)}) collective-permute-start(bf16[528,768]{1,0:T(8,128)(2,1)} %get-tuple-element.14.refs_0_), channel_id=1, source_target_pairs={{0,1},{1,2},{2,3},{3,0},{4,5},{5,6},{6,7},{7,4},{8,9},{9,10},{10,1... | collective-permute-start | bytes 2433032 | tf_op jit(solution)/shard_map/ppermute | solution.py:186
  7.3 19.2 %all-to-all-start = ((bf16[24,2,32,128]{3,2,1,0:T(8,128)(2,1)}), bf16[24,2,32,128]{3,2,1,0:T(8,128)(2,1)S(1)}, u32[]{:S(2)}, u32[]{:S(2)}) async-start(bf16[24,2,32,128]{3,2,1,0:T(8,128)(2,1)} %get-tuple-element.15), calls=%async_computation | async-start | bytes 786432 | tf_op jit(solution)/shard_map/all_to_all | solution.py:185
  26.5 3.4 %collective-permute-start.4 = (bf16[528,768]{1,0:T(8,128)(2,1)}, bf16[528,768]{1,0:T(8,128)(2,1)S(1)}, u32[]{:S(2)}, u32[]{:S(2)}) collective-permute-start(bf16[528,768]{1,0:T(8,128)(2,1)} %get-tuple-element.14.refs_0_), channel_id=1, source_target_pairs={{1,0},{2,1},{3,2},{0,3},{5,4},{6,5},{7,6},{4,7},{9,8},{10,9},{11,1... | collective-permute-start | bytes 2433032 | tf_op jit(solution)/shard_map/ppermute | solution.py:187
  29.9 0.0 collective-permute-done.refs_1_
  29.9 1.9 %collective-permute-start.5 = (bf16[528,768]{1,0:T(8,128)(2,1)S(1)}, bf16[528,768]{1,0:T(8,128)(2,1)S(1)}, u32[]{:S(2)}, u32[]{:S(2)}) collective-permute-start(bf16[528,768]{1,0:T(8,128)(2,1)S(1)} %collective-permute-done.refs_1_), channel_id=1, source_target_pairs={{0,1},{1,2},{2,3},{3,0},{4,5},{5,6},{6,7},{7,4},{8,9},{9,10},{10,1... | collective-permute-start | bytes 2433032 | tf_op jit(solution)/shard_map/ppermute | solution.py:188
  31.8 0.1 pad_add_fusion.place_ref
  31.9 0.7 slice_bitcast_fusion.3
  32.6 6.8 %all-to-all-done = bf16[24,2,32,128]{3,2,1,0:T(8,128)(2,1)S(1)} async-done(((bf16[24,2,32,128]{3,2,1,0:T(8,128)(2,1)}), bf16[24,2,32,128]{3,2,1,0:T(8,128)(2,1)S(1)}, u32[]{:S(2)}, u32[]{:S(2)}) %all-to-all-start) | async-done | bytes 393248 | tf_op jit(solution)/shard_map/all_to_all | solution.py:185
  39.4 9.6 %collective-permute-start.1 = (bf16[24,2,32,128]{3,2,1,0:T(8,128)(2,1)S(1)}, bf16[24,2,32,128]{3,2,1,0:T(8,128)(2,1)S(1)}, u32[]{:S(2)}, u32[]{:S(2)}) collective-permute-start(bf16[24,2,32,128]{3,2,1,0:T(8,128)(2,1)S(1)} %all-to-all-done), channel_id=1, source_target_pairs={{0,16},{4,132},{8,56},{12,140},{16,32},{20,148},{24,8},{28,156},{3... | collective-permute-start | bytes 1179656 | tf_op jit(solution)/shard_map/ppermute | solution.py:189
  49.0 5.6 %collective-permute-start.2 = (bf16[24,2,32,128]{3,2,1,0:T(8,128)(2,1)S(1)}, bf16[24,2,32,128]{3,2,1,0:T(8,128)(2,1)S(1)}, u32[]{:S(2)}, u32[]{:S(2)}) collective-permute-start(bf16[24,2,32,128]{3,2,1,0:T(8,128)(2,1)S(1)} %all-to-all-done), channel_id=1, source_target_pairs={{0,8},{4,68},{8,16},{12,76},{16,24},{20,84},{24,32},{28,92},{32,40... | collective-permute-start | bytes 1179656 | tf_op jit(solution)/shard_map/ppermute | solution.py:189
  54.6 1.9 %collective-permute-start.3 = (bf16[24,2,32,128]{3,2,1,0:T(8,128)(2,1)S(1)}, bf16[24,2,32,128]{3,2,1,0:T(8,128)(2,1)S(1)}, u32[]{:S(2)}, u32[]{:S(2)}) collective-permute-start(bf16[24,2,32,128]{3,2,1,0:T(8,128)(2,1)S(1)} %all-to-all-done), channel_id=1, source_target_pairs={{0,56},{4,708},{8,0},{12,716},{16,8},{20,724},{24,16},{28,732},{32... | collective-permute-start | bytes 1179656 | tf_op jit(solution)/shard_map/ppermute | solution.py:189
  56.6 6.0 %all-gather = bf16[48,2,32,128]{3,2,1,0:T(8,128)(2,1)S(1)} all-gather(bf16[24,2,32,128]{3,2,1,0:T(8,128)(2,1)S(1)} %all-to-all-done), channel_id=2, replica_groups={{0,4},{8,12},{16,20},{24,28},{32,36},{40,44},{48,52},{56,60},{64,68},{7..., dimensions={0}, use_global_device_ids=true | all-gather | bytes 1179648 | tf_op jit(solution)/shard_map/all_gather | solution.py:193
  62.5 0.0 copy-start
  62.5 0.0 copy-start.1
  62.5 0.0 collective-permute-done.4.refs_2_
  62.5 0.0 collective-permute-done.1
  62.5 0.0 collective-permute-done.2
  62.5 0.9 collective-permute-done.3
  63.4 0.0 collective-permute-done.5.refs_3_
  63.5 5.5 %all-gather.3 = bf16[48,2,32,128]{3,2,1,0:T(8,128)(2,1)S(1)} all-gather(bf16[24,2,32,128]{3,2,1,0:T(8,128)(2,1)S(1)} %collective-permute-done.3), channel_id=5, replica_groups={{0,4},{8,12},{16,20},{24,28},{32,36},{40,44},{48,52},{56,60},{64,68},{7..., dimensions={0}, use_global_device_ids=true | all-gather | bytes 1179648 | tf_op jit(solution)/shard_map/all_gather | solution.py:193
  69.0 2.4 %all-gather.1 = bf16[48,2,32,128]{3,2,1,0:T(8,128)(2,1)S(1)} all-gather(bf16[24,2,32,128]{3,2,1,0:T(8,128)(2,1)S(1)} %collective-permute-done.1), channel_id=3, replica_groups={{0,4},{8,12},{16,20},{24,28},{32,36},{40,44},{48,52},{56,60},{64,68},{7..., dimensions={0}, use_global_device_ids=true | all-gather | bytes 1179648 | tf_op jit(solution)/shard_map/all_gather | solution.py:193
  71.3 2.4 %all-gather.2 = bf16[48,2,32,128]{3,2,1,0:T(8,128)(2,1)S(1)} all-gather(bf16[24,2,32,128]{3,2,1,0:T(8,128)(2,1)S(1)} %collective-permute-done.2), channel_id=4, replica_groups={{0,4},{8,12},{16,20},{24,28},{32,36},{40,44},{48,52},{56,60},{64,68},{7..., dimensions={0}, use_global_device_ids=true | all-gather | bytes 1179648 | tf_op jit(solution)/shard_map/all_gather | solution.py:193
  73.7 0.1 maximum_convert_fusion.words_ref
  73.8 0.0 copy-done
  73.8 0.0 copy-done.1
  73.8 2.1 %shard_map.47 = (f32[256,128]{1,0:T(8,128)S(1)}, f32[16,8,128]{2,1,0:T(8,128)S(1)}) custom-call(s32[2]{0:T(128)S(1)} %pad_add_fusion.place_ref, s32[112]{0:T(128)S(1)} %maximum_convert_fusion.words_ref, s32[2]{0:T(128)S(1)} %bitcast.19, bf16[528,768]{1,0:T(8,128)(2,1)S(1)} %copy-done, bf16[528,768]{1,0:T(8,128)(2,1)S(1)} %collective-permute-done.refs_1_, ...), custom_call_target="tpu_custom_call" | custom-call | flops 402653184 | bytes 7340032 | tf_op jit(solution)/shard_map/pallas_call | solution.py:162
  75.8 12.4 %all_to_all.15 = f32[16,8,128]{2,1,0:T(8,128)S(1)} all-to-all(f32[16,8,128]{2,1,0:T(8,128)S(1)} %get-tuple-element.22), channel_id=1, replica_groups={{0,4,8,12,16,20,24,28,32,36,40,44,48,52,56,60},{64,68,72,76,80,84,88,92..., dimensions={0} | all-to-all | bytes 131072 | tf_op jit(solution)/shard_map/all_to_all | solution.py:200
  88.2 14.0 %all_to_all.16 = f32[12,8,128]{2,1,0:T(8,128)S(1)} all-to-all(f32[12,8,128]{2,1,0:T(8,128)S(1)} %broadcast_in_dim.2), channel_id=1, replica_groups={{0,64,128,192,256,320,384,448,512,576,640,704},{4,68,132,196,260,324,38..., dimensions={0} | all-to-all | bytes 98304 | tf_op jit(solution)/shard_map/all_to_all | solution.py:22
  102.2 0.7 broadcast_multiply_fusion
  (6 shorter events, 0.1 us)
Async XLA Ops:
  3.4 26.5 %collective-permute-start = (bf16[528,768]{1,0:T(8,128)(2,1)}, bf16[528,768]{1,0:T(8,128)(2,1)S(1)}, u32[]{:S(2)}, u32[]{:S(2)}) collective-permute-start(bf16[528,768]{1,0:T(8,128)(2,1)} %get-tuple-element.14.refs_0_), channel_id=1, source_target_pairs={{0,1},{1,2},{2,3},{3,0},{4,5},{5,6},{6,7},{7,4},{8,9},{9,10},{10,1... | collective-permute-start | bytes 2433032 | tf_op jit(solution)/shard_map/ppermute | solution.py:186
  7.3 32.0 %all-to-all-start = ((bf16[24,2,32,128]{3,2,1,0:T(8,128)(2,1)}), bf16[24,2,32,128]{3,2,1,0:T(8,128)(2,1)S(1)}, u32[]{:S(2)}, u32[]{:S(2)}) async-start(bf16[24,2,32,128]{3,2,1,0:T(8,128)(2,1)} %get-tuple-element.15), calls=%async_computation | async-start | bytes 786432 | tf_op jit(solution)/shard_map/all_to_all | solution.py:185
  26.5 36.0 %collective-permute-start.4 = (bf16[528,768]{1,0:T(8,128)(2,1)}, bf16[528,768]{1,0:T(8,128)(2,1)S(1)}, u32[]{:S(2)}, u32[]{:S(2)}) collective-permute-start(bf16[528,768]{1,0:T(8,128)(2,1)} %get-tuple-element.14.refs_0_), channel_id=1, source_target_pairs={{1,0},{2,1},{3,2},{0,3},{5,4},{6,5},{7,6},{4,7},{9,8},{10,9},{11,1... | collective-permute-start | bytes 2433032 | tf_op jit(solution)/shard_map/ppermute | solution.py:187
  29.9 33.6 %collective-permute-start.5 = (bf16[528,768]{1,0:T(8,128)(2,1)S(1)}, bf16[528,768]{1,0:T(8,128)(2,1)S(1)}, u32[]{:S(2)}, u32[]{:S(2)}) collective-permute-start(bf16[528,768]{1,0:T(8,128)(2,1)S(1)} %collective-permute-done.refs_1_), channel_id=1, source_target_pairs={{0,1},{1,2},{2,3},{3,0},{4,5},{5,6},{6,7},{7,4},{8,9},{9,10},{10,1... | collective-permute-start | bytes 2433032 | tf_op jit(solution)/shard_map/ppermute | solution.py:188
  39.4 23.2 %collective-permute-start.1 = (bf16[24,2,32,128]{3,2,1,0:T(8,128)(2,1)S(1)}, bf16[24,2,32,128]{3,2,1,0:T(8,128)(2,1)S(1)}, u32[]{:S(2)}, u32[]{:S(2)}) collective-permute-start(bf16[24,2,32,128]{3,2,1,0:T(8,128)(2,1)S(1)} %all-to-all-done), channel_id=1, source_target_pairs={{0,16},{4,132},{8,56},{12,140},{16,32},{20,148},{24,8},{28,156},{3... | collective-permute-start | bytes 1179656 | tf_op jit(solution)/shard_map/ppermute | solution.py:189
  49.0 13.5 %collective-permute-start.2 = (bf16[24,2,32,128]{3,2,1,0:T(8,128)(2,1)S(1)}, bf16[24,2,32,128]{3,2,1,0:T(8,128)(2,1)S(1)}, u32[]{:S(2)}, u32[]{:S(2)}) collective-permute-start(bf16[24,2,32,128]{3,2,1,0:T(8,128)(2,1)S(1)} %all-to-all-done), channel_id=1, source_target_pairs={{0,8},{4,68},{8,16},{12,76},{16,24},{20,84},{24,32},{28,92},{32,40... | collective-permute-start | bytes 1179656 | tf_op jit(solution)/shard_map/ppermute | solution.py:189
  54.6 8.8 %collective-permute-start.3 = (bf16[24,2,32,128]{3,2,1,0:T(8,128)(2,1)S(1)}, bf16[24,2,32,128]{3,2,1,0:T(8,128)(2,1)S(1)}, u32[]{:S(2)}, u32[]{:S(2)}) collective-permute-start(bf16[24,2,32,128]{3,2,1,0:T(8,128)(2,1)S(1)} %all-to-all-done), channel_id=1, source_target_pairs={{0,56},{4,708},{8,0},{12,716},{16,8},{20,724},{24,16},{28,732},{32... | collective-permute-start | bytes 1179656 | tf_op jit(solution)/shard_map/ppermute | solution.py:189
  62.5 11.2 %copy-start = (bf16[528,768]{1,0:T(8,128)(2,1)S(1)}, bf16[528,768]{1,0:T(8,128)(2,1)}, u32[]{:S(2)}) copy-start(bf16[528,768]{1,0:T(8,128)(2,1)} %get-tuple-element.14.refs_0_) | copy-start | bytes 2433028
  62.5 11.2 %copy-start.1 = (s32[2,1]{0,1:T(1,128)S(1)}, s32[2,1]{0,1:T(1,128)}, u32[]{:S(2)}) copy-start(s32[2,1]{0,1:T(1,128)} %param.7) | copy-start | bytes 28
